TPU v7x, 32 devices: a whole 2x2x4 slice. The times are simulated.
32 devices in a mesh: dp: 4 (over z), label: 4 (over y, x), section: 2 (over core).
Axes of the slice: x: 2, y: 2, z: 4, core: 2. Of those that a mesh axis runs over, the one named last changes fastest.
Arguments:
- queries: bfloat16 [4096, 1024], P(('dp', 'label', 'section')), may hold values from -6 to 6
- label_weights: bfloat16 [128, 128, 1024], P('label'), may hold values from -0.1875 to 0.1875
- propensity: float32 [128, 128], P('label'), may hold values from 0.1 to 1
- positives: int32 [4096, 8], P(('dp', 'label', 'section')), may hold values from 0 to 6143
- shortlist: int32 [16, 48], P(('dp', 'label')), may hold values from 0 to 127, as said below
- owner_map: int32 [128], replicated, may hold values from 0 to 127, as said below
Outputs:
- query_grad: float32 [4096, 1024], P(('dp', 'label', 'section'))
- weight_grad: float32 [128, 128, 1024], P('label', ('dp', 'section'))
Inputs may be any that keep to these rules, and one draw needn't show every extreme that they name: owner_map is a permutation of the 128 row blocks. `shortlist`: each row lists 48 different label-block ids. Of one row's blocks at most 24 are stored in the row blocks of one owner (rows o * 32 to o * 32 + 31 of label_weights), and in every draw one owner holds exactly 24 of the blocks of every row.
All inputs are finite; a program needn't handle non-finite values.
Results may differ from a plain program's by a relative error of at most 0.0021.
Values may be sent and summed in bfloat16 or wider, within the bound.
No kernel may reach another device: no remote copies, remote signals or barrier semaphores. Data moves between devices by JAX's collectives and lax.ppermute only.
A program may use at most 128 MiB of HBM per device.

v0:
```python
import jax
import jax.numpy as jnp
from jax import lax
from jax.sharding import PartitionSpec as P

grad_scale = 0.25


def per_device(queries, label_weights, propensity, positives, shortlist, owner_map):
    label_count = lax.axis_size("label")
    own_index = lax.axis_index("label")
    peer_rows, peer_pos, peer_lists = (
        lax.all_gather(queries, "label", axis=0, tiled=True),
        lax.all_gather(positives, "label", axis=0, tiled=True),
        lax.all_gather(shortlist, "label", axis=0, tiled=True),
    )
    block_count, block_rows, feature_dim = label_weights.shape
    half_rows = queries.shape[0]
    short_len = peer_lists.shape[1]
    capacity = 2 * short_len // label_count
    table_len = owner_map.shape[0]
    lookup = (
        peer_lists[:, :, None] == jnp.arange(table_len, dtype=jnp.int32)[None, None, :]
    ).astype(jnp.int32)
    stored = jnp.sum(lookup * owner_map[None, None, :], axis=2)
    owners = stored // block_count
    local_slot = stored % block_count
    own_entry = (owners == own_index).astype(jnp.int32)
    entry_rank = jnp.cumsum(own_entry, axis=1) - 1
    select = own_entry[:, :, None] * (
        entry_rank[:, :, None] == jnp.arange(capacity, dtype=jnp.int32)[None, None, :]
    ).astype(jnp.int32)
    slot_ids = jnp.sum(select * local_slot[:, :, None], axis=1)
    entries = jnp.sum(select * jnp.arange(short_len, dtype=jnp.int32)[None, :, None], axis=1)
    live_slot = jnp.sum(select, axis=1).astype(jnp.float32)
    tokens = peer_rows.reshape(label_count, half_rows, feature_dim)
    pos_rows = peer_pos.reshape(label_count, half_rows, -1)
    label_offsets = jnp.arange(block_rows, dtype=jnp.int32)

    def slot_grad(slot_index, score_grads):
        slot_col = lax.dynamic_index_in_dim(slot_ids, slot_index, 1, keepdims=False)
        entry_col = lax.dynamic_index_in_dim(entries, slot_index, 1, keepdims=False)
        live_col = lax.dynamic_index_in_dim(live_slot, slot_index, 1, keepdims=False)
        weights_sel = jnp.take(label_weights, slot_col, axis=0)
        prop_sel = jnp.take(propensity, slot_col, axis=0)
        scores = jnp.einsum("jqd,jld->jql", tokens, weights_sel, preferred_element_type=jnp.float32)
        label_ids = entry_col[:, None] * block_rows + label_offsets[None, :]
        target = jnp.any(pos_rows[:, :, :, None] == label_ids[:, None, None, :], axis=2).astype(
            jnp.float32
        )
        gradient = (
            (jax.nn.sigmoid(scores) - target / prop_sel[:, None, :])
            * live_col[:, None, None]
            * grad_scale
        )
        return lax.dynamic_update_index_in_dim(
            score_grads, gradient.astype(jnp.bfloat16), slot_index, 1
        )

    empty_grads = jnp.zeros((label_count, capacity, half_rows, block_rows), jnp.bfloat16)
    score_grads = lax.fori_loop(0, capacity, slot_grad, empty_grads)
    number = lax.axis_size("label") * half_rows // half_rows
    grad_part = score_grads

    def add_slot(slot_index, running):
        slot_col = lax.dynamic_index_in_dim(slot_ids, slot_index, 1, keepdims=False)
        weights_sel = jnp.take(label_weights, slot_col, axis=0)
        grad_col = lax.dynamic_index_in_dim(grad_part, slot_index, 1, keepdims=False)
        return running + jnp.einsum(
            "jql,jld->jqd", grad_col, weights_sel, preferred_element_type=jnp.float32
        )

    running = lax.fori_loop(
        0, capacity, add_slot, jnp.zeros((number, half_rows, feature_dim), jnp.float32)
    )
    query_grad = lax.psum_scatter(
        running.reshape(lax.axis_size("label") * half_rows, feature_dim),
        "label",
        scatter_dimension=0,
        tiled=True,
    )
    onehot = (
        slot_ids[None, :, :] == jnp.arange(block_count, dtype=jnp.int32)[:, None, None]
    ).astype(jnp.bfloat16)
    picked = jnp.einsum(
        "bjk,jkql->bjql", onehot, score_grads, preferred_element_type=jnp.float32
    ).astype(jnp.bfloat16)
    weight_part = jnp.einsum("bjql,jqd->bld", picked, tokens, preferred_element_type=jnp.float32)
    weight_grad = lax.psum_scatter(weight_part, ("dp", "section"), scatter_dimension=1, tiled=True)
    return (query_grad, weight_grad)


def solution(mesh):
    in_specs = (
        P(("dp", "label", "section"), None),
        P("label", None, None),
        P("label", None),
        P(("dp", "label", "section"), None),
        P(("dp", "label"), None),
        P(),
    )
    out_specs = (P(("dp", "label", "section"), None), P("label", ("dp", "section"), None))
    return jax.shard_map(
        per_device, mesh=mesh, in_specs=in_specs, out_specs=out_specs, check_vma=False
    )
```

profile of v0, /device:TPU:0, one launch (start us, length us, event | category | flops | bytes accessed | tf_op | source)
XLA Modules:
  0.0 661.3 jit_solution(9591312442516511346)
XLA Ops:
  8.0 9.5 %all-gather = s32[4,1,48]{2,1,0:T(1,128)S(1)} all-gather(s32[1,1,48]{2,1,0:T(1,128)} %bitcast.79), channel_id=1, replica_groups=mesh['dp'=4,'label'=4,'section'=2] {'label'}, dimensions={0}, use_global_device_ids=true | all-gather | bytes 960 | tf_op jit(solution)/shard_map/all_gather | solution.py:15
  19.9 9.7 %all_gather.11 = s32[512,8]{1,0:T(8,128)S(1)} all-gather(s32[128,8]{1,0:T(8,128)S(1)} %copy.15), channel_id=1, replica_groups=mesh['dp'=4,'label'=4,'section'=2] {'label'}, dimensions={0}, use_global_device_ids=true | all-gather | bytes 20480 | tf_op jit(solution)/shard_map/all_gather | solution.py:14
  29.6 10.6 %all-gather.3.cloned.1.call-done = bf16[512,1024]{1,0:T(8,128)(2,1)} async-done(((bf16[128,1024]{1,0:T(8,128)(2,1)}), bf16[512,1024]{1,0:T(8,128)(2,1)}) %all-gather.3.cloned.1.call-update) | async-done | bytes 1048592 | tf_op jit(solution)/shard_map/all_gather | solution.py:13
  40.3 262.8 %while.28 = (s32[]{:T(128)}, bf16[4,24,128,128]{2,3,0,1:T(8,128)(2,1)}, s32[4,24]{0,1:T(8,128)S(1)}, bf16[32,128,1024]{2,1,0:T(8,128)(2,1)}, bf16[4,128,1024]{2,...) while((s32[]{:T(128)}, ...), condition=%wide.region_7.9_spmd.clone, body=%wide.region_5.8_spmd.clone.sunk | while | flops 136318000 | bytes 4626801 | solution.py:61
  44.8 4.0 gather_fusion
  55.7 4.0 gather_fusion
  66.7 4.0 gather_fusion
  77.6 4.0 gather_fusion
  88.6 4.0 gather_fusion
  99.5 4.0 gather_fusion
  110.5 4.0 gather_fusion
  121.4 4.0 gather_fusion
  132.4 4.0 gather_fusion
  143.3 4.0 gather_fusion
  154.3 4.0 gather_fusion
  165.2 4.0 gather_fusion
  176.2 4.0 gather_fusion
  187.1 4.0 gather_fusion
  198.1 4.0 gather_fusion
  209.0 4.0 gather_fusion
  220.0 4.0 gather_fusion
  230.9 4.0 gather_fusion
  241.9 4.0 gather_fusion
  252.8 4.0 gather_fusion
  263.8 4.0 gather_fusion
  303.0 143.7 %while.29 = (s32[]{:T(128)}, f32[4,128,1024]{2,1,0:T(8,128)S(1)}, bf16[4,24,128,128]{2,3,0,1:T(8,128)(2,1)}, s32[4,24]{0,1:T(8,128)S(1)}, bf16[32,128,1024]{2,1,0:T(8,128)(2,1)}, /*index=5*/s32[]{:T(128)}, s32[]{:T(128)}) while((s32[]{:T(128)}, f32[4,128,1024]{2,1,0:T(8,128)S(1)}, bf16[4,24,128,128]{2,3,0,1:T(8,128)(2,1)}, ...), condition=%wide.region_9.11_spmd.clone, body=%wide.region_8.10_spmd.clone.sunk | while | flops 135791648 | bytes 7475375 | solution.py:73
  368.9 4.0 gather_fusion.2
  410.8 4.0 gather_fusion.2
  448.1 4.9 copy.21
  456.6 11.2 %convolution_bitcast_fusion = f32[32,128,1024]{2,1,0:T(8,128)} fusion(bf16[4,128,1024,1]{2,1,0,3:T(8,128)(2,1)S(1)} %bitcast.76, bf16[32,4,128,128]{3,0,2,1:T(8,128)(2,1)S(1)} %convert_bitcast_fusion), kind=kOutput, calls=%fused_computation.45 | convolution fusion | flops 4294967296 | bytes 22020096 | tf_op jit(solution)/shard_map/bjql,jqd->bld/dot_general | solution.py:88
  467.8 15.7 %reduce-scatter.3.cloned.1.call-done = f32[128,1024]{1,0:T(8,128)} async-done(((f32[512,1024]{1,0:T(8,128)}), f32[128,1024]{1,0:T(8,128)}) %reduce-scatter.3.cloned.1.call-update) | async-done | bytes 524304 | tf_op jit(solution)/shard_map/reduce_scatter | solution.py:76
  483.4 171.3 %reduce-scatter.5.cloned.1.call-done = f32[32,16,1024]{2,1,0:T(8,128)} async-done(((f32[32,128,1024]{2,1,0:T(8,128)}), f32[32,16,1024]{2,1,0:T(8,128)}) %reduce-scatter.5.cloned.1.call-update) | async-done | bytes 2097168 | tf_op jit(solution)/shard_map/reduce_scatter | solution.py:89
  (408 shorter events, 320.6 us)
Async XLA Ops:
  7.2 33.1 %all-gather.3.cloned.1.call-start = ((), (), s32[]{:S(2)}) async-start(), calls=%async_computation.2 | async-start | bytes 1310720 | tf_op jit(solution)/shard_map/all_gather | solution.py:13
  7.9 475.5 %reduce-scatter.3.cloned.1.call-start = ((), (), s32[]{:S(2)}) async-start(), calls=%async_computation.3 | async-start | bytes 2621440 | tf_op jit(solution)/shard_map/reduce_scatter | solution.py:76
  446.7 1.4 copy-start
  448.1 206.7 %reduce-scatter.5.cloned.1.call-start = ((), (), s32[]{:S(2)}) async-start(), calls=%async_computation.4 | async-start | bytes 18874368 | tf_op jit(solution)/shard_map/reduce_scatter | solution.py:89
  453.0 3.5 copy-start.1
Sparse Core Ops, SparseCore 0:
  9.8 30.3 all-gather.2
  448.2 35.1 reduce-scatter.2
  486.5 168.2 reduce-scatter.4
where the time goes:
time: 666 us; the launch traced here: 661 us
  local copies, waits for them, and re-layouts  233 us (35%)
  waiting for transfers between devices  198 us (30%)
  matrix products  118 us (18%)
  other arithmetic  76.1 us (11%)
  blocking collectives  19.2 us (3%)
  between operations  13.8 us (2%)
    reduce_scatter x1, waiting for transfers between devices, per_device(): lax.psum_scatter(weight_part, ('dp', 'section'), scatter_dimension=1, til...  171 us
    gather x24, local copies, waits for them, and re-layouts, add_slot(): weights_sel = jnp.take(label_weights, slot_col, axis=0)  95.9 us
    gather x24, local copies, waits for them, and re-layouts, slot_grad(): weights_sel = jnp.take(label_weights, slot_col, axis=0)  95.9 us
    reduce_or x24, other arithmetic, slot_grad(): jnp.any(pos_rows[:, :, :, None] == label_ids[:, None, None, :], axis=2)  69.4 us
    dot_general x24, matrix products, slot_grad(): jnp.einsum('jqd,jld->jql', tokens, weights_sel, preferred_element_type=jn...  57.7 us
    dot_general x24, matrix products, add_slot(): jnp.einsum('jql,jld->jqd', grad_col, weights_sel, preferred_element_type=...  46.1 us
    gather x24, local copies, waits for them, and re-layouts, slot_grad(): prop_sel = jnp.take(propensity, slot_col, axis=0)  30.6 us
    reduce_scatter x1, waiting for transfers between devices, per_device(): lax.psum_scatter(running.reshape(lax.axis_size('label') * half_rows, feat...  15.7 us
  transfers between devices with their start and end apart: 3, of which 3 were waited for; matrix products, arithmetic and copies ran while one was open for 3% of the time, Pallas kernels for 0%

commit v1 on v0

v1 whole, which is shorter than its diff:
```python
import functools
import jax
import jax.numpy as jnp
from jax import lax
from jax.experimental import pallas as pl
from jax.experimental.pallas import tpu as pltpu
from jax.sharding import PartitionSpec as P

scale = 0.25
NT = (((1,), (1,)), ((), ()))
NN = (((1,), (0,)), ((), ()))
f32, bf16, i32 = jnp.float32, jnp.bfloat16, jnp.int32
LANES = 128
WORD = 32


def pack_body(queries, positives, shortlist, owner_map, out):
    rows, feats = queries.shape
    count = positives.shape[1]
    short_len = shortlist.shape[1]
    width = LANES
    out[0:rows, :] = queries[...]
    wide = jnp.concatenate(
        [positives[...], jnp.zeros((rows, LANES - count), i32)], axis=1)
    pos = wide.T[0:count, :]
    entry = pos // width
    label = pos - entry * width
    ids = lax.broadcasted_iota(i32, (count, LANES), 1)
    stored = jnp.zeros((count, rows), i32)
    present = jnp.zeros((count, LANES), i32)
    for e in range(short_len):
        place = owner_map[shortlist[0, e]]
        stored = jnp.where(entry == e, place, stored)
        present = jnp.where(ids == place, 1, present)
    out[rows:, :] = jnp.zeros((out.shape[0] - rows, feats), bf16)
    out[rows:, 0:rows] = stored.astype(f32).astype(bf16)
    out[rows:, rows:2 * rows] = label.astype(f32).astype(bf16)
    out[rows:, 2 * rows:2 * rows + LANES] = present.astype(f32).astype(bf16)


def pack(queries, positives, shortlist, owner_map):
    rows, feats = queries.shape
    vm = pl.BlockSpec(memory_space=pltpu.VMEM)
    sm = pl.BlockSpec(memory_space=pltpu.SMEM)
    return pl.pallas_call(
        pack_body, out_shape=jax.ShapeDtypeStruct((rows + positives.shape[1], feats), bf16),
        in_specs=[vm, vm, sm, sm], out_specs=vm, name="pack",
    )(queries, positives, shortlist, owner_map)


def info(ref, at, rows, extra):
    block = ref[at + rows:at + rows + extra, 0:2 * rows + LANES].astype(f32).astype(i32)
    return block[:, 0:rows], block[:, rows:2 * rows], block[0:1, 2 * rows:]


def a_body(n, group, base, *refs):
    xs, (w, prop), outs = refs[:n], refs[n:n + 2], refs[n + 2:2 * n + 2]
    x_all, acc, words, live, grads = refs[2 * n + 2:]
    step = pl.program_id(0)
    rows = outs[0].shape[0]
    per = LANES // WORD
    width = w.shape[1]

    @pl.when(step == 0)
    def _():
        for k in range(n):
            x_all[k * rows:(k + 1) * rows, :] = xs[k][0:rows, :]
            stored, label, present = info(xs[k], 0, rows, xs[k].shape[0] - rows)
            key = (stored - base[0]) * per + label // WORD
            bit = jnp.left_shift(jnp.ones_like(label), label % WORD)
            line = lax.broadcasted_iota(i32, (LANES, rows), 0)
            word = jnp.zeros((LANES, rows), i32)
            for p in range(stored.shape[0]):
                word = word | jnp.where(line == key[p:p + 1, :], bit[p:p + 1, :], 0)
            words[k * rows:(k + 1) * rows, :] = word.T
            live[k] = jnp.broadcast_to(present.astype(f32), (8, LANES))
        acc[...] = jnp.zeros_like(acc)

    lane = lax.broadcasted_iota(i32, (8, LANES), 1)
    probe = jnp.left_shift(jnp.ones((8, LANES), i32), lane % WORD)
    probe = jnp.broadcast_to(probe[0:1], (rows, LANES))
    flat = w[...].reshape(group * width, w.shape[2])
    scores = lax.dot_general(x_all[...], flat, NT, preferred_element_type=f32)
    for j in range(group):
        block = step * group + j
        weight = scale / prop[pl.ds(block, 1), :]
        idx = jnp.broadcast_to((block * per + lane // WORD)[0:1], (rows, LANES))
        for k in range(n):
            span = slice(k * rows, (k + 1) * rows)
            act = jnp.take_along_axis(live[k], jnp.broadcast_to(base[0] + block, (8, LANES)), axis=1)
            half = act[0:1] * (0.5 * scale)
            inv = act[0:1] * weight
            got = jnp.take_along_axis(words[span, :], idx, axis=1)
            s = scores[span, j * width:(j + 1) * width]
            g = half * jnp.tanh(0.5 * s) + (half - jnp.where((got & probe) != 0, inv, 0.0))
            grads[span, j * width:(j + 1) * width] = g.astype(bf16)
    acc[...] += lax.dot_general(grads[...], flat, NN, preferred_element_type=f32)

    @pl.when(step == pl.num_programs(0) - 1)
    def _():
        for k in range(n):
            outs[k][...] = acc[k * rows:(k + 1) * rows, :].astype(outs[k].dtype)


def a_call(xs, w, prop, base, group=4):
    n = len(xs)
    blocks, width, feats = w.shape
    rows = xs[0].shape[0] - 8
    group = min(group, blocks)
    whole = lambda shape: pl.BlockSpec(shape, lambda i, b: (0,) * len(shape))
    out_types = [jax.ShapeDtypeStruct((rows, feats), f32 if k == 0 else bf16) for k in range(n)]
    return pl.pallas_call(
        functools.partial(a_body, n, group),
        out_shape=out_types,
        grid_spec=pltpu.PrefetchScalarGridSpec(
            num_scalar_prefetch=1, grid=(blocks // group,),
            in_specs=[whole(x.shape) for x in xs] + [
                pl.BlockSpec((group, width, feats), lambda i, b: (i, 0, 0)),
                whole(prop.shape)],
            out_specs=[whole((rows, feats))] * n,
            scratch_shapes=[
                pltpu.VMEM((n * rows, feats), bf16), pltpu.VMEM((n * rows, feats), f32),
                pltpu.VMEM((n * rows, LANES), i32), pltpu.VMEM((n, 8, LANES), f32),
                pltpu.VMEM((n * rows, group * width), bf16)]),
        compiler_params=pltpu.CompilerParams(vmem_limit_bytes=48 << 20),
        cost_estimate=pl.CostEstimate(flops=4 * n * rows * blocks * width * feats,
            bytes_accessed=2 * blocks * width * feats, transcendentals=n * rows * blocks * width),
        name="owner_side",
    )(base, *xs, w, prop)


def b_body(n, pair, has_acc, blocks, rows, extra, where, *refs):
    xs, (w, inv), rest = refs[:n], refs[n:n + 2], refs[n + 2:]
    if has_acc:
        before, rest = rest[0], rest[1:]
    out, x_all, grads = rest
    labels = w.shape[0]
    each = labels // blocks
    base, off = where[0], where[1]
    line = lax.broadcasted_iota(i32, (blocks, rows), 0)
    probe = jnp.left_shift(jnp.ones((labels, rows), i32), lax.broadcasted_iota(i32, (labels, rows), 0) % each)
    spread = lambda a: jnp.broadcast_to(a[:, None, :], (blocks, each, rows)).reshape(labels, rows)
    shards = [(x, at) for x in xs for at in range(0, x.shape[0], rows + extra)]
    count = len(shards)
    for k, (x, at) in enumerate(shards):
        x_all[k * rows:(k + 1) * rows, :] = x[at:at + rows, :]
    for k0 in range(0, count, pair):
        scores = lax.dot_general(w[...], x_all[k0 * rows:(k0 + pair) * rows, :], NT, preferred_element_type=f32)
        for k in range(k0, k0 + pair):
            stored, label, present = info(*shards[k], rows, extra)
            local = label - off
            bit = jnp.where((local >= 0) & (local < each), jnp.left_shift(jnp.ones_like(label), local & (WORD - 1)), 0)
            word = jnp.zeros((blocks, rows), i32)
            for p in range(stored.shape[0]):
                word = word | jnp.where(line + base == stored[p:p + 1, :], bit[p:p + 1, :], 0)
            here = jnp.sum(jnp.where(lax.broadcasted_iota(i32, (blocks, LANES), 1) == line + base,
                           jnp.broadcast_to(present, (blocks, LANES)), 0), axis=1, keepdims=True)
            act = jnp.broadcast_to(here.astype(f32), (blocks, rows))
            half = spread(act * (0.5 * scale))
            got = (spread(word) & probe) != 0
            s = scores[:, (k - k0) * rows:(k - k0 + 1) * rows]
            g = half * jnp.tanh(0.5 * s) + (half - jnp.where(got, inv[...], 0.0))
            grads[:, k * rows:(k + 1) * rows] = g.astype(bf16)
    total = lax.dot_general(grads[...], x_all[...], NN, preferred_element_type=f32)
    out[...] = before[...] + total if has_acc else total


def b_call(xs, w, inv, where, blocks, rows, extra, before=None, pair=2):
    n = len(xs)
    count = sum(x.shape[0] for x in xs) // (rows + extra)
    pair = min(pair, count)
    labels, feats = w.shape
    vm = pl.BlockSpec(memory_space=pltpu.VMEM)
    sm = pl.BlockSpec(memory_space=pltpu.SMEM)
    more = [] if before is None else [before]
    return pl.pallas_call(
        functools.partial(b_body, n, pair, before is not None, blocks, rows, extra),
        out_shape=jax.ShapeDtypeStruct((labels, feats), f32),
        in_specs=[sm] + [vm] * (n + 2 + len(more)), out_specs=vm,
        scratch_shapes=[pltpu.VMEM((count * rows, feats), bf16), pltpu.VMEM((labels, count * rows), bf16)],
        input_output_aliases={n + 3: 0} if more else {},
        compiler_params=pltpu.CompilerParams(vmem_limit_bytes=56 << 20),
        cost_estimate=pl.CostEstimate(flops=4 * count * rows * labels * feats,
            bytes_accessed=2 * count * rows * feats, transcendentals=count * rows * labels),
        name="label_side",
    )(where, *xs, w, inv, *more)


def swap(x, axis, bit):
    size = lax.axis_size(axis)
    return lax.ppermute(x, axis, [(i, i ^ bit) for i in range(size)])


def gather_plane(x, bits):
    held = [x]
    for bit in bits:
        whole = held[0] if len(held) == 1 else jnp.concatenate(held, axis=0)
        held = [whole, swap(whole, "label", bit)]
    return held


def per_device(queries, label_weights, propensity, positives, shortlist, owner_map):
    label_count, dp_count = lax.axis_size("label"), lax.axis_size("dp")
    own, plane, section = (lax.axis_index(a) for a in ("label", "dp", "section"))
    blocks, width, feats = label_weights.shape
    rows, extra = queries.shape[0], positives.shape[1]
    packed = pack(queries, positives, shortlist, owner_map)
    bits = [1 << i for i in range(label_count.bit_length() - 1)]
    sections = lax.axis_size("section")
    each = width // (dp_count * sections)
    base = own * blocks

    if label_count == 4:
        by_x, by_y = swap(packed, "label", 1), swap(packed, "label", 2)
        cut = rows // 2
        far = jnp.concatenate([swap(by_x[:cut], "label", 2), swap(by_y[cut:], "label", 1)], axis=0)
        own_plane = [packed, by_x, by_y, far]
    else:
        own_plane = [packed]
        for bit in bits:
            own_plane = own_plane + [swap(x, "label", bit) for x in own_plane]
    planes = [own_plane]
    for shift in range(1, dp_count):
        got = lax.ppermute(packed, "dp", [(i, (i + shift) % dp_count) for i in range(dp_count)])
        planes.append(gather_plane(got, bits if shift % 2 else bits[::-1]))

    parts = a_call(own_plane, label_weights, propensity, base.astype(i32).reshape(1))
    query_grad = parts[0]
    for k in range(1, label_count):
        query_grad = query_grad + swap(parts[k], "label", k).astype(f32)

    sides = []
    for side in (section ^ 1, section) if sections == 2 else (section,):
        off = (plane * sections + side) * each
        w = lax.dynamic_slice_in_dim(label_weights, off, each, 1).reshape(blocks * each, feats)
        inv = scale / lax.dynamic_slice_in_dim(propensity, off, each, 1).reshape(blocks * each, 1)
        where = jnp.stack([base, off]).astype(i32)
        sides.append((w, jnp.broadcast_to(inv, (blocks * each, rows)), where))
    limit = 12
    groups, room = [], 0
    for held in planes[:-1]:
        if room < label_count:
            groups.append([])
            room = limit
        groups[-1] += held
        room -= label_count
    groups.append(planes[-1])
    totals = [None] * len(sides)
    for held in groups:
        for i, (w, inv, where) in enumerate(sides):
            totals[i] = b_call(held, w, inv, where, blocks, rows, extra, totals[i])
    weight_grad = totals[-1]
    if sections == 2:
        weight_grad = weight_grad + swap(totals[0], "section", 1)
    return query_grad, weight_grad.reshape(blocks, each, feats)


def solution(mesh):
    in_specs = (
        P(("dp", "label", "section"), None),
        P("label", None, None),
        P("label", None),
        P(("dp", "label", "section"), None),
        P(("dp", "label"), None),
        P(),
    )
    out_specs = (P(("dp", "label", "section"), None), P("label", ("dp", "section"), None))
    return jax.shard_map(
        per_device, mesh=mesh, in_specs=in_specs, out_specs=out_specs, check_vma=False
    )
```

time: 666 us -> 116 us (0.17)
  local copies, waits for them, and re-layouts: 233 us -> 7.54 us
  waiting for transfers between devices: 198 us -> 34.3 us
  matrix products: 118 us -> 0 us
  other arithmetic: 76.1 us -> 6.43 us
  Pallas kernels: 0 us -> 40.9 us
  starting transfers between devices: 0.12 us -> 24 us
  blocking collectives: 19.2 us -> 0 us
  between operations: 13.8 us -> 0.88 us
    gather x72 -> x0, local copies, waits for them, and re-layouts: 222 us -> none  [the longest x24 95.9 us: add_slot(): weights_sel = jnp.take(label_weights, slot_col, axis=0)]
    reduce_scatter x2 -> x0, waiting for transfers between devices: 187 us -> none  [the longest x1 171 us: per_device(): lax.psum_scatter(weight_part, ('dp', 'section'), scatter_dimension=1, til...]
    dot_general x50 -> x0, matrix products: 118 us -> none  [the longest x24 57.7 us: slot_grad(): jnp.einsum('jqd,jld->jql', tokens, weights_sel, preferred_element_type=jn...]
    reduce_or x24 -> x0, other arithmetic: 69.4 us -> none  [slot_grad(): jnp.any(pos_rows[:, :, :, None] == label_ids[:, None, None, :], axis=2)]
    pallas_call x0 -> x6, Pallas kernels: none -> 40.9 us  [the longest x4 25.8 us: b_call(): pl.pallas_call(functools.partial(b_body, n, pair, before is not None, blo...]
    ppermute x0 -> x17, waiting for transfers between devices: none -> 34.3 us  [the longest x14 27.3 us: swap(): return lax.ppermute(x, axis, [(i, i ^ bit) for i in range(size)])]
    ppermute x0 -> x17, starting transfers between devices: none -> 24 us  [the longest x14 17 us: swap(): return lax.ppermute(x, axis, [(i, i ^ bit) for i in range(size)])]
    all_gather x2 -> x0, blocking collectives: 19.2 us -> none  [the longest x1 9.71 us: per_device(): lax.all_gather(positives, 'label', axis=0, tiled=True)]
  transfers between devices with their start and end apart: 3 -> 17, of which waited for: 3 -> 7; matrix products, arithmetic and copies ran while one was open for 3% -> 7% of each run, Pallas kernels for 0% -> 30%
where the time goes in v1:
time: 116 us; the launch traced here: 114 us
  Pallas kernels  40.9 us (35%)
  waiting for transfers between devices  34.3 us (30%)
  starting transfers between devices  24 us (21%)
  local copies, waits for them, and re-layouts  7.54 us (6%)
  other arithmetic  6.43 us (6%)
    ppermute x14, waiting for transfers between devices, swap(): return lax.ppermute(x, axis, [(i, i ^ bit) for i in range(size)])  27.3 us
    pallas_call x4, Pallas kernels, b_call(): pl.pallas_call(functools.partial(b_body, n, pair, before is not None, blo...  25.8 us
    ppermute x14, starting transfers between devices, swap(): return lax.ppermute(x, axis, [(i, i ^ bit) for i in range(size)])  17 us
    pallas_call x1, Pallas kernels, a_call(): pl.pallas_call(functools.partial(a_body, n, group), out_shape=out_types,...  13.4 us
    ppermute x3, waiting for transfers between devices, per_device(): lax.ppermute(packed, 'dp', [(i, (i + shift) % dp_count) for i in range(dp...  6.99 us
    ppermute x3, starting transfers between devices, per_device(): lax.ppermute(packed, 'dp', [(i, (i + shift) % dp_count) for i in range(dp...  6.96 us
    add x1, other arithmetic, per_device(): weight_grad = weight_grad + swap(totals[0], 'section', 1)  4.1 us
    dynamic_slice x1, local copies, waits for them, and re-layouts, per_device(): lax.dynamic_slice_in_dim(label_weights, off, each, 1)  3.23 us
  transfers between devices with their start and end apart: 17, of which 7 were waited for; matrix products, arithmetic and copies ran while one was open for 7% of the time, Pallas kernels for 30%

profile of v1, /device:TPU:0, one launch (start us, length us, event | category | flops | bytes accessed | tf_op | source)
XLA Modules:
  0.0 114.1 jit_solution(5783590359436241480)
XLA Ops:
  0.6 1.4 %copy.11.positives = s32[128,8]{1,0:T(8,128)} copy(s32[128,8]{0,1:T(8,128)} %param.9) | data formatting | bytes 8192 | tf_op args[3]
  2.0 1.8 %pack.1.refs_0_ = bf16[136,1024]{1,0:T(8,128)(2,1)} custom-call(bf16[128,1024]{1,0:T(8,128)(2,1)} %queries.1, s32[128,8]{1,0:T(8,128)} %copy.11.positives, s32[1,48]{1,0:T(1,128)} %shortlist.1, s32[128]{0:T(128)} %owner_map.1), custom_call_target="tpu_custom_call" | custom-call | tf_op jit(solution)/shard_map/pack/pallas_call | solution.py:45
  3.8 3.0 %collective-permute-start.10 = (bf16[136,1024]{1,0:T(8,128)(2,1)}, bf16[136,1024]{1,0:T(8,128)(2,1)S(1)}, u32[]{:S(2)}, u32[]{:S(2)}) collective-permute-start(bf16[136,1024]{1,0:T(8,128)(2,1)} %pack.1.refs_0_), channel_id=1, source_target_pairs={{0,8},{8,16},{16,24},{24,0},{1,9},{9,17},{17,25},{25,1},{2,10},{10... | collective-permute-start | bytes 835592 | tf_op jit(solution)/shard_map/ppermute | solution.py:224
  6.9 1.5 %collective-permute-start = (bf16[136,1024]{1,0:T(8,128)(2,1)}, bf16[136,1024]{1,0:T(8,128)(2,1)S(1)}, u32[]{:S(2)}, u32[]{:S(2)}) collective-permute-start(bf16[136,1024]{1,0:T(8,128)(2,1)} %pack.1.refs_0_), channel_id=1, source_target_pairs={{0,2},{2,0},{4,6},{6,4},{1,3},{3,1},{5,7},{7,5},{8,10},{10,8},{12,... | collective-permute-start | bytes 835592 | tf_op jit(solution)/shard_map/ppermute | solution.py:191
  8.4 1.5 %collective-permute-start.1 = (bf16[136,1024]{1,0:T(8,128)(2,1)}, bf16[136,1024]{1,0:T(8,128)(2,1)S(1)}, u32[]{:S(2)}, u32[]{:S(2)}) collective-permute-start(bf16[136,1024]{1,0:T(8,128)(2,1)} %pack.1.refs_0_), channel_id=1, source_target_pairs={{0,4},{2,6},{4,0},{6,2},{1,5},{3,7},{5,1},{7,3},{8,12},{10,14},{12... | collective-permute-start | bytes 835592 | tf_op jit(solution)/shard_map/ppermute | solution.py:191
  9.9 2.6 %collective-permute-start.13 = (bf16[136,1024]{1,0:T(8,128)(2,1)}, bf16[136,1024]{1,0:T(8,128)(2,1)S(1)}, u32[]{:S(2)}, u32[]{:S(2)}) collective-permute-start(bf16[136,1024]{1,0:T(8,128)(2,1)} %pack.1.refs_0_), channel_id=1, source_target_pairs={{0,16},{8,24},{16,0},{24,8},{1,17},{9,25},{17,1},{25,9},{2,18},{10... | collective-permute-start | bytes 835592 | tf_op jit(solution)/shard_map/ppermute | solution.py:224
  12.5 1.3 %collective-permute-start.7 = (bf16[136,1024]{1,0:T(8,128)(2,1)}, bf16[136,1024]{1,0:T(8,128)(2,1)S(1)}, u32[]{:S(2)}, u32[]{:S(2)}) collective-permute-start(bf16[136,1024]{1,0:T(8,128)(2,1)} %pack.1.refs_0_), channel_id=1, source_target_pairs={{0,24},{8,0},{16,8},{24,16},{1,25},{9,1},{17,9},{25,17},{2,26},{10... | collective-permute-start | bytes 835592 | tf_op jit(solution)/shard_map/ppermute | solution.py:224
  13.8 3.2 %constant_dynamic-slice_fusion = (bf16[32,16,1024]{2,1,0:T(8,128)(2,1)}, bf16[32,16,1024]{2,1,0:T(8,128)(2,1)}) fusion(bf16[32,128,1024]{2,1,0:T(8,128)(2,1)} %refs_4_.1, s32[]{:T(128)S(6)} %select_n.9, s32[]{:T(128)S(6)} %select_n.8), kind=kLoop, calls=%fused_computation.11 | loop fusion | bytes 4194312 | tf_op jit(solution)/shard_map/dynamic_slice | solution.py:235
  17.0 1.4 %collective-permute-start.11 = (bf16[136,1024]{1,0:T(8,128)(2,1)S(1)}, bf16[136,1024]{1,0:T(8,128)(2,1)S(1)}, u32[]{:S(2)}, u32[]{:S(2)}) collective-permute-start(bf16[136,1024]{1,0:T(8,128)(2,1)S(1)} %collective-permute-done.10), channel_id=1, source_target_pairs={{0,2},{2,0},{4,6},{6,4},{1,3},{3,1},{5,7},{7,5},{8,10},{10,8},{12,... | collective-permute-start | bytes 835592 | tf_op jit(solution)/shard_map/ppermute | solution.py:191
  18.6 1.6 %collective-permute-start.2 = (bf16[64,1024]{1,0:T(8,128)(2,1)S(1)}, bf16[64,1024]{1,0:T(8,128)(2,1)S(1)}, u32[]{:S(2)}, u32[]{:S(2)}) collective-permute-start(bf16[64,1024]{1,0:T(8,128)(2,1)S(1)} %slice.8), channel_id=1, source_target_pairs={{0,4},{2,6},{4,0},{6,2},{1,5},{3,7},{5,1},{7,3},{8,12},{10,14},{12... | collective-permute-start | bytes 393224 | tf_op jit(solution)/shard_map/ppermute | solution.py:191
  20.8 7.0 %collective-permute-done.13 = bf16[136,1024]{1,0:T(8,128)(2,1)S(1)} collective-permute-done((bf16[136,1024]{1,0:T(8,128)(2,1)}, bf16[136,1024]{1,0:T(8,128)(2,1)S(1)}, u32[]{:S(2)}, u32[]{:S(2)}) %collective-permute-start.13) | collective-permute-done | bytes 278560 | tf_op jit(solution)/shard_map/ppermute | solution.py:224
  27.8 1.6 %collective-permute-start.14 = (bf16[136,1024]{1,0:T(8,128)(2,1)S(1)}, bf16[136,1024]{1,0:T(8,128)(2,1)S(1)}, u32[]{:S(2)}, u32[]{:S(2)}) collective-permute-start(bf16[136,1024]{1,0:T(8,128)(2,1)S(1)} %collective-permute-done.13), channel_id=1, source_target_pairs={{0,4},{2,6},{4,0},{6,2},{1,5},{3,7},{5,1},{7,3},{8,12},{10,14},{12... | collective-permute-start | bytes 835592 | tf_op jit(solution)/shard_map/ppermute | solution.py:191
  29.4 1.6 %collective-permute-start.8 = (bf16[136,1024]{1,0:T(8,128)(2,1)S(1)}, bf16[136,1024]{1,0:T(8,128)(2,1)S(1)}, u32[]{:S(2)}, u32[]{:S(2)}) collective-permute-start(bf16[136,1024]{1,0:T(8,128)(2,1)S(1)} %collective-permute-done.7), channel_id=1, source_target_pairs={{0,2},{2,0},{4,6},{6,4},{1,3},{3,1},{5,7},{7,5},{8,10},{10,8},{12,... | collective-permute-start | bytes 835592 | tf_op jit(solution)/shard_map/ppermute | solution.py:191
  31.6 5.8 %collective-permute-done.14 = bf16[136,1024]{1,0:T(8,128)(2,1)S(1)} collective-permute-done((bf16[136,1024]{1,0:T(8,128)(2,1)S(1)}, bf16[136,1024]{1,0:T(8,128)(2,1)S(1)}, u32[]{:S(2)}, u32[]{:S(2)}) %collective-permute-start.14) | collective-permute-done | bytes 278560 | tf_op jit(solution)/shard_map/ppermute | solution.py:191
  37.3 1.6 %collective-permute-start.15 = (bf16[272,1024]{1,0:T(8,128)(2,1)S(1)}, bf16[272,1024]{1,0:T(8,128)(2,1)}, u32[]{:S(2)}, u32[]{:S(2)}) collective-permute-start(bf16[272,1024]{1,0:T(8,128)(2,1)S(1)} %constant_dynamic-update-slice_fusion.6.refs_6_), channel_id=1, source_target_pairs={{0,2},{2,0},{4,6},{6,4},{1,3},{3,1},{5,7},{7,5},{8,10},{10,8},{12,... | collective-permute-start | bytes 1671176 | tf_op jit(solution)/shard_map/ppermute | solution.py:191
  39.0 1.6 %collective-permute-start.9 = (bf16[272,1024]{1,0:T(8,128)(2,1)S(1)}, bf16[272,1024]{1,0:T(8,128)(2,1)S(1)}, u32[]{:S(2)}, u32[]{:S(2)}) collective-permute-start(bf16[272,1024]{1,0:T(8,128)(2,1)S(1)} %constant_dynamic-update-slice_fusion.2.refs_0_), channel_id=1, source_target_pairs={{0,4},{2,6},{4,0},{6,2},{1,5},{3,7},{5,1},{7,3},{8,12},{10,14},{12... | collective-permute-start | bytes 1671176 | tf_op jit(solution)/shard_map/ppermute | solution.py:191
  41.4 7.9 %collective-permute-done.12.refs_5_ = bf16[272,1024]{1,0:T(8,128)(2,1)} collective-permute-done((bf16[272,1024]{1,0:T(8,128)(2,1)S(1)}, bf16[272,1024]{1,0:T(8,128)(2,1)}, u32[]{:S(2)}, u32[]{:S(2)}) %collective-permute-start.12) | collective-permute-done | bytes 557088 | tf_op jit(solution)/shard_map/ppermute | solution.py:191
  50.1 0.8 broadcast_in_dim.5.refs_9_.refs_3_
  50.9 7.6 %label_side.6.refs_4_ = f32[512,1024]{1,0:T(8,128)} custom-call(s32[2]{0:T(128)} %pad_add_fusion.1.where, bf16[136,1024]{1,0:T(8,128)(2,1)} %pack.1.refs_0_, bf16[136,1024]{1,0:T(8,128)(2,1)} %copy-done.4, bf16[136,1024]{1,0:T(8,128)(2,1)} %copy-done.1, bf16[136,1024]{1,0:T(8,128)(2,1)} %copy-done.6, bf16[272,1024]{1,0:T(8,128)(2,1)} %copy-done.11, ...), custom_call_target="tpu_custom_call" | custom-call | flops 3221225472 | bytes 3145728 | tf_op jit(solution)/shard_map/label_side/pallas_call | solution.py:176
  58.6 1.6 %collective-permute-done.9.refs_1_ = bf16[272,1024]{1,0:T(8,128)(2,1)S(1)} collective-permute-done((bf16[272,1024]{1,0:T(8,128)(2,1)S(1)}, bf16[272,1024]{1,0:T(8,128)(2,1)S(1)}, u32[]{:S(2)}, u32[]{:S(2)}) %collective-permute-start.9) | collective-permute-done | bytes 557088 | tf_op jit(solution)/shard_map/ppermute | solution.py:191
  60.1 0.8 copy-done.9
  61.0 5.3 %label_side.7 = f32[512,1024]{1,0:T(8,128)} custom-call(s32[2]{0:T(128)} %pad_add_fusion.1.where, bf16[272,1024]{1,0:T(8,128)(2,1)} %copy-done.8, bf16[272,1024]{1,0:T(8,128)(2,1)} %copy-done.9, bf16[512,1024]{1,0:T(8,128)(2,1)} %bitcast.9, f32[512,128]{1,0:T(8,128)} %broadcast_in_dim.5.refs_9_.refs_3_, ...), custom_call_target="tpu_custom_call", output_to_operand_aliasing={{}: (5, {})} | custom-call | flops 1073741824 | bytes 1048576 | tf_op jit(solution)/shard_map/label_side/pallas_call | solution.py:176
  66.3 13.4 %owner_side.1 = (f32[128,1024]{1,0:T(8,128)S(1)}, bf16[128,1024]{1,0:T(8,128)(2,1)S(1)}, bf16[128,1024]{1,0:T(8,128)(2,1)S(1)}, bf16[128,1024]{1,0:T(8,128)(2,1)S(1)}) custom-call(s32[1]{0:T(128)} %bitcast.base, bf16[136,1024]{1,0:T(8,128)(2,1)S(1)} %copy-done, bf16[136,1024]{1,0:T(8,128)(2,1)S(1)} %copy-done.5, bf16[136,1024]{1,0:T(8,128)(2,1)S(1)} %copy-done.2, ...), custom_call_target="tpu_custom_call" | custom-call | flops 8589934592 | bytes 8388608 | tf_op jit(solution)/shard_map/owner_side/pallas_call | solution.py:112
  79.7 1.6 %collective-permute-start.4 = (bf16[128,1024]{1,0:T(8,128)(2,1)S(1)}, bf16[128,1024]{1,0:T(8,128)(2,1)S(1)}, u32[]{:S(2)}, u32[]{:S(2)}) collective-permute-start(bf16[128,1024]{1,0:T(8,128)(2,1)S(1)} %get-tuple-element.7), channel_id=1, source_target_pairs={{0,2},{2,0},{4,6},{6,4},{1,3},{3,1},{5,7},{7,5},{8,10},{10,8},{12,... | collective-permute-start | bytes 786440 | tf_op jit(solution)/shard_map/ppermute | solution.py:191
  81.2 1.5 %collective-permute-start.5 = (bf16[128,1024]{1,0:T(8,128)(2,1)S(1)}, bf16[128,1024]{1,0:T(8,128)(2,1)S(1)}, u32[]{:S(2)}, u32[]{:S(2)}) collective-permute-start(bf16[128,1024]{1,0:T(8,128)(2,1)S(1)} %get-tuple-element.8), channel_id=1, source_target_pairs={{0,4},{2,6},{4,0},{6,2},{1,5},{3,7},{5,1},{7,3},{8,12},{10,14},{12... | collective-permute-start | bytes 786440 | tf_op jit(solution)/shard_map/ppermute | solution.py:191
  83.9 4.9 %collective-permute-done.4 = bf16[128,1024]{1,0:T(8,128)(2,1)S(1)} collective-permute-done((bf16[128,1024]{1,0:T(8,128)(2,1)S(1)}, bf16[128,1024]{1,0:T(8,128)(2,1)S(1)}, u32[]{:S(2)}, u32[]{:S(2)}) %collective-permute-start.4) | collective-permute-done | bytes 262176 | tf_op jit(solution)/shard_map/ppermute | solution.py:191
  88.8 6.4 %collective-permute-done.5 = bf16[128,1024]{1,0:T(8,128)(2,1)S(1)} collective-permute-done((bf16[128,1024]{1,0:T(8,128)(2,1)S(1)}, bf16[128,1024]{1,0:T(8,128)(2,1)S(1)}, u32[]{:S(2)}, u32[]{:S(2)}) %collective-permute-start.5) | collective-permute-done | bytes 262176 | tf_op jit(solution)/shard_map/ppermute | solution.py:191
  95.3 0.9 convert_add_fusion
  96.2 0.8 broadcast_in_dim.4.refs_9_.refs_3_
  97.1 7.6 %label_side.4.refs_4_ = f32[512,1024]{1,0:T(8,128)} custom-call(s32[2]{0:T(128)} %pad_add_fusion.where, bf16[136,1024]{1,0:T(8,128)(2,1)} %pack.1.refs_0_, bf16[136,1024]{1,0:T(8,128)(2,1)} %copy-done.4, bf16[136,1024]{1,0:T(8,128)(2,1)} %copy-done.1, bf16[136,1024]{1,0:T(8,128)(2,1)} %copy-done.6, bf16[272,1024]{1,0:T(8,128)(2,1)} %copy-done.11, ...), custom_call_target="tpu_custom_call" | custom-call | flops 3221225472 | bytes 3145728 | tf_op jit(solution)/shard_map/label_side/pallas_call | solution.py:176
  104.7 5.3 %label_side.5 = f32[512,1024]{1,0:T(8,128)} custom-call(s32[2]{0:T(128)} %pad_add_fusion.where, bf16[272,1024]{1,0:T(8,128)(2,1)} %copy-done.8, bf16[272,1024]{1,0:T(8,128)(2,1)} %copy-done.9, bf16[512,1024]{1,0:T(8,128)(2,1)} %bitcast.7, f32[512,128]{1,0:T(8,128)} %broadcast_in_dim.4.refs_9_.refs_3_, ...), custom_call_target="tpu_custom_call", output_to_operand_aliasing={{}: (5, {})} | custom-call | flops 1073741824 | bytes 1048576 | tf_op jit(solution)/shard_map/label_side/pallas_call | solution.py:176
  110.0 4.1 %add.33 = f32[512,1024]{1,0:T(8,128)} add(f32[512,1024]{1,0:T(8,128)} %label_side.5, f32[512,1024]{1,0:T(8,128)} %collective-permute-done.16) | non-fusion elementwise | flops 524288 | bytes 6291456 | tf_op jit(solution)/shard_map/add | solution.py:254
  (53 shorter events, 4.1 us)
Async XLA Ops:
  3.8 13.2 %collective-permute-start.10 = (bf16[136,1024]{1,0:T(8,128)(2,1)}, bf16[136,1024]{1,0:T(8,128)(2,1)S(1)}, u32[]{:S(2)}, u32[]{:S(2)}) collective-permute-start(bf16[136,1024]{1,0:T(8,128)(2,1)} %pack.1.refs_0_), channel_id=1, source_target_pairs={{0,8},{8,16},{16,24},{24,0},{1,9},{9,17},{17,25},{25,1},{2,10},{10... | collective-permute-start | bytes 835592 | tf_op jit(solution)/shard_map/ppermute | solution.py:224
  6.9 11.7 %collective-permute-start = (bf16[136,1024]{1,0:T(8,128)(2,1)}, bf16[136,1024]{1,0:T(8,128)(2,1)S(1)}, u32[]{:S(2)}, u32[]{:S(2)}) collective-permute-start(bf16[136,1024]{1,0:T(8,128)(2,1)} %pack.1.refs_0_), channel_id=1, source_target_pairs={{0,2},{2,0},{4,6},{6,4},{1,3},{3,1},{5,7},{7,5},{8,10},{10,8},{12,... | collective-permute-start | bytes 835592 | tf_op jit(solution)/shard_map/ppermute | solution.py:191
  8.4 11.8 %collective-permute-start.1 = (bf16[136,1024]{1,0:T(8,128)(2,1)}, bf16[136,1024]{1,0:T(8,128)(2,1)S(1)}, u32[]{:S(2)}, u32[]{:S(2)}) collective-permute-start(bf16[136,1024]{1,0:T(8,128)(2,1)} %pack.1.refs_0_), channel_id=1, source_target_pairs={{0,4},{2,6},{4,0},{6,2},{1,5},{3,7},{5,1},{7,3},{8,12},{10,14},{12... | collective-permute-start | bytes 835592 | tf_op jit(solution)/shard_map/ppermute | solution.py:191
  9.9 17.9 %collective-permute-start.13 = (bf16[136,1024]{1,0:T(8,128)(2,1)}, bf16[136,1024]{1,0:T(8,128)(2,1)S(1)}, u32[]{:S(2)}, u32[]{:S(2)}) collective-permute-start(bf16[136,1024]{1,0:T(8,128)(2,1)} %pack.1.refs_0_), channel_id=1, source_target_pairs={{0,16},{8,24},{16,0},{24,8},{1,17},{9,25},{17,1},{25,9},{2,18},{10... | collective-permute-start | bytes 835592 | tf_op jit(solution)/shard_map/ppermute | solution.py:224
  12.5 16.9 %collective-permute-start.7 = (bf16[136,1024]{1,0:T(8,128)(2,1)}, bf16[136,1024]{1,0:T(8,128)(2,1)S(1)}, u32[]{:S(2)}, u32[]{:S(2)}) collective-permute-start(bf16[136,1024]{1,0:T(8,128)(2,1)} %pack.1.refs_0_), channel_id=1, source_target_pairs={{0,24},{8,0},{16,8},{24,16},{1,25},{9,1},{17,9},{25,17},{2,26},{10... | collective-permute-start | bytes 835592 | tf_op jit(solution)/shard_map/ppermute | solution.py:224
  13.8 4.6 %copy-start.3 = (f32[32,128]{1,0:T(8,128)S(1)}, f32[32,128]{1,0:T(8,128)}, u32[]{:S(2)}) copy-start(f32[32,128]{1,0:T(8,128)} %refs_5_.1) | copy-start | bytes 49156
  17.0 13.9 %collective-permute-start.11 = (bf16[136,1024]{1,0:T(8,128)(2,1)S(1)}, bf16[136,1024]{1,0:T(8,128)(2,1)S(1)}, u32[]{:S(2)}, u32[]{:S(2)}) collective-permute-start(bf16[136,1024]{1,0:T(8,128)(2,1)S(1)} %collective-permute-done.10), channel_id=1, source_target_pairs={{0,2},{2,0},{4,6},{6,4},{1,3},{3,1},{5,7},{7,5},{8,10},{10,8},{12,... | collective-permute-start | bytes 835592 | tf_op jit(solution)/shard_map/ppermute | solution.py:191
  18.6 22.9 %copy-start.4 = (bf16[136,1024]{1,0:T(8,128)(2,1)}, bf16[136,1024]{1,0:T(8,128)(2,1)S(1)}, u32[]{:S(2)}) copy-start(bf16[136,1024]{1,0:T(8,128)(2,1)S(1)} %collective-permute-done.refs_1_) | copy-start | bytes 835588
  18.6 22.8 %collective-permute-start.2 = (bf16[64,1024]{1,0:T(8,128)(2,1)S(1)}, bf16[64,1024]{1,0:T(8,128)(2,1)S(1)}, u32[]{:S(2)}, u32[]{:S(2)}) collective-permute-start(bf16[64,1024]{1,0:T(8,128)(2,1)S(1)} %slice.8), channel_id=1, source_target_pairs={{0,4},{2,6},{4,0},{6,2},{1,5},{3,7},{5,1},{7,3},{8,12},{10,14},{12... | collective-permute-start | bytes 393224 | tf_op jit(solution)/shard_map/ppermute | solution.py:191
  20.2 21.2 %copy-start.1 = (bf16[136,1024]{1,0:T(8,128)(2,1)}, bf16[136,1024]{1,0:T(8,128)(2,1)S(1)}, u32[]{:S(2)}) copy-start(bf16[136,1024]{1,0:T(8,128)(2,1)S(1)} %collective-permute-done.1.refs_2_) | copy-start | bytes 835588
  20.2 21.2 %collective-permute-start.3 = (bf16[72,1024]{1,0:T(8,128)(2,1)S(1)}, bf16[72,1024]{1,0:T(8,128)(2,1)S(1)}, u32[]{:S(2)}, u32[]{:S(2)}) collective-permute-start(bf16[72,1024]{1,0:T(8,128)(2,1)S(1)} %slice.9), channel_id=1, source_target_pairs={{0,2},{2,0},{4,6},{6,4},{1,3},{3,1},{5,7},{7,5},{8,10},{10,8},{12,... | collective-permute-start | bytes 442376 | tf_op jit(solution)/shard_map/ppermute | solution.py:191
  27.8 9.5 %collective-permute-start.14 = (bf16[136,1024]{1,0:T(8,128)(2,1)S(1)}, bf16[136,1024]{1,0:T(8,128)(2,1)S(1)}, u32[]{:S(2)}, u32[]{:S(2)}) collective-permute-start(bf16[136,1024]{1,0:T(8,128)(2,1)S(1)} %collective-permute-done.13), channel_id=1, source_target_pairs={{0,4},{2,6},{4,0},{6,2},{1,5},{3,7},{5,1},{7,3},{8,12},{10,14},{12... | collective-permute-start | bytes 835592 | tf_op jit(solution)/shard_map/ppermute | solution.py:191
  29.4 9.6 %collective-permute-start.8 = (bf16[136,1024]{1,0:T(8,128)(2,1)S(1)}, bf16[136,1024]{1,0:T(8,128)(2,1)S(1)}, u32[]{:S(2)}, u32[]{:S(2)}) collective-permute-start(bf16[136,1024]{1,0:T(8,128)(2,1)S(1)} %collective-permute-done.7), channel_id=1, source_target_pairs={{0,2},{2,0},{4,6},{6,4},{1,3},{3,1},{5,7},{7,5},{8,10},{10,8},{12,... | collective-permute-start | bytes 835592 | tf_op jit(solution)/shard_map/ppermute | solution.py:191
  31.0 19.9 %copy-start.11 = (bf16[272,1024]{1,0:T(8,128)(2,1)}, bf16[272,1024]{1,0:T(8,128)(2,1)S(1)}, u32[]{:S(2)}) copy-start(bf16[272,1024]{1,0:T(8,128)(2,1)S(1)} %constant_dynamic-update-slice_fusion.4.refs_4_) | copy-start | bytes 1671172
  31.0 18.4 %collective-permute-start.12 = (bf16[272,1024]{1,0:T(8,128)(2,1)S(1)}, bf16[272,1024]{1,0:T(8,128)(2,1)}, u32[]{:S(2)}, u32[]{:S(2)}) collective-permute-start(bf16[272,1024]{1,0:T(8,128)(2,1)S(1)} %constant_dynamic-update-slice_fusion.4.refs_4_), channel_id=1, source_target_pairs={{0,4},{2,6},{4,0},{6,2},{1,5},{3,7},{5,1},{7,3},{8,12},{10,14},{12... | collective-permute-start | bytes 1671176 | tf_op jit(solution)/shard_map/ppermute | solution.py:191
  37.3 13.6 %copy-start.10 = (bf16[272,1024]{1,0:T(8,128)(2,1)}, bf16[272,1024]{1,0:T(8,128)(2,1)S(1)}, u32[]{:S(2)}) copy-start(bf16[272,1024]{1,0:T(8,128)(2,1)S(1)} %constant_dynamic-update-slice_fusion.6.refs_6_) | copy-start | bytes 1671172
  37.3 12.7 %collective-permute-start.15 = (bf16[272,1024]{1,0:T(8,128)(2,1)S(1)}, bf16[272,1024]{1,0:T(8,128)(2,1)}, u32[]{:S(2)}, u32[]{:S(2)}) collective-permute-start(bf16[272,1024]{1,0:T(8,128)(2,1)S(1)} %constant_dynamic-update-slice_fusion.6.refs_6_), channel_id=1, source_target_pairs={{0,2},{2,0},{4,6},{6,4},{1,3},{3,1},{5,7},{7,5},{8,10},{10,8},{12,... | collective-permute-start | bytes 1671176 | tf_op jit(solution)/shard_map/ppermute | solution.py:191
  39.0 19.5 %copy-start.8 = (bf16[272,1024]{1,0:T(8,128)(2,1)}, bf16[272,1024]{1,0:T(8,128)(2,1)S(1)}, u32[]{:S(2)}) copy-start(bf16[272,1024]{1,0:T(8,128)(2,1)S(1)} %constant_dynamic-update-slice_fusion.2.refs_0_) | copy-start | bytes 1671172
  39.0 21.1 %collective-permute-start.9 = (bf16[272,1024]{1,0:T(8,128)(2,1)S(1)}, bf16[272,1024]{1,0:T(8,128)(2,1)S(1)}, u32[]{:S(2)}, u32[]{:S(2)}) collective-permute-start(bf16[272,1024]{1,0:T(8,128)(2,1)S(1)} %constant_dynamic-update-slice_fusion.2.refs_0_), channel_id=1, source_target_pairs={{0,4},{2,6},{4,0},{6,2},{1,5},{3,7},{5,1},{7,3},{8,12},{10,14},{12... | collective-permute-start | bytes 1671176 | tf_op jit(solution)/shard_map/ppermute | solution.py:191
  41.4 9.5 %copy-start.6 = (bf16[136,1024]{1,0:T(8,128)(2,1)}, bf16[136,1024]{1,0:T(8,128)(2,1)S(1)}, u32[]{:S(2)}) copy-start(bf16[136,1024]{1,0:T(8,128)(2,1)S(1)} %constant_dynamic-update-slice_fusion.refs_3_) | copy-start | bytes 835588
  58.5 7.7 %copy-start = (bf16[136,1024]{1,0:T(8,128)(2,1)S(1)}, bf16[136,1024]{1,0:T(8,128)(2,1)}, u32[]{:S(2)}) copy-start(bf16[136,1024]{1,0:T(8,128)(2,1)} %pack.1.refs_0_) | copy-start | bytes 835588
  58.5 7.7 %copy-start.2 = (bf16[136,1024]{1,0:T(8,128)(2,1)S(1)}, bf16[136,1024]{1,0:T(8,128)(2,1)}, u32[]{:S(2)}) copy-start(bf16[136,1024]{1,0:T(8,128)(2,1)} %copy-done.1) | copy-start | bytes 835588
  58.5 7.7 %copy-start.5 = (bf16[136,1024]{1,0:T(8,128)(2,1)S(1)}, bf16[136,1024]{1,0:T(8,128)(2,1)}, u32[]{:S(2)}) copy-start(bf16[136,1024]{1,0:T(8,128)(2,1)} %copy-done.4) | copy-start | bytes 835588
  58.5 7.7 %copy-start.7 = (bf16[136,1024]{1,0:T(8,128)(2,1)S(1)}, bf16[136,1024]{1,0:T(8,128)(2,1)}, u32[]{:S(2)}) copy-start(bf16[136,1024]{1,0:T(8,128)(2,1)} %copy-done.6) | copy-start | bytes 835588
  60.1 0.8 copy-start.9
  66.3 43.7 %collective-permute-start.16 = (f32[512,1024]{1,0:T(8,128)}, f32[512,1024]{1,0:T(8,128)}, u32[]{:S(2)}, u32[]{:S(2)}) collective-permute-start(f32[512,1024]{1,0:T(8,128)} %label_side.7), channel_id=1, source_target_pairs={{0,1},{1,0},{2,3},{3,2},{4,5},{5,4},{6,7},{7,6},{8,9},{9,8},{10,11... | collective-permute-start | bytes 6291464 | tf_op jit(solution)/shard_map/ppermute | solution.py:191
  79.7 9.2 %collective-permute-start.4 = (bf16[128,1024]{1,0:T(8,128)(2,1)S(1)}, bf16[128,1024]{1,0:T(8,128)(2,1)S(1)}, u32[]{:S(2)}, u32[]{:S(2)}) collective-permute-start(bf16[128,1024]{1,0:T(8,128)(2,1)S(1)} %get-tuple-element.7), channel_id=1, source_target_pairs={{0,2},{2,0},{4,6},{6,4},{1,3},{3,1},{5,7},{7,5},{8,10},{10,8},{12,... | collective-permute-start | bytes 786440 | tf_op jit(solution)/shard_map/ppermute | solution.py:191
  81.2 14.0 %collective-permute-start.5 = (bf16[128,1024]{1,0:T(8,128)(2,1)S(1)}, bf16[128,1024]{1,0:T(8,128)(2,1)S(1)}, u32[]{:S(2)}, u32[]{:S(2)}) collective-permute-start(bf16[128,1024]{1,0:T(8,128)(2,1)S(1)} %get-tuple-element.8), channel_id=1, source_target_pairs={{0,4},{2,6},{4,0},{6,2},{1,5},{3,7},{5,1},{7,3},{8,12},{10,14},{12... | collective-permute-start | bytes 786440 | tf_op jit(solution)/shard_map/ppermute | solution.py:191
  82.8 12.5 %collective-permute-start.6 = (bf16[128,1024]{1,0:T(8,128)(2,1)S(1)}, bf16[128,1024]{1,0:T(8,128)(2,1)S(1)}, u32[]{:S(2)}, u32[]{:S(2)}) collective-permute-start(bf16[128,1024]{1,0:T(8,128)(2,1)S(1)} %get-tuple-element.9), channel_id=1, source_target_pairs={{0,6},{2,4},{4,2},{6,0},{1,7},{3,5},{5,3},{7,1},{8,14},{10,12},{12... | collective-permute-start | bytes 786440 | tf_op jit(solution)/shard_map/ppermute | solution.py:191

commit v2 on v1

v2 whole, which is shorter than its diff:
```python
import functools
import jax
import jax.numpy as jnp
from jax import lax
from jax.experimental import pallas as pl
from jax.experimental.pallas import tpu as pltpu
from jax.sharding import PartitionSpec as P

scale = 0.25
NT = (((1,), (1,)), ((), ()))
NN = (((1,), (0,)), ((), ()))
f32, bf16, i32 = jnp.float32, jnp.bfloat16, jnp.int32
LANES = 128
WORD = 32


def pack_body(queries, positives, shortlist, owner_map, out):
    rows, feats = queries.shape
    count = positives.shape[0]
    short_len = shortlist.shape[1]
    width = LANES
    out[0:rows, :] = queries[...]
    pos = positives[...]
    entry = pos // width
    label = pos - entry * width
    ids = lax.broadcasted_iota(i32, (count, LANES), 1)
    stored = jnp.zeros((count, rows), i32)
    present = jnp.zeros((count, LANES), i32)
    for e in range(short_len):
        place = owner_map[shortlist[0, e]]
        stored = jnp.where(entry == e, place, stored)
        present = jnp.where(ids == place, 1, present)
    out[rows:, :] = jnp.zeros((out.shape[0] - rows, feats), bf16)
    out[rows:, 0:rows] = stored.astype(f32).astype(bf16)
    out[rows:, rows:2 * rows] = label.astype(f32).astype(bf16)
    out[rows:, 2 * rows:2 * rows + LANES] = present.astype(f32).astype(bf16)


def pack(queries, positives, shortlist, owner_map):
    rows, feats = queries.shape
    vm = pl.BlockSpec(memory_space=pltpu.VMEM)
    sm = pl.BlockSpec(memory_space=pltpu.SMEM)
    return pl.pallas_call(
        pack_body, out_shape=jax.ShapeDtypeStruct((rows + positives.shape[0], feats), bf16),
        in_specs=[vm, vm, sm, sm], out_specs=vm, name="pack",
    )(queries, positives, shortlist, owner_map)


def info(ref, at, rows, extra):
    block = ref[at + rows:at + rows + extra, 0:2 * rows + LANES].astype(f32).astype(i32)
    return block[:, 0:rows], block[:, rows:2 * rows], block[0:1, 2 * rows:]


def a_body(n, group, base, *refs):
    xs, (w, prop), outs = refs[:n], refs[n:n + 2], refs[n + 2:2 * n + 2]
    x_all, acc, words, live, grads = refs[2 * n + 2:]
    rows = outs[0].shape[0]
    per = LANES // WORD
    blocks, width, feats = w.shape
    for k in range(n):
        x_all[k * rows:(k + 1) * rows, :] = xs[k][0:rows, :]
        stored, label, present = info(xs[k], 0, rows, xs[k].shape[0] - rows)
        key = (stored - base[0]) * per + label // WORD
        bit = jnp.left_shift(jnp.ones_like(label), label % WORD)
        line = lax.broadcasted_iota(i32, (LANES, rows), 0)
        word = jnp.zeros((LANES, rows), i32)
        for p in range(stored.shape[0]):
            word = word | jnp.where(line == key[p:p + 1, :], bit[p:p + 1, :], 0)
        words[k * rows:(k + 1) * rows, :] = word.T
        live[k] = jnp.broadcast_to(present.astype(f32), (8, LANES))
    lane = lax.broadcasted_iota(i32, (8, LANES), 1)
    probe = jnp.left_shift(jnp.ones((8, LANES), i32), lane % WORD)
    probe = jnp.broadcast_to(probe[0:1], (rows, LANES))

    def step_fn(step, first):
        flat = w[pl.ds(step * group, group)].reshape(group * width, feats)
        scores = lax.dot_general(x_all[...], flat, NT, preferred_element_type=f32)
        for j in range(group):
            block = step * group + j
            weight = scale / prop[pl.ds(block, 1), :]
            idx = jnp.broadcast_to((block * per + lane // WORD)[0:1], (rows, LANES))
            for k in range(n):
                span = slice(k * rows, (k + 1) * rows)
                act = jnp.take_along_axis(live[k], jnp.broadcast_to(base[0] + block, (8, LANES)), axis=1)
                half = act[0:1] * (0.5 * scale)
                inv = act[0:1] * weight
                got = jnp.take_along_axis(words[span, :], idx, axis=1)
                s = scores[span, j * width:(j + 1) * width]
                g = half * jnp.tanh(0.5 * s) + (half - jnp.where((got & probe) != 0, inv, 0.0))
                grads[span, j * width:(j + 1) * width] = g.astype(bf16)
        total = lax.dot_general(grads[...], flat, NN, preferred_element_type=f32)
        if first:
            acc[...] = total
        else:
            acc[...] += total
    steps = blocks // group
    for i in range(steps):
        step_fn(i, i == 0)
    for k in range(n):
        outs[k][...] = acc[k * rows:(k + 1) * rows, :].astype(outs[k].dtype)


def a_call(xs, w, prop, base, rows, types, group=8):
    n = len(xs)
    blocks, width, feats = w.shape
    group = min(group, blocks)
    out_types = [jax.ShapeDtypeStruct((rows, feats), kind) for kind in types]
    vm = pl.BlockSpec(memory_space=pltpu.VMEM)
    sm = pl.BlockSpec(memory_space=pltpu.SMEM)
    return pl.pallas_call(
        functools.partial(a_body, n, group),
        out_shape=out_types,
        in_specs=[sm] + [vm] * (n + 2), out_specs=[vm] * n,
        scratch_shapes=[
                pltpu.VMEM((n * rows, feats), bf16), pltpu.VMEM((n * rows, feats), f32),
                pltpu.VMEM((n * rows, LANES), i32), pltpu.VMEM((n, 8, LANES), f32),
                pltpu.VMEM((n * rows, group * width), bf16)],
        compiler_params=pltpu.CompilerParams(vmem_limit_bytes=40 << 20),
        cost_estimate=pl.CostEstimate(flops=1, bytes_accessed=1, transcendentals=0),
        name="owner_side",
    )(base, *xs, w, prop)


def b_body(n, sides, pair, has_acc, blocks, rows, extra, where, *refs):
    xs, ws, invs, rest = refs[:n], refs[n:n + sides], refs[n + sides:n + 2 * sides], refs[n + 2 * sides:]
    before = None
    if has_acc:
        before, rest = rest[:sides], rest[sides:]
    outs, (x_all, grads) = rest[:sides], rest[sides:]
    labels = ws[0].shape[0]
    each = labels // blocks
    base = where[0]
    line = lax.broadcasted_iota(i32, (blocks, rows), 0)
    probe = jnp.left_shift(jnp.ones((labels, rows), i32), lax.broadcasted_iota(i32, (labels, rows), 0) % each)
    spread = lambda a: jnp.broadcast_to(a[:, None, :], (blocks, each, rows)).reshape(labels, rows)
    shards = [(x, at) for x in xs for at in range(0, x.shape[0], rows + extra)]
    count = len(shards)
    for k, (x, at) in enumerate(shards):
        x_all[k * rows:(k + 1) * rows, :] = x[at:at + rows, :]
    for side in range(sides):
        off = where[1 + side]
        for k0 in range(0, count, pair):
            scores = lax.dot_general(ws[side][...], x_all[k0 * rows:(k0 + pair) * rows, :], NT, preferred_element_type=f32)
            for k in range(k0, k0 + pair):
                stored, label, present = info(*shards[k], rows, extra)
                local = label - off
                bit = jnp.where((local >= 0) & (local < each), jnp.left_shift(jnp.ones_like(label), local & (WORD - 1)), 0)
                word = jnp.zeros((blocks, rows), i32)
                for p in range(stored.shape[0]):
                    word = word | jnp.where(line + base == stored[p:p + 1, :], bit[p:p + 1, :], 0)
                here = jnp.sum(jnp.where(lax.broadcasted_iota(i32, (blocks, LANES), 1) == line + base,
                               jnp.broadcast_to(present, (blocks, LANES)), 0), axis=1, keepdims=True)
                act = jnp.broadcast_to(here.astype(f32), (blocks, rows))
                half = spread(act * (0.5 * scale))
                got = (spread(word) & probe) != 0
                s = scores[:, (k - k0) * rows:(k - k0 + 1) * rows]
                g = half * jnp.tanh(0.5 * s) + (half - jnp.where(got, invs[side][...], 0.0))
                grads[:, k * rows:(k + 1) * rows] = g.astype(bf16)
        total = lax.dot_general(grads[...], x_all[...], NN, preferred_element_type=f32)
        outs[side][...] = before[side][...] + total if has_acc else total


def b_call(xs, ws, invs, where, blocks, rows, extra, before=None, pair=2):
    n, sides = len(xs), len(ws)
    count = sum(x.shape[0] for x in xs) // (rows + extra)
    pair = min(pair, count)
    labels, feats = ws[0].shape
    vm = pl.BlockSpec(memory_space=pltpu.VMEM)
    sm = pl.BlockSpec(memory_space=pltpu.SMEM)
    more = [] if before is None else list(before)
    return pl.pallas_call(
        functools.partial(b_body, n, sides, pair, before is not None, blocks, rows, extra),
        out_shape=[jax.ShapeDtypeStruct((labels, feats), f32)] * sides,
        in_specs=[sm] + [vm] * (n + 2 * sides + len(more)), out_specs=[vm] * sides,
        scratch_shapes=[pltpu.VMEM((count * rows, feats), bf16), pltpu.VMEM((labels, count * rows), bf16)],
        compiler_params=pltpu.CompilerParams(vmem_limit_bytes=40 << 20),
        cost_estimate=pl.CostEstimate(flops=1, bytes_accessed=1, transcendentals=0),
        name="label_side",
    )(where, *xs, *ws, *invs, *more)


def swap(x, axis, bit):
    size = lax.axis_size(axis)
    return lax.ppermute(x, axis, [(i, i ^ bit) for i in range(size)])


def after(x, *done):
    return lax.optimization_barrier((x,) + done)[0]


def per_device(queries, label_weights, propensity, positives, shortlist, owner_map):
    label_count, dp_count = lax.axis_size("label"), lax.axis_size("dp")
    sections = lax.axis_size("section")
    own, plane, section = (lax.axis_index(a) for a in ("label", "dp", "section"))
    blocks, width, feats = label_weights.shape
    rows, extra = queries.shape[0], positives.shape[1]
    packed = pack(queries, positives.T, shortlist, owner_map)
    bits = [1 << i for i in range(label_count.bit_length() - 1)]
    each = width // (dp_count * sections)
    base = own * blocks

    offs = [(plane * sections + side) * each for side in ([section ^ 1, section] if sections == 2 else [section])]
    ws = [lax.dynamic_slice_in_dim(label_weights, off, each, 1).reshape(blocks * each, feats) for off in offs]
    invs = [scale / lax.dynamic_slice_in_dim(propensity, off, each, 1).reshape(blocks * each, 1) for off in offs]
    invs = [jnp.broadcast_to(inv, (blocks * each, rows)) for inv in invs]
    one = base.astype(i32).reshape(1)
    cut = label_count // 2 + 1
    first, second = list(range(1, cut)), list(range(cut, label_count)) + [0]
    ring = list(range(0, dp_count, 2))[:1] + list(range(1, dp_count, 2)) + list(range(0, dp_count, 2))[:0:-1]
    forward = [(a, ring[(i + 1) % dp_count]) for i, a in enumerate(ring)]
    backward = [(b, a) for a, b in forward]

    def owner_call(ks, one):
        out = a_call([here[k] for k in ks], label_weights, propensity, one, rows,
                     [f32 if k == 0 else bf16 for k in ks])
        return dict(zip(ks, out))

    def label_call(xs, before, *done, only=None):
        pick = range(len(offs)) if only is None else [only]
        where = after(jnp.stack([base] + [offs[k] for k in pick]).astype(i32), *done)
        out = b_call(xs, [ws[k] for k in pick], [invs[k] for k in pick], where, blocks, rows, extra,
                     None if before is None else [before[k] for k in pick])
        return out

    here = {0: packed}
    for k in first:
        here[k] = swap(packed, "label", k)
    column = lax.ppermute(packed, "dp", forward)
    gate = [here[k] for k in first] + [column]
    for k in second[:-1]:
        here[k] = swap(after(packed, *gate), "label", k)
    columns = [column]
    orders = [bits if k % 2 else bits[::-1] for k in range(dp_count - 2)]

    def spread(x, order, *done):
        for bit in order:
            x = jnp.concatenate([x, swap(after(x, *done), "label", bit)], axis=0)
        return x

    halves = [spread(column, orders[0][:-1], *gate)]
    for _ in range(dp_count - 3):
        columns.append(lax.ppermute(after(columns[-1], *gate), "dp", forward))
    parts = owner_call(first, after(one, *gate, *ws, *invs))
    gate = [halves[0], parts[1]] + columns[1:] + [here[k] for k in second[:-1]]
    own_plane = after(jnp.concatenate([here[k] for k in range(label_count)], axis=0), *gate)
    next_plane = lax.ppermute(own_plane, "dp", backward)
    back = {k: swap(after(parts[k], *gate), "label", k) for k in first}
    for k in range(1, len(columns)):
        halves.append(spread(columns[k], orders[k][:-1], *gate))
    tops = [swap(after(halves[0], *gate), "label", orders[0][-1])]
    parts.update(owner_call(second, after(one, *gate)))
    gate = [parts[0]] + halves[1:] + [back[k] for k in first]
    for k in second[:-1]:
        back[k] = swap(after(parts[k], *gate), "label", k)
    for k in range(1, len(columns)):
        tops.append(swap(after(halves[k], *gate), "label", orders[k][-1]))
    total = label_call([own_plane, halves[0]], None, *gate)
    gate = [total[0], next_plane, tops[0]] + [back[k] for k in second[:-1]]
    total = label_call([next_plane, tops[0]], total, *gate)
    for k in range(1, len(columns)):
        xs = [halves[k], tops[k]]
        if k < len(columns) - 1 or len(offs) == 1:
            total = label_call(xs, total, total[0])
        else:
            theirs = label_call(xs, total, total[0], only=0)[0]
            theirs = swap(theirs, "section", 1)
            mine = label_call(xs, total, total[0], only=1)[0]
            total = [mine + theirs]
    query_grad = parts[0]
    for k in range(1, label_count):
        query_grad = query_grad + back[k].astype(f32)
    return query_grad, total[0].reshape(blocks, each, feats)


def solution(mesh):
    in_specs = (
        P(("dp", "label", "section"), None),
        P("label", None, None),
        P("label", None),
        P(("dp", "label", "section"), None),
        P(("dp", "label"), None),
        P(),
    )
    out_specs = (P(("dp", "label", "section"), None), P("label", ("dp", "section"), None))
    return jax.shard_map(
        per_device, mesh=mesh, in_specs=in_specs, out_specs=out_specs, check_vma=False
    )
```

time: 116 us -> 75.3 us (0.65); the launches traced: 114 us -> 75 us
  Pallas kernels: 40.9 us -> 25.1 us
  waiting for transfers between devices: 34.3 us -> 21.2 us
  starting transfers between devices: 24 us -> 18.3 us
  other arithmetic: 6.43 us -> 3.13 us
    pallas_call x4, Pallas kernels: 25.8 us -> 13.4 us  [b_call(): pl.pallas_call(functools.partial(b_body, n, sides, pair, before is not No...]
    ppermute x14 -> x11, waiting for transfers between devices: 27.3 us -> 19 us  [swap(): return lax.ppermute(x, axis, [(i, i ^ bit) for i in range(size)])]
    ppermute x3, waiting for transfers between devices: 6.99 us -> 2.13 us  [the longest x1 2.13 us: per_device(): column = lax.ppermute(packed, 'dp', forward)]
    ppermute x14 -> x11, starting transfers between devices: 17 us -> 13.6 us  [swap(): return lax.ppermute(x, axis, [(i, i ^ bit) for i in range(size)])]
    pallas_call x1 -> x2, Pallas kernels: 13.4 us -> 9.95 us  [a_call(): pl.pallas_call(functools.partial(a_body, n, group), out_shape=out_types,...]
    ppermute x3, starting transfers between devices: 6.96 us -> 4.74 us  [the longest x1 2.29 us: per_device(): next_plane = lax.ppermute(own_plane, 'dp', backward)]
    add x2, other arithmetic: 5.03 us -> 2.82 us  [the longest x1 1.88 us: per_device(): total = [mine + theirs]]
    dynamic_slice x1, local copies, waits for them, and re-layouts: 3.23 us -> 1.73 us  [per_device(): lax.dynamic_slice_in_dim(label_weights, off, each, 1)]
  transfers between devices with their start and end apart: 17 -> 14, of which waited for: 7 -> 7; matrix products, arithmetic and copies ran while one was open for 7% -> 6% of each run, Pallas kernels for 30% -> 28%
where the time goes in v2:
time: 75.3 us; the launch traced here: 75 us
  Pallas kernels  25.1 us (33%)
  waiting for transfers between devices  21.2 us (28%)
  starting transfers between devices  18.3 us (24%)
  local copies, waits for them, and re-layouts  6.56 us (9%)
  other arithmetic  3.13 us (4%)
  between operations  0.81 us (1%)
    ppermute x11, waiting for transfers between devices, swap(): return lax.ppermute(x, axis, [(i, i ^ bit) for i in range(size)])  19 us
    ppermute x11, starting transfers between devices, swap(): return lax.ppermute(x, axis, [(i, i ^ bit) for i in range(size)])  13.6 us
    pallas_call x4, Pallas kernels, b_call(): pl.pallas_call(functools.partial(b_body, n, sides, pair, before is not No...  13.4 us
    pallas_call x2, Pallas kernels, a_call(): pl.pallas_call(functools.partial(a_body, n, group), out_shape=out_types,...  9.95 us
    unnamed x8, local copies, waits for them, and re-layouts  3.43 us
    ppermute x1, starting transfers between devices, per_device(): next_plane = lax.ppermute(own_plane, 'dp', backward)  2.29 us
    ppermute x1, waiting for transfers between devices, per_device(): column = lax.ppermute(packed, 'dp', forward)  2.13 us
    add x1, other arithmetic, per_device(): total = [mine + theirs]  1.88 us
  transfers between devices with their start and end apart: 14, of which 7 were waited for; matrix products, arithmetic and copies ran while one was open for 6% of the time, Pallas kernels for 28%

profile of v2, /device:TPU:0, one launch (start us, length us, event | category | flops | bytes accessed | tf_op | source)
XLA Modules:
  0.0 75.0 jit_solution(12972735063440461787)
XLA Ops:
  0.6 1.7 %pack.1.refs_1_ = bf16[136,1024]{1,0:T(8,128)(2,1)} custom-call(bf16[128,1024]{1,0:T(8,128)(2,1)} %queries.1, s32[8,128]{1,0:T(8,128)} %bitcast.14, s32[1,48]{1,0:T(1,128)} %shortlist.1, s32[128]{0:T(128)} %owner_map.1), custom_call_target="tpu_custom_call" | custom-call | tf_op jit(solution)/shard_map/pack/pallas_call | solution.py:43
  2.4 3.0 %collective-permute-start.2 = (bf16[136,1024]{1,0:T(8,128)(2,1)}, bf16[136,1024]{1,0:T(8,128)(2,1)S(1)}, u32[]{:S(2)}, u32[]{:S(2)}) collective-permute-start(bf16[136,1024]{1,0:T(8,128)(2,1)} %pack.1.refs_1_), channel_id=1, source_target_pairs={{0,4},{2,6},{4,0},{6,2},{1,5},{3,7},{5,1},{7,3},{8,12},{10,14},{12... | collective-permute-start | bytes 835592 | tf_op jit(solution)/shard_map/ppermute | solution.py:184
  5.3 1.5 %collective-permute-start.1 = (bf16[136,1024]{1,0:T(8,128)(2,1)}, bf16[136,1024]{1,0:T(8,128)(2,1)S(1)}, u32[]{:S(2)}, u32[]{:S(2)}) collective-permute-start(bf16[136,1024]{1,0:T(8,128)(2,1)} %pack.1.refs_1_), channel_id=1, source_target_pairs={{0,2},{2,0},{4,6},{6,4},{1,3},{3,1},{5,7},{7,5},{8,10},{10,8},{12,... | collective-permute-start | bytes 835592 | tf_op jit(solution)/shard_map/ppermute | solution.py:184
  6.8 1.6 %collective-permute-start = (bf16[136,1024]{1,0:T(8,128)(2,1)}, bf16[136,1024]{1,0:T(8,128)(2,1)S(1)}, u32[]{:S(2)}, u32[]{:S(2)}) collective-permute-start(bf16[136,1024]{1,0:T(8,128)(2,1)} %pack.1.refs_1_), channel_id=1, source_target_pairs={{0,8},{8,24},{24,16},{16,0},{1,9},{9,25},{25,17},{17,1},{2,10},{10... | collective-permute-start | bytes 835592 | tf_op jit(solution)/shard_map/ppermute | solution.py:228
  8.4 3.8 %collective-permute-done.2.refs_1_ = bf16[136,1024]{1,0:T(8,128)(2,1)S(1)} collective-permute-done((bf16[136,1024]{1,0:T(8,128)(2,1)}, bf16[136,1024]{1,0:T(8,128)(2,1)S(1)}, u32[]{:S(2)}, u32[]{:S(2)}) %collective-permute-start.2) | collective-permute-done | bytes 278560 | tf_op jit(solution)/shard_map/ppermute | solution.py:184
  12.2 1.5 %collective-permute-done.1.refs_0_ = bf16[136,1024]{1,0:T(8,128)(2,1)S(1)} collective-permute-done((bf16[136,1024]{1,0:T(8,128)(2,1)}, bf16[136,1024]{1,0:T(8,128)(2,1)S(1)}, u32[]{:S(2)}, u32[]{:S(2)}) %collective-permute-start.1) | collective-permute-done | bytes 278560 | tf_op jit(solution)/shard_map/ppermute | solution.py:184
  13.6 2.1 %collective-permute-done = bf16[136,1024]{1,0:T(8,128)(2,1)S(1)} collective-permute-done((bf16[136,1024]{1,0:T(8,128)(2,1)}, bf16[136,1024]{1,0:T(8,128)(2,1)S(1)}, u32[]{:S(2)}, u32[]{:S(2)}) %collective-permute-start) | collective-permute-done | bytes 278560 | tf_op jit(solution)/shard_map/ppermute | solution.py:228
  15.8 0.5 collective-permute-start.3
  16.3 1.7 %constant_dynamic-slice_fusion = (bf16[32,16,1024]{2,1,0:T(8,128)(2,1)S(1)}, bf16[32,16,1024]{2,1,0:T(8,128)(2,1)S(1)}) fusion(bf16[32,128,1024]{2,1,0:T(8,128)(2,1)} %refs_2_.3, s32[]{:T(128)S(6)} %select_n.9, s32[]{:T(128)S(6)} %select_n.8), kind=kLoop, calls=%fused_computation.8 | loop fusion | bytes 4194312 | tf_op jit(solution)/shard_map/dynamic_slice | solution.py:203
  18.0 1.6 %collective-permute-start.5 = (bf16[136,1024]{1,0:T(8,128)(2,1)S(1)}, bf16[136,1024]{1,0:T(8,128)(2,1)S(1)}, u32[]{:S(2)}, u32[]{:S(2)}) collective-permute-start(bf16[136,1024]{1,0:T(8,128)(2,1)S(1)} %copy-done.1), channel_id=1, source_target_pairs={{0,6},{2,4},{4,2},{6,0},{1,7},{3,5},{5,3},{7,1},{8,14},{10,12},{12... | collective-permute-start | bytes 835592 | tf_op jit(solution)/shard_map/ppermute | solution.py:184
  19.8 0.9 %collective-permute-start.4 = (bf16[136,1024]{1,0:T(8,128)(2,1)S(1)}, bf16[136,1024]{1,0:T(8,128)(2,1)S(1)}, u32[]{:S(2)}, u32[]{:S(2)}) collective-permute-start(bf16[136,1024]{1,0:T(8,128)(2,1)S(1)} %collective-permute-done), channel_id=1, source_target_pairs={{0,8},{8,24},{24,16},{16,0},{1,9},{9,25},{25,17},{17,1},{2,10},{10... | collective-permute-start | bytes 835592 | tf_op jit(solution)/shard_map/ppermute | solution.py:242
  21.0 3.4 %copy-done = bf16[32,128,1024]{2,1,0:T(8,128)(2,1)S(1)} copy-done((bf16[32,128,1024]{2,1,0:T(8,128)(2,1)S(1)}, bf16[32,128,1024]{2,1,0:T(8,128)(2,1)}, u32[]{:S(2)}) %copy-start) | copy-done | bytes 8388632
  24.4 5.0 %owner_side.2 = (bf16[128,1024]{1,0:T(8,128)(2,1)S(1)}, bf16[128,1024]{1,0:T(8,128)(2,1)S(1)}) custom-call(s32[1]{0:T(128)} %bitcast.base, bf16[136,1024]{1,0:T(8,128)(2,1)S(1)} %collective-permute-done.1.refs_0_, bf16[136,1024]{1,0:T(8,128)(2,1)S(1)} %collective-permute-done.2.refs_1_, bf16[32,128,1024]{2,1,0:T(8,128)(2,1)S(1)} %copy-done, ...), custom_call_target="tpu_custom_call" | custom-call | flops 1 | bytes 1 | tf_op jit(solution)/shard_map/owner_side/pallas_call | solution.py:110
  29.4 1.0 %constant_dynamic-update-slice_fusion.refs_1_ = bf16[272,1024]{1,0:T(8,128)(2,1)S(1)} fusion(bf16[272,1024]{1,0:T(8,128)(2,1)S(1)} %constant_dynamic-update-slice_fusion.1, bf16[136,1024]{1,0:T(8,128)(2,1)} %collective-permute-done.3), kind=kLoop, calls=%fused_computation.4 | loop fusion | bytes 557056 | tf_op jit(solution)/shard_map/concatenate | solution.py:237
  30.5 2.3 %collective-permute-start.10 = (bf16[544,1024]{1,0:T(8,128)(2,1)S(1)}, bf16[544,1024]{1,0:T(8,128)(2,1)S(1)}, u32[]{:S(2)}, u32[]{:S(2)}) collective-permute-start(bf16[544,1024]{1,0:T(8,128)(2,1)S(1)} %pad_maximum_fusion.refs_0_), channel_id=1, source_target_pairs={{8,0},{24,8},{16,24},{0,16},{9,1},{25,9},{17,25},{1,17},{10,2},{26... | collective-permute-start | bytes 3342344 | tf_op jit(solution)/shard_map/ppermute | solution.py:246
  32.8 1.5 %collective-permute-start.8 = (bf16[136,1024]{1,0:T(8,128)(2,1)S(1)}, bf16[136,1024]{1,0:T(8,128)(2,1)S(1)}, u32[]{:S(2)}, u32[]{:S(2)}) collective-permute-start(bf16[136,1024]{1,0:T(8,128)(2,1)S(1)} %collective-permute-done.4), channel_id=1, source_target_pairs={{0,2},{2,0},{4,6},{6,4},{1,3},{3,1},{5,7},{7,5},{8,10},{10,8},{12,... | collective-permute-start | bytes 835592 | tf_op jit(solution)/shard_map/ppermute | solution.py:184
  34.3 0.5 collective-permute-start.6
  34.8 0.5 collective-permute-start.7
  35.3 1.5 %collective-permute-start.11 = (bf16[272,1024]{1,0:T(8,128)(2,1)S(1)}, bf16[272,1024]{1,0:T(8,128)(2,1)S(1)}, u32[]{:S(2)}, u32[]{:S(2)}) collective-permute-start(bf16[272,1024]{1,0:T(8,128)(2,1)S(1)} %constant_dynamic-update-slice_fusion.refs_1_), channel_id=1, source_target_pairs={{0,2},{2,0},{4,6},{6,4},{1,3},{3,1},{5,7},{7,5},{8,10},{10,8},{12,... | collective-permute-start | bytes 1671176 | tf_op jit(solution)/shard_map/ppermute | solution.py:184
  36.8 5.0 %owner_side.3 = (bf16[128,1024]{1,0:T(8,128)(2,1)S(1)}, f32[128,1024]{1,0:T(8,128)S(1)}) custom-call(s32[1]{0:T(128)} %bitcast.base, bf16[136,1024]{1,0:T(8,128)(2,1)S(1)} %collective-permute-done.5.refs_0_, bf16[136,1024]{1,0:T(8,128)(2,1)S(1)} %copy-done.1, bf16[32,128,1024]{2,1,0:T(8,128)(2,1)S(1)} %copy-done, f32[32,128]{1,0:T(8,128)S(1)} %copy-done.2), custom_call_target="tpu_custom_call" | custom-call | flops 1 | bytes 1 | tf_op jit(solution)/shard_map/owner_side/pallas_call | solution.py:110
  41.8 0.6 collective-permute-done.8
  42.4 5.6 %collective-permute-done.6 = bf16[128,1024]{1,0:T(8,128)(2,1)S(1)} collective-permute-done((bf16[128,1024]{1,0:T(8,128)(2,1)S(1)}, bf16[128,1024]{1,0:T(8,128)(2,1)S(1)}, u32[]{:S(2)}, u32[]{:S(2)}) %collective-permute-start.6) | collective-permute-done | bytes 262176 | tf_op jit(solution)/shard_map/ppermute | solution.py:184
  48.0 0.5 collective-permute-start.12
  48.4 2.5 %collective-permute-start.9 = (bf16[128,1024]{1,0:T(8,128)(2,1)S(1)}, bf16[128,1024]{1,0:T(8,128)(2,1)S(1)}, u32[]{:S(2)}, u32[]{:S(2)}) collective-permute-start(bf16[128,1024]{1,0:T(8,128)(2,1)S(1)} %get-tuple-element.36), channel_id=1, source_target_pairs={{0,6},{2,4},{4,2},{6,0},{1,7},{3,5},{5,3},{7,1},{8,14},{10,12},{12... | collective-permute-start | bytes 786440 | tf_op jit(solution)/shard_map/ppermute | solution.py:184
  51.1 4.4 %label_side.4 = (f32[512,1024]{1,0:T(8,128)S(1)}, f32[512,1024]{1,0:T(8,128)S(1)}) custom-call(s32[3]{0:T(128)S(1)} %pad_add_fusion.1.where, bf16[544,1024]{1,0:T(8,128)(2,1)S(1)} %pad_maximum_fusion.refs_0_, bf16[272,1024]{1,0:T(8,128)(2,1)S(1)} %constant_dynamic-update-slice_fusion.refs_1_, bf16[512,1024]{1,0:T(8,128)(2,1)S(1)} %bitcast.10, ...), custom_call_target="tpu_custom_call" | custom-call | flops 1 | bytes 1 | tf_op jit(solution)/shard_map/label_side/pallas_call | solution.py:171
  55.5 6.5 %collective-permute-done.9 = bf16[128,1024]{1,0:T(8,128)(2,1)S(1)} collective-permute-done((bf16[128,1024]{1,0:T(8,128)(2,1)S(1)}, bf16[128,1024]{1,0:T(8,128)(2,1)S(1)}, u32[]{:S(2)}, u32[]{:S(2)}) %collective-permute-start.9) | collective-permute-done | bytes 262176 | tf_op jit(solution)/shard_map/ppermute | solution.py:184
  62.0 4.5 %label_side.5 = (f32[512,1024]{1,0:T(8,128)S(1)}, f32[512,1024]{1,0:T(8,128)S(1)}) custom-call(s32[3]{0:T(128)S(1)} %pad_add_fusion.1.where, bf16[544,1024]{1,0:T(8,128)(2,1)S(1)} %collective-permute-done.10.refs_0_, bf16[272,1024]{1,0:T(8,128)(2,1)S(1)} %collective-permute-done.11.refs_1_, bf16[512,1024]{1,0:T(8,128)(2,1)S(1)} %bitcast.11, ...), custom_call_target="tpu_custom_call" | custom-call | flops 1 | bytes 1 | tf_op jit(solution)/shard_map/label_side/pallas_call | solution.py:171
  66.5 2.4 %label_side.7 = f32[512,1024]{1,0:T(8,128)S(1)} custom-call(s32[2]{0:T(128)S(1)} %get-tuple-element.47.where, bf16[272,1024]{1,0:T(8,128)(2,1)S(1)} %constant_dynamic-update-slice_fusion.2.refs_0_, bf16[272,1024]{1,0:T(8,128)(2,1)S(1)} %collective-permute-done.12.refs_1_, bf16[512,1024]{1,0:T(8,128)(2,1)S(1)} %bitcast.12, ...), custom_call_target="tpu_custom_call" | custom-call | flops 1 | bytes 1 | tf_op jit(solution)/shard_map/label_side/pallas_call | solution.py:171
  69.0 0.9 %convert_add_fusion = f32[128,1024]{1,0:T(8,128)} fusion(bf16[128,1024]{1,0:T(8,128)(2,1)S(1)} %collective-permute-done.9, bf16[128,1024]{1,0:T(8,128)(2,1)S(1)} %collective-permute-done.7, f32[128,1024]{1,0:T(8,128)S(1)} %get-tuple-element.30, bf16[128,1024]{1,0:T(8,128)(2,1)S(1)} %collective-permute-done.6), kind=kLoop, calls=%fused_computation.1 | loop fusion | flops 786432 | bytes 1835008 | tf_op jit(solution)/shard_map/add | solution.py:271
  70.0 2.1 %label_side.6 = f32[512,1024]{1,0:T(8,128)S(1)} custom-call(s32[2]{0:T(128)S(1)} %get-tuple-element.44.where, bf16[272,1024]{1,0:T(8,128)(2,1)S(1)} %constant_dynamic-update-slice_fusion.2.refs_0_, bf16[272,1024]{1,0:T(8,128)(2,1)S(1)} %collective-permute-done.12.refs_1_, bf16[512,1024]{1,0:T(8,128)(2,1)S(1)} %bitcast.9, ...), custom_call_target="tpu_custom_call" | custom-call | flops 1 | bytes 1 | tf_op jit(solution)/shard_map/label_side/pallas_call | solution.py:171
  72.1 1.1 %collective-permute-done.13 = f32[512,1024]{1,0:T(8,128)S(1)} collective-permute-done((f32[512,1024]{1,0:T(8,128)S(1)}, f32[512,1024]{1,0:T(8,128)S(1)}, u32[]{:S(2)}, u32[]{:S(2)}) %collective-permute-start.13) | collective-permute-done | bytes 2097184 | tf_op jit(solution)/shard_map/ppermute | solution.py:184
  73.2 1.9 %add.33 = f32[512,1024]{1,0:T(8,128)} add(f32[512,1024]{1,0:T(8,128)S(1)} %label_side.6, f32[512,1024]{1,0:T(8,128)S(1)} %collective-permute-done.13) | non-fusion elementwise | flops 524288 | bytes 6291456 | tf_op jit(solution)/shard_map/add | solution.py:268
  (24 shorter events, 0.9 us)
Async XLA Ops:
  2.4 9.8 %collective-permute-start.2 = (bf16[136,1024]{1,0:T(8,128)(2,1)}, bf16[136,1024]{1,0:T(8,128)(2,1)S(1)}, u32[]{:S(2)}, u32[]{:S(2)}) collective-permute-start(bf16[136,1024]{1,0:T(8,128)(2,1)} %pack.1.refs_1_), channel_id=1, source_target_pairs={{0,4},{2,6},{4,0},{6,2},{1,5},{3,7},{5,1},{7,3},{8,12},{10,14},{12... | collective-permute-start | bytes 835592 | tf_op jit(solution)/shard_map/ppermute | solution.py:184
  5.3 8.3 %collective-permute-start.1 = (bf16[136,1024]{1,0:T(8,128)(2,1)}, bf16[136,1024]{1,0:T(8,128)(2,1)S(1)}, u32[]{:S(2)}, u32[]{:S(2)}) collective-permute-start(bf16[136,1024]{1,0:T(8,128)(2,1)} %pack.1.refs_1_), channel_id=1, source_target_pairs={{0,2},{2,0},{4,6},{6,4},{1,3},{3,1},{5,7},{7,5},{8,10},{10,8},{12,... | collective-permute-start | bytes 835592 | tf_op jit(solution)/shard_map/ppermute | solution.py:184
  6.8 9.0 %collective-permute-start = (bf16[136,1024]{1,0:T(8,128)(2,1)}, bf16[136,1024]{1,0:T(8,128)(2,1)S(1)}, u32[]{:S(2)}, u32[]{:S(2)}) collective-permute-start(bf16[136,1024]{1,0:T(8,128)(2,1)} %pack.1.refs_1_), channel_id=1, source_target_pairs={{0,8},{8,24},{24,16},{16,0},{1,9},{9,25},{25,17},{17,1},{2,10},{10... | collective-permute-start | bytes 835592 | tf_op jit(solution)/shard_map/ppermute | solution.py:228
  8.4 9.6 %copy-start.1 = (bf16[136,1024]{1,0:T(8,128)(2,1)S(1)}, bf16[136,1024]{1,0:T(8,128)(2,1)}, u32[]{:S(2)}) copy-start(bf16[136,1024]{1,0:T(8,128)(2,1)} %pack.1.refs_1_) | copy-start | bytes 835588
  8.4 11.2 %copy-start.2 = (f32[32,128]{1,0:T(8,128)S(1)}, f32[32,128]{1,0:T(8,128)}, u32[]{:S(2)}) copy-start(f32[32,128]{1,0:T(8,128)} %refs_3_.3) | copy-start | bytes 49156
  15.8 13.6 %collective-permute-start.3 = (bf16[136,1024]{1,0:T(8,128)(2,1)S(1)}, bf16[136,1024]{1,0:T(8,128)(2,1)}, u32[]{:S(2)}, u32[]{:S(2)}) collective-permute-start(bf16[136,1024]{1,0:T(8,128)(2,1)S(1)} %collective-permute-done), channel_id=1, source_target_pairs={{0,4},{2,6},{4,0},{6,2},{1,5},{3,7},{5,1},{7,3},{8,12},{10,14},{12... | collective-permute-start | bytes 835592 | tf_op jit(solution)/shard_map/ppermute | solution.py:184
  18.0 12.3 %collective-permute-start.5 = (bf16[136,1024]{1,0:T(8,128)(2,1)S(1)}, bf16[136,1024]{1,0:T(8,128)(2,1)S(1)}, u32[]{:S(2)}, u32[]{:S(2)}) collective-permute-start(bf16[136,1024]{1,0:T(8,128)(2,1)S(1)} %copy-done.1), channel_id=1, source_target_pairs={{0,6},{2,4},{4,2},{6,0},{1,7},{3,5},{5,3},{7,1},{8,14},{10,12},{12... | collective-permute-start | bytes 835592 | tf_op jit(solution)/shard_map/ppermute | solution.py:184
  19.8 10.6 %collective-permute-start.4 = (bf16[136,1024]{1,0:T(8,128)(2,1)S(1)}, bf16[136,1024]{1,0:T(8,128)(2,1)S(1)}, u32[]{:S(2)}, u32[]{:S(2)}) collective-permute-start(bf16[136,1024]{1,0:T(8,128)(2,1)S(1)} %collective-permute-done), channel_id=1, source_target_pairs={{0,8},{8,24},{24,16},{16,0},{1,9},{9,25},{25,17},{17,1},{2,10},{10... | collective-permute-start | bytes 835592 | tf_op jit(solution)/shard_map/ppermute | solution.py:242
  21.0 3.4 %copy-start = (bf16[32,128,1024]{2,1,0:T(8,128)(2,1)S(1)}, bf16[32,128,1024]{2,1,0:T(8,128)(2,1)}, u32[]{:S(2)}) copy-start(bf16[32,128,1024]{2,1,0:T(8,128)(2,1)} %refs_2_.3) | copy-start | bytes 25165828
  30.5 31.6 %collective-permute-start.10 = (bf16[544,1024]{1,0:T(8,128)(2,1)S(1)}, bf16[544,1024]{1,0:T(8,128)(2,1)S(1)}, u32[]{:S(2)}, u32[]{:S(2)}) collective-permute-start(bf16[544,1024]{1,0:T(8,128)(2,1)S(1)} %pad_maximum_fusion.refs_0_), channel_id=1, source_target_pairs={{8,0},{24,8},{16,24},{0,16},{9,1},{25,9},{17,25},{1,17},{10,2},{26... | collective-permute-start | bytes 3342344 | tf_op jit(solution)/shard_map/ppermute | solution.py:246
  32.8 9.6 %collective-permute-start.8 = (bf16[136,1024]{1,0:T(8,128)(2,1)S(1)}, bf16[136,1024]{1,0:T(8,128)(2,1)S(1)}, u32[]{:S(2)}, u32[]{:S(2)}) collective-permute-start(bf16[136,1024]{1,0:T(8,128)(2,1)S(1)} %collective-permute-done.4), channel_id=1, source_target_pairs={{0,2},{2,0},{4,6},{6,4},{1,3},{3,1},{5,7},{7,5},{8,10},{10,8},{12,... | collective-permute-start | bytes 835592 | tf_op jit(solution)/shard_map/ppermute | solution.py:184
  34.3 13.7 %collective-permute-start.6 = (bf16[128,1024]{1,0:T(8,128)(2,1)S(1)}, bf16[128,1024]{1,0:T(8,128)(2,1)S(1)}, u32[]{:S(2)}, u32[]{:S(2)}) collective-permute-start(bf16[128,1024]{1,0:T(8,128)(2,1)S(1)} %get-tuple-element.31), channel_id=1, source_target_pairs={{0,2},{2,0},{4,6},{6,4},{1,3},{3,1},{5,7},{7,5},{8,10},{10,8},{12,... | collective-permute-start | bytes 786440 | tf_op jit(solution)/shard_map/ppermute | solution.py:184
  34.8 13.2 %collective-permute-start.7 = (bf16[128,1024]{1,0:T(8,128)(2,1)S(1)}, bf16[128,1024]{1,0:T(8,128)(2,1)S(1)}, u32[]{:S(2)}, u32[]{:S(2)}) collective-permute-start(bf16[128,1024]{1,0:T(8,128)(2,1)S(1)} %get-tuple-element.33), channel_id=1, source_target_pairs={{0,4},{2,6},{4,0},{6,2},{1,5},{3,7},{5,1},{7,3},{8,12},{10,14},{12... | collective-permute-start | bytes 786440 | tf_op jit(solution)/shard_map/ppermute | solution.py:184
  35.3 26.8 %collective-permute-start.11 = (bf16[272,1024]{1,0:T(8,128)(2,1)S(1)}, bf16[272,1024]{1,0:T(8,128)(2,1)S(1)}, u32[]{:S(2)}, u32[]{:S(2)}) collective-permute-start(bf16[272,1024]{1,0:T(8,128)(2,1)S(1)} %constant_dynamic-update-slice_fusion.refs_1_), channel_id=1, source_target_pairs={{0,2},{2,0},{4,6},{6,4},{1,3},{3,1},{5,7},{7,5},{8,10},{10,8},{12,... | collective-permute-start | bytes 1671176 | tf_op jit(solution)/shard_map/ppermute | solution.py:184
  48.0 18.5 %collective-permute-start.12 = (bf16[272,1024]{1,0:T(8,128)(2,1)S(1)}, bf16[272,1024]{1,0:T(8,128)(2,1)S(1)}, u32[]{:S(2)}, u32[]{:S(2)}) collective-permute-start(bf16[272,1024]{1,0:T(8,128)(2,1)S(1)} %constant_dynamic-update-slice_fusion.2.refs_0_), channel_id=1, source_target_pairs={{0,4},{2,6},{4,0},{6,2},{1,5},{3,7},{5,1},{7,3},{8,12},{10,14},{12... | collective-permute-start | bytes 1671176 | tf_op jit(solution)/shard_map/ppermute | solution.py:184
  48.4 13.6 %collective-permute-start.9 = (bf16[128,1024]{1,0:T(8,128)(2,1)S(1)}, bf16[128,1024]{1,0:T(8,128)(2,1)S(1)}, u32[]{:S(2)}, u32[]{:S(2)}) collective-permute-start(bf16[128,1024]{1,0:T(8,128)(2,1)S(1)} %get-tuple-element.36), channel_id=1, source_target_pairs={{0,6},{2,4},{4,2},{6,0},{1,7},{3,5},{5,3},{7,1},{8,14},{10,12},{12... | collective-permute-start | bytes 786440 | tf_op jit(solution)/shard_map/ppermute | solution.py:184
  68.9 4.2 %collective-permute-start.13 = (f32[512,1024]{1,0:T(8,128)S(1)}, f32[512,1024]{1,0:T(8,128)S(1)}, u32[]{:S(2)}, u32[]{:S(2)}) collective-permute-start(f32[512,1024]{1,0:T(8,128)S(1)} %label_side.7), channel_id=1, source_target_pairs={{0,1},{1,0},{2,3},{3,2},{4,5},{5,4},{6,7},{7,6},{8,9},{9,8},{10,11... | collective-permute-start | bytes 6291464 | tf_op jit(solution)/shard_map/ppermute | solution.py:184

commit v3 on v2

--- a/solution.py
+++ b/solution.py
@@ -49,6 +49,35 @@
 def info(ref, at, rows, extra):
     block = ref[at + rows:at + rows + extra, 0:2 * rows + LANES].astype(f32).astype(i32)
     return block[:, 0:rows], block[:, rows:2 * rows], block[0:1, 2 * rows:]
+
+
+def prepare_body(sides, each, where, w, prop, *outs):
+    blocks, width, feats = w.shape
+    inv = scale / prop[...]
+    wide = (blocks, each, width)
+    lane, row = lax.broadcasted_iota(i32, wide, 2), lax.broadcasted_iota(i32, wide, 1)
+    for side in range(sides):
+        off = pl.multiple_of(where[1 + side], each)
+        outs[side][...] = w[:, pl.ds(off, each), :].reshape(blocks * each, feats)
+        picked = jnp.where(lane == row + off, jnp.broadcast_to(inv[:, None, :], wide), 0.0)
+        picked = jnp.sum(picked, axis=2, keepdims=True)
+        outs[sides + side][...] = jnp.broadcast_to(picked, (blocks, each, LANES)).reshape(blocks * each, LANES)
+
+
+def prepare(w, prop, where, each):
+    blocks, width, feats = w.shape
+    sides = where.shape[0] - 1
+    vm = pl.BlockSpec(memory_space=pltpu.VMEM)
+    outs = pl.pallas_call(
+        functools.partial(prepare_body, sides, each),
+        out_shape=[jax.ShapeDtypeStruct((blocks * each, feats), bf16)] * sides
+        + [jax.ShapeDtypeStruct((blocks * each, LANES), f32)] * sides,
+        in_specs=[pl.BlockSpec(memory_space=pltpu.SMEM), vm, vm], out_specs=[vm] * (2 * sides),
+        compiler_params=pltpu.CompilerParams(vmem_limit_bytes=(8 << 20) + 16 * sides * blocks * each * feats),
+        cost_estimate=pl.CostEstimate(flops=1, bytes_accessed=32 * blocks * width * feats, transcendentals=0),
+        name="prepare",
+    )(where, w, prop)
+    return outs[:sides], outs[sides:]
 
 
 def a_body(n, group, base, *refs):
@@ -115,17 +144,15 @@
                 pltpu.VMEM((n * rows, feats), bf16), pltpu.VMEM((n * rows, feats), f32),
                 pltpu.VMEM((n * rows, LANES), i32), pltpu.VMEM((n, 8, LANES), f32),
                 pltpu.VMEM((n * rows, group * width), bf16)],
-        compiler_params=pltpu.CompilerParams(vmem_limit_bytes=40 << 20),
+        compiler_params=pltpu.CompilerParams(vmem_limit_bytes=(12 << 20) + 16 * n * rows * feats),
         cost_estimate=pl.CostEstimate(flops=1, bytes_accessed=1, transcendentals=0),
         name="owner_side",
     )(base, *xs, w, prop)
 
 
-def b_body(n, sides, pair, has_acc, blocks, rows, extra, where, *refs):
+def b_body(n, sides, pair, adds, blocks, rows, extra, where, *refs):
     xs, ws, invs, rest = refs[:n], refs[n:n + sides], refs[n + sides:n + 2 * sides], refs[n + 2 * sides:]
-    before = None
-    if has_acc:
-        before, rest = rest[:sides], rest[sides:]
+    before, rest = rest[:adds * sides], rest[adds * sides:]
     outs, (x_all, grads) = rest[:sides], rest[sides:]
     labels = ws[0].shape[0]
     each = labels // blocks
@@ -140,8 +167,9 @@
     for side in range(sides):
         off = where[1 + side]
         for k0 in range(0, count, pair):
-            scores = lax.dot_general(ws[side][...], x_all[k0 * rows:(k0 + pair) * rows, :], NT, preferred_element_type=f32)
-            for k in range(k0, k0 + pair):
+            stop = min(k0 + pair, count)
+            scores = lax.dot_general(ws[side][...], x_all[k0 * rows:stop * rows, :], NT, preferred_element_type=f32)
+            for k in range(k0, stop):
                 stored, label, present = info(*shards[k], rows, extra)
                 local = label - off
                 bit = jnp.where((local >= 0) & (local < each), jnp.left_shift(jnp.ones_like(label), local & (WORD - 1)), 0)
@@ -157,23 +185,25 @@
                 g = half * jnp.tanh(0.5 * s) + (half - jnp.where(got, invs[side][...], 0.0))
                 grads[:, k * rows:(k + 1) * rows] = g.astype(bf16)
         total = lax.dot_general(grads[...], x_all[...], NN, preferred_element_type=f32)
-        outs[side][...] = before[side][...] + total if has_acc else total
-
-
-def b_call(xs, ws, invs, where, blocks, rows, extra, before=None, pair=2):
+        for old in before[side * adds:(side + 1) * adds]:
+            total = total + old[...]
+        outs[side][...] = total.astype(outs[side].dtype)
+
+
+def b_call(xs, ws, invs, where, blocks, rows, extra, before, kind, pair=2):
     n, sides = len(xs), len(ws)
     count = sum(x.shape[0] for x in xs) // (rows + extra)
     pair = min(pair, count)
     labels, feats = ws[0].shape
     vm = pl.BlockSpec(memory_space=pltpu.VMEM)
     sm = pl.BlockSpec(memory_space=pltpu.SMEM)
-    more = [] if before is None else list(before)
+    more = [x for side in before for x in side]
     return pl.pallas_call(
-        functools.partial(b_body, n, sides, pair, before is not None, blocks, rows, extra),
-        out_shape=[jax.ShapeDtypeStruct((labels, feats), f32)] * sides,
+        functools.partial(b_body, n, sides, pair, len(more) // sides, blocks, rows, extra),
+        out_shape=[jax.ShapeDtypeStruct((labels, feats), kind)] * sides,
         in_specs=[sm] + [vm] * (n + 2 * sides + len(more)), out_specs=[vm] * sides,
         scratch_shapes=[pltpu.VMEM((count * rows, feats), bf16), pltpu.VMEM((labels, count * rows), bf16)],
-        compiler_params=pltpu.CompilerParams(vmem_limit_bytes=40 << 20),
+        compiler_params=pltpu.CompilerParams(vmem_limit_bytes=(16 << 20) + 8 * (count * rows + sides * labels) * feats),
         cost_estimate=pl.CostEstimate(flops=1, bytes_accessed=1, transcendentals=0),
         name="label_side",
     )(where, *xs, *ws, *invs, *more)
@@ -200,76 +230,79 @@
     base = own * blocks
 
     offs = [(plane * sections + side) * each for side in ([section ^ 1, section] if sections == 2 else [section])]
-    ws = [lax.dynamic_slice_in_dim(label_weights, off, each, 1).reshape(blocks * each, feats) for off in offs]
-    invs = [scale / lax.dynamic_slice_in_dim(propensity, off, each, 1).reshape(blocks * each, 1) for off in offs]
-    invs = [jnp.broadcast_to(inv, (blocks * each, rows)) for inv in invs]
+    if each % 16 == 0:
+        ws, invs = prepare(label_weights, propensity, jnp.stack([base] + offs).astype(i32), each)
+    else:
+        cut_label = lambda x, off: lax.dynamic_slice_in_dim(x, off, each, 1).reshape(blocks * each, -1)
+        ws = [cut_label(label_weights, off) for off in offs]
+        invs = [jnp.broadcast_to(scale / cut_label(propensity, off), (blocks * each, rows)) for off in offs]
     one = base.astype(i32).reshape(1)
     cut = label_count // 2 + 1
     first, second = list(range(1, cut)), list(range(cut, label_count)) + [0]
     ring = list(range(0, dp_count, 2))[:1] + list(range(1, dp_count, 2)) + list(range(0, dp_count, 2))[:0:-1]
     forward = [(a, ring[(i + 1) % dp_count]) for i, a in enumerate(ring)]
-    backward = [(b, a) for a, b in forward]
 
     def owner_call(ks, one):
         out = a_call([here[k] for k in ks], label_weights, propensity, one, rows,
                      [f32 if k == 0 else bf16 for k in ks])
         return dict(zip(ks, out))
 
-    def label_call(xs, before, *done, only=None):
-        pick = range(len(offs)) if only is None else [only]
+    def label_call(xs, before, *done, kind=f32):
+        pick = list(range(len(offs)))
+        if len(before) < len(pick):
+            pick = pick[:1] if kind == bf16 else pick[1:]
         where = after(jnp.stack([base] + [offs[k] for k in pick]).astype(i32), *done)
-        out = b_call(xs, [ws[k] for k in pick], [invs[k] for k in pick], where, blocks, rows, extra,
-                     None if before is None else [before[k] for k in pick])
-        return out
-
+        out = b_call(xs, [ws[k] for k in pick], [invs[k] for k in pick], where, blocks, rows, extra, before, kind)
+        return [[x] for x in out]
+
+    column = lax.ppermute(packed, "dp", forward)
     here = {0: packed}
     for k in first:
         here[k] = swap(packed, "label", k)
-    column = lax.ppermute(packed, "dp", forward)
-    gate = [here[k] for k in first] + [column]
+    gate = [here[k] for k in first] + [column] + list(ws) + list(invs)
     for k in second[:-1]:
         here[k] = swap(after(packed, *gate), "label", k)
     columns = [column]
-    orders = [bits if k % 2 else bits[::-1] for k in range(dp_count - 2)]
-
-    def spread(x, order, *done):
-        for bit in order:
-            x = jnp.concatenate([x, swap(after(x, *done), "label", bit)], axis=0)
-        return x
-
-    halves = [spread(column, orders[0][:-1], *gate)]
     for _ in range(dp_count - 3):
         columns.append(lax.ppermute(after(columns[-1], *gate), "dp", forward))
-    parts = owner_call(first, after(one, *gate, *ws, *invs))
-    gate = [halves[0], parts[1]] + columns[1:] + [here[k] for k in second[:-1]]
+    last_plane = [(b, a) for a, b in forward]
+    if dp_count == 4:
+        last_plane = [(a, a ^ 1) for a in range(dp_count)]
+        columns[0] = lax.ppermute(after(column, *gate), "dp", [(0, 0), (1, 2), (2, 1), (3, 3)])
+    parts = owner_call(first, after(one, *gate))
+    gate = [parts[1]] + columns + [here[k] for k in second[:-1]]
     own_plane = after(jnp.concatenate([here[k] for k in range(label_count)], axis=0), *gate)
-    next_plane = lax.ppermute(own_plane, "dp", backward)
+    columns = after(jnp.concatenate(columns, axis=0), *gate)
+    spread = [swap(columns, "label", bit) for bit in bits[:2]]
+    next_plane = lax.ppermute(own_plane, "dp", last_plane)
     back = {k: swap(after(parts[k], *gate), "label", k) for k in first}
-    for k in range(1, len(columns)):
-        halves.append(spread(columns[k], orders[k][:-1], *gate))
-    tops = [swap(after(halves[0], *gate), "label", orders[0][-1])]
     parts.update(owner_call(second, after(one, *gate)))
-    gate = [parts[0]] + halves[1:] + [back[k] for k in first]
+    total = label_call([own_plane], [[]] * len(offs), parts[0])
+    gate = total[0] + spread + [back[k] for k in first]
+    cut = columns.shape[0] // (rows + extra) // 2 * (rows + extra)
+    corners = [
+        swap(after(spread[1][:cut], *gate), "label", bits[0]),
+        swap(after(spread[0][cut:], *gate), "label", bits[1]),
+    ]
     for k in second[:-1]:
         back[k] = swap(after(parts[k], *gate), "label", k)
-    for k in range(1, len(columns)):
-        tops.append(swap(after(halves[k], *gate), "label", orders[k][-1]))
-    total = label_call([own_plane, halves[0]], None, *gate)
-    gate = [total[0], next_plane, tops[0]] + [back[k] for k in second[:-1]]
-    total = label_call([next_plane, tops[0]], total, *gate)
-    for k in range(1, len(columns)):
-        xs = [halves[k], tops[k]]
-        if k < len(columns) - 1 or len(offs) == 1:
-            total = label_call(xs, total, total[0])
-        else:
-            theirs = label_call(xs, total, total[0], only=0)[0]
-            theirs = swap(theirs, "section", 1)
-            mine = label_call(xs, total, total[0], only=1)[0]
-            total = [mine + theirs]
+    total = label_call([columns] + spread, total, *gate)
+    total = label_call([next_plane], total)
+    rest = []
+    for bit in bits[2:]:
+        rest += [swap(x, "label", bit) for x in [columns] + spread + corners + rest]
+    for x in rest:
+        total = label_call([x], total)
+    if sections == 2:
+        theirs = label_call(corners, total[:1], *back.values(), kind=bf16)[0][0]
+        mine = label_call(corners, total[1:], theirs)[0][0]
+        total = [[mine + swap(theirs, "section", 1).astype(f32)]]
+    else:
+        total = label_call(corners, total, *back.values())
     query_grad = parts[0]
     for k in range(1, label_count):
         query_grad = query_grad + back[k].astype(f32)
-    return query_grad, total[0].reshape(blocks, each, feats)
+    return query_grad, total[-1][0].reshape(blocks, each, feats)
 
 
 def solution(mesh):

time: 75.3 us -> 71.1 us (0.944)
  waiting for transfers between devices: 21.2 us -> 11.2 us
  starting transfers between devices: 18.3 us -> 23.6 us
  Pallas kernels: 25.1 us -> 28 us
  local copies, waits for them, and re-layouts: 6.56 us -> 4.14 us
    ppermute x11, waiting for transfers between devices: 19 us -> 10.4 us  [swap(): return lax.ppermute(x, axis, [(i, i ^ bit) for i in range(size)])]
    ppermute x1 -> x2, starting transfers between devices: 2.29 us -> 5.8 us  [the longest x1 5.13 us: per_device(): next_plane = lax.ppermute(own_plane, 'dp', last_plane)]
    pallas_call x4 -> x6, Pallas kernels: 13.4 us -> 16.3 us  [the longest x5 15.5 us: b_call(): pl.pallas_call(functools.partial(b_body, n, sides, pair, len(more) // sid...]
    ppermute x1, waiting for transfers between devices: 2.13 us -> 0.01 us  [per_device(): column = lax.ppermute(packed, 'dp', forward)]
    dynamic_slice x1 -> x0, local copies, waits for them, and re-layouts: 1.73 us -> none  [per_device(): lax.dynamic_slice_in_dim(label_weights, off, each, 1)]
    ppermute x1, starting transfers between devices: 0.88 us -> 2.59 us  [per_device(): columns.append(lax.ppermute(after(columns[-1], *gate), 'dp', forward))]
    ppermute x1, starting transfers between devices: 1.58 us -> 3.02 us  [per_device(): column = lax.ppermute(packed, 'dp', forward)]
    ppermute x11, starting transfers between devices: 13.6 us -> 12.2 us  [swap(): return lax.ppermute(x, axis, [(i, i ^ bit) for i in range(size)])]
  transfers between devices with their start and end apart: 14 -> 15, of which waited for: 7 -> 7; matrix products, arithmetic and copies ran while one was open for 6% -> 2% of each run, Pallas kernels for 28% -> 34%
where the time goes in v3:
time: 71.1 us; the launch traced here: 70.8 us
  Pallas kernels  28 us (39%)
  starting transfers between devices  23.6 us (33%)
  waiting for transfers between devices  11.2 us (16%)
  local copies, waits for them, and re-layouts  4.14 us (6%)
  other arithmetic  3.07 us (4%)
  between operations  0.79 us (1%)
    pallas_call x5, Pallas kernels, b_call(): pl.pallas_call(functools.partial(b_body, n, sides, pair, len(more) // sid...  15.5 us
    ppermute x11, starting transfers between devices, swap(): return lax.ppermute(x, axis, [(i, i ^ bit) for i in range(size)])  12.2 us
    ppermute x11, waiting for transfers between devices, swap(): return lax.ppermute(x, axis, [(i, i ^ bit) for i in range(size)])  10.4 us
    pallas_call x2, Pallas kernels, a_call(): pl.pallas_call(functools.partial(a_body, n, group), out_shape=out_types,...  9.96 us
    ppermute x1, starting transfers between devices, per_device(): next_plane = lax.ppermute(own_plane, 'dp', last_plane)  5.13 us
    unnamed x8, local copies, waits for them, and re-layouts  4.11 us
    ppermute x1, starting transfers between devices, per_device(): column = lax.ppermute(packed, 'dp', forward)  3.02 us
    ppermute x1, starting transfers between devices, per_device(): columns.append(lax.ppermute(after(columns[-1], *gate), 'dp', forward))  2.59 us
  transfers between devices with their start and end apart: 15, of which 7 were waited for; matrix products, arithmetic and copies ran while one was open for 2% of the time, Pallas kernels for 34%

profile of v3, /device:TPU:0, one launch (start us, length us, event | category | flops | bytes accessed | tf_op | source)
XLA Modules:
  0.0 70.8 jit_solution(4631157809102240958)
XLA Ops:
  0.6 1.7 %pack.1.refs_1_ = bf16[136,1024]{1,0:T(8,128)(2,1)} custom-call(bf16[128,1024]{1,0:T(8,128)(2,1)} %queries.1, s32[8,128]{1,0:T(8,128)} %bitcast.6, s32[1,48]{1,0:T(1,128)} %shortlist.1, s32[128]{0:T(128)} %owner_map.1), custom_call_target="tpu_custom_call" | custom-call | tf_op jit(solution)/shard_map/pack/pallas_call | solution.py:43
  2.4 3.0 %collective-permute-start.2 = (bf16[136,1024]{1,0:T(8,128)(2,1)}, bf16[136,1024]{1,0:T(8,128)(2,1)S(1)}, u32[]{:S(2)}, u32[]{:S(2)}) collective-permute-start(bf16[136,1024]{1,0:T(8,128)(2,1)} %pack.1.refs_1_), channel_id=1, source_target_pairs={{0,8},{8,24},{24,16},{16,0},{1,9},{9,25},{25,17},{17,1},{2,10},{10... | collective-permute-start | bytes 835592 | tf_op jit(solution)/shard_map/ppermute | solution.py:258
  5.4 1.5 %collective-permute-start.1 = (bf16[136,1024]{1,0:T(8,128)(2,1)}, bf16[136,1024]{1,0:T(8,128)(2,1)S(1)}, u32[]{:S(2)}, u32[]{:S(2)}) collective-permute-start(bf16[136,1024]{1,0:T(8,128)(2,1)} %pack.1.refs_1_), channel_id=1, source_target_pairs={{0,4},{2,6},{4,0},{6,2},{1,5},{3,7},{5,1},{7,3},{8,12},{10,14},{12... | collective-permute-start | bytes 835592 | tf_op jit(solution)/shard_map/ppermute | solution.py:214
  6.9 1.5 %collective-permute-start = (bf16[136,1024]{1,0:T(8,128)(2,1)}, bf16[136,1024]{1,0:T(8,128)(2,1)S(1)}, u32[]{:S(2)}, u32[]{:S(2)}) collective-permute-start(bf16[136,1024]{1,0:T(8,128)(2,1)} %pack.1.refs_1_), channel_id=1, source_target_pairs={{0,2},{2,0},{4,6},{6,4},{1,3},{3,1},{5,7},{7,5},{8,10},{10,8},{12,... | collective-permute-start | bytes 835592 | tf_op jit(solution)/shard_map/ppermute | solution.py:214
  8.5 3.4 %copy-done = bf16[32,128,1024]{2,1,0:T(8,128)(2,1)S(1)} copy-done((bf16[32,128,1024]{2,1,0:T(8,128)(2,1)S(1)}, bf16[32,128,1024]{2,1,0:T(8,128)(2,1)}, u32[]{:S(2)}) %copy-start) | copy-done | bytes 8388632
  11.9 0.7 %copy-done.3 = f32[32,128]{1,0:T(8,128)S(1)} copy-done((f32[32,128]{1,0:T(8,128)S(1)}, f32[32,128]{1,0:T(8,128)}, u32[]{:S(2)}) %copy-start.3) | copy-done | bytes 16408
  12.6 0.8 %prepare.1 = (bf16[512,1024]{1,0:T(8,128)(2,1)S(1)}, bf16[512,1024]{1,0:T(8,128)(2,1)S(1)}, f32[512,128]{1,0:T(8,128)S(1)}, f32[512,128]{1,0:T(8,128)S(1)}) custom-call(s32[3]{0:T(128)S(1)} %pad_add_fusion.where, bf16[32,128,1024]{2,1,0:T(8,128)(2,1)S(1)} %copy-done, f32[32,128]{1,0:T(8,128)S(1)} %copy-done.3), custom_call_target="tpu_custom_call" | custom-call | flops 1 | bytes 134217728 | tf_op jit(solution)/shard_map/prepare/pallas_call | solution.py:71
  13.7 1.2 %collective-permute-done.refs_0_ = bf16[136,1024]{1,0:T(8,128)(2,1)S(1)} collective-permute-done((bf16[136,1024]{1,0:T(8,128)(2,1)}, bf16[136,1024]{1,0:T(8,128)(2,1)S(1)}, u32[]{:S(2)}, u32[]{:S(2)}) %collective-permute-start) | collective-permute-done | bytes 278560 | tf_op jit(solution)/shard_map/ppermute | solution.py:214
  14.9 1.4 %collective-permute-start.5 = (bf16[136,1024]{1,0:T(8,128)(2,1)}, bf16[136,1024]{1,0:T(8,128)(2,1)S(1)}, u32[]{:S(2)}, u32[]{:S(2)}) collective-permute-start(bf16[136,1024]{1,0:T(8,128)(2,1)} %pack.1.refs_1_), channel_id=1, source_target_pairs={{0,6},{2,4},{4,2},{6,0},{1,7},{3,5},{5,3},{7,1},{8,14},{10,12},{12... | collective-permute-start | bytes 835592 | tf_op jit(solution)/shard_map/ppermute | solution.py:214
  16.4 2.6 %collective-permute-start.4 = (bf16[136,1024]{1,0:T(8,128)(2,1)S(1)}, bf16[136,1024]{1,0:T(8,128)(2,1)S(1)}, u32[]{:S(2)}, u32[]{:S(2)}) collective-permute-start(bf16[136,1024]{1,0:T(8,128)(2,1)S(1)} %collective-permute-done.2), channel_id=1, source_target_pairs={{0,8},{8,24},{24,16},{16,0},{1,9},{9,25},{25,17},{17,1},{2,10},{10... | collective-permute-start | bytes 835592 | tf_op jit(solution)/shard_map/ppermute | solution.py:267
  19.0 0.7 collective-permute-start.3
  19.7 5.0 %owner_side.2 = (bf16[128,1024]{1,0:T(8,128)(2,1)S(1)}, bf16[128,1024]{1,0:T(8,128)(2,1)S(1)}) custom-call(s32[1]{0:T(128)} %bitcast.base, bf16[136,1024]{1,0:T(8,128)(2,1)S(1)} %collective-permute-done.refs_0_, bf16[136,1024]{1,0:T(8,128)(2,1)S(1)} %collective-permute-done.1.refs_1_, bf16[32,128,1024]{2,1,0:T(8,128)(2,1)S(1)} %copy-done.1, ...), custom_call_target="tpu_custom_call" | custom-call | flops 1 | bytes 1 | tf_op jit(solution)/shard_map/owner_side/pallas_call | solution.py:139
  24.7 0.9 %collective-permute-done.4 = bf16[136,1024]{1,0:T(8,128)(2,1)S(1)} collective-permute-done((bf16[136,1024]{1,0:T(8,128)(2,1)S(1)}, bf16[136,1024]{1,0:T(8,128)(2,1)S(1)}, u32[]{:S(2)}, u32[]{:S(2)}) %collective-permute-start.4) | collective-permute-done | bytes 278560 | tf_op jit(solution)/shard_map/ppermute | solution.py:267
  25.6 5.1 %collective-permute-start.13 = (bf16[544,1024]{1,0:T(8,128)(2,1)S(1)}, bf16[544,1024]{1,0:T(8,128)(2,1)S(1)}, u32[]{:S(2)}, u32[]{:S(2)}) collective-permute-start(bf16[544,1024]{1,0:T(8,128)(2,1)S(1)} %pad_maximum_fusion.refs_0_), channel_id=1, source_target_pairs={{0,8},{8,0},{16,24},{24,16},{1,9},{9,1},{17,25},{25,17},{2,10},{10... | collective-permute-start | bytes 3342344 | tf_op jit(solution)/shard_map/ppermute | solution.py:277
  30.8 0.6 collective-permute-start.8
  31.4 1.2 %collective-permute-start.9 = (bf16[272,1024]{1,0:T(8,128)(2,1)S(1)}, bf16[272,1024]{1,0:T(8,128)(2,1)S(1)}, u32[]{:S(2)}, u32[]{:S(2)}) collective-permute-start(bf16[272,1024]{1,0:T(8,128)(2,1)S(1)} %pad_maximum_fusion.1.refs_0_), channel_id=1, source_target_pairs={{0,4},{2,6},{4,0},{6,2},{1,5},{3,7},{5,1},{7,3},{8,12},{10,14},{12... | collective-permute-start | bytes 1671176 | tf_op jit(solution)/shard_map/ppermute | solution.py:214
  32.6 1.5 %collective-permute-start.6 = (bf16[128,1024]{1,0:T(8,128)(2,1)S(1)}, bf16[128,1024]{1,0:T(8,128)(2,1)S(1)}, u32[]{:S(2)}, u32[]{:S(2)}) collective-permute-start(bf16[128,1024]{1,0:T(8,128)(2,1)S(1)} %get-tuple-element.41), channel_id=1, source_target_pairs={{0,2},{2,0},{4,6},{6,4},{1,3},{3,1},{5,7},{7,5},{8,10},{10,8},{12,... | collective-permute-start | bytes 786440 | tf_op jit(solution)/shard_map/ppermute | solution.py:214
  34.1 0.8 %collective-permute-start.7 = (bf16[128,1024]{1,0:T(8,128)(2,1)S(1)}, bf16[128,1024]{1,0:T(8,128)(2,1)S(1)}, u32[]{:S(2)}, u32[]{:S(2)}) collective-permute-start(bf16[128,1024]{1,0:T(8,128)(2,1)S(1)} %get-tuple-element.43), channel_id=1, source_target_pairs={{0,4},{2,6},{4,0},{6,2},{1,5},{3,7},{5,1},{7,3},{8,12},{10,14},{12... | collective-permute-start | bytes 786440 | tf_op jit(solution)/shard_map/ppermute | solution.py:214
  34.9 5.0 %owner_side.3 = (bf16[128,1024]{1,0:T(8,128)(2,1)S(1)}, f32[128,1024]{1,0:T(8,128)S(1)}) custom-call(s32[1]{0:T(128)} %bitcast.base, bf16[136,1024]{1,0:T(8,128)(2,1)S(1)} %collective-permute-done.5.refs_0_, bf16[136,1024]{1,0:T(8,128)(2,1)S(1)} %copy-done.2, bf16[32,128,1024]{2,1,0:T(8,128)(2,1)S(1)} %copy-done.1, f32[32,128]{1,0:T(8,128)S(1)} %copy-done.3), custom_call_target="tpu_custom_call" | custom-call | flops 1 | bytes 1 | tf_op jit(solution)/shard_map/owner_side/pallas_call | solution.py:139
  39.9 3.7 %label_side.5 = (f32[512,1024]{1,0:T(8,128)S(1)}, f32[512,1024]{1,0:T(8,128)S(1)}) custom-call(s32[3]{0:T(128)S(1)} %pad_add_fusion.where, bf16[544,1024]{1,0:T(8,128)(2,1)S(1)} %pad_maximum_fusion.refs_0_, bf16[512,1024]{1,0:T(8,128)(2,1)S(1)} %get-tuple-element.31.refs_1_.refs_3_.refs_2_, bf16[512,1024]{1,0:T(8,128)(2,1)S(1)} %get-tuple-element.32.refs_2_.refs_4_, ...), custom_call_target="tpu_custom_call" | custom-call | flops 1 | bytes 1 | tf_op jit(solution)/shard_map/label_side/pallas_call | solution.py:201
  43.6 2.6 %collective-permute-done.8.refs_1_ = bf16[272,1024]{1,0:T(8,128)(2,1)S(1)} collective-permute-done((bf16[272,1024]{1,0:T(8,128)(2,1)S(1)}, bf16[272,1024]{1,0:T(8,128)(2,1)S(1)}, u32[]{:S(2)}, u32[]{:S(2)}) %collective-permute-start.8) | collective-permute-done | bytes 557088 | tf_op jit(solution)/shard_map/ppermute | solution.py:214
  46.2 2.9 %collective-permute-done.6 = bf16[128,1024]{1,0:T(8,128)(2,1)S(1)} collective-permute-done((bf16[128,1024]{1,0:T(8,128)(2,1)S(1)}, bf16[128,1024]{1,0:T(8,128)(2,1)S(1)}, u32[]{:S(2)}, u32[]{:S(2)}) %collective-permute-start.6) | collective-permute-done | bytes 262176 | tf_op jit(solution)/shard_map/ppermute | solution.py:214
  49.3 1.7 %collective-permute-start.11 = (bf16[136,1024]{1,0:T(8,128)(2,1)S(1)}, bf16[136,1024]{1,0:T(8,128)(2,1)S(1)}, u32[]{:S(2)}, u32[]{:S(2)}) collective-permute-start(bf16[136,1024]{1,0:T(8,128)(2,1)S(1)} %slice.8), channel_id=1, source_target_pairs={{0,2},{2,0},{4,6},{6,4},{1,3},{3,1},{5,7},{7,5},{8,10},{10,8},{12,... | collective-permute-start | bytes 835592 | tf_op jit(solution)/shard_map/ppermute | solution.py:214
  51.0 0.4 collective-permute-start.12
  51.4 1.4 %collective-permute-start.10 = (bf16[128,1024]{1,0:T(8,128)(2,1)S(1)}, bf16[128,1024]{1,0:T(8,128)(2,1)S(1)}, u32[]{:S(2)}, u32[]{:S(2)}) collective-permute-start(bf16[128,1024]{1,0:T(8,128)(2,1)S(1)} %get-tuple-element.49), channel_id=1, source_target_pairs={{0,6},{2,4},{4,2},{6,0},{1,7},{3,5},{5,3},{7,1},{8,14},{10,12},{12... | collective-permute-start | bytes 786440 | tf_op jit(solution)/shard_map/ppermute | solution.py:214
  52.9 4.5 %label_side.6 = (f32[512,1024]{1,0:T(8,128)S(1)}, f32[512,1024]{1,0:T(8,128)S(1)}) custom-call(s32[3]{0:T(128)S(1)} %pad_add_fusion.where, bf16[272,1024]{1,0:T(8,128)(2,1)S(1)} %pad_maximum_fusion.1.refs_0_, bf16[272,1024]{1,0:T(8,128)(2,1)S(1)} %collective-permute-done.8.refs_1_, bf16[272,1024]{1,0:T(8,128)(2,1)S(1)} %collective-permute-done.9.refs_2_, ...), custom_call_target="tpu_custom_call" | custom-call | flops 1 | bytes 1 | tf_op jit(solution)/shard_map/label_side/pallas_call | solution.py:201
  57.4 3.1 %collective-permute-done.10 = bf16[128,1024]{1,0:T(8,128)(2,1)S(1)} collective-permute-done((bf16[128,1024]{1,0:T(8,128)(2,1)S(1)}, bf16[128,1024]{1,0:T(8,128)(2,1)S(1)}, u32[]{:S(2)}, u32[]{:S(2)}) %collective-permute-start.10) | collective-permute-done | bytes 262176 | tf_op jit(solution)/shard_map/ppermute | solution.py:214
  60.5 3.6 %label_side.7 = (f32[512,1024]{1,0:T(8,128)S(1)}, f32[512,1024]{1,0:T(8,128)S(1)}) custom-call(s32[3]{0:T(128)S(1)} %pad_add_fusion.where, bf16[544,1024]{1,0:T(8,128)(2,1)S(1)} %collective-permute-done.13.refs_0_, bf16[512,1024]{1,0:T(8,128)(2,1)S(1)} %get-tuple-element.31.refs_1_.refs_3_.refs_2_, bf16[512,1024]{1,0:T(8,128)(2,1)S(1)} %get-tuple-element.32.refs_2_.refs_4_, ...), custom_call_target="tpu_custom_call" | custom-call | flops 1 | bytes 1 | tf_op jit(solution)/shard_map/label_side/pallas_call | solution.py:201
  64.1 1.9 %label_side.8 = bf16[512,1024]{1,0:T(8,128)(2,1)S(1)} custom-call(s32[2]{0:T(128)S(1)} %pad_add_fusion.2.where, bf16[136,1024]{1,0:T(8,128)(2,1)S(1)} %collective-permute-done.11.refs_0_, bf16[136,1024]{1,0:T(8,128)(2,1)S(1)} %collective-permute-done.12.refs_1_, bf16[512,1024]{1,0:T(8,128)(2,1)S(1)} %get-tuple-element.31.refs_1_.refs_3_.refs_2_, ...), custom_call_target="tpu_custom_call" | custom-call | flops 1 | bytes 1 | tf_op jit(solution)/shard_map/label_side/pallas_call | solution.py:201
  66.2 0.9 %convert_add_fusion.1 = f32[128,1024]{1,0:T(8,128)} fusion(bf16[128,1024]{1,0:T(8,128)(2,1)S(1)} %collective-permute-done.10, bf16[128,1024]{1,0:T(8,128)(2,1)S(1)} %collective-permute-done.7, f32[128,1024]{1,0:T(8,128)S(1)} %get-tuple-element.40, bf16[128,1024]{1,0:T(8,128)(2,1)S(1)} %collective-permute-done.6), kind=kLoop, calls=%fused_computation.3 | loop fusion | flops 786432 | bytes 1835008 | tf_op jit(solution)/shard_map/add | solution.py:304
  67.1 1.9 %label_side.9 = f32[512,1024]{1,0:T(8,128)S(1)} custom-call(s32[2]{0:T(128)S(1)} %pad_add_fusion.1.where, bf16[136,1024]{1,0:T(8,128)(2,1)S(1)} %collective-permute-done.11.refs_0_, bf16[136,1024]{1,0:T(8,128)(2,1)S(1)} %collective-permute-done.12.refs_1_, bf16[512,1024]{1,0:T(8,128)(2,1)S(1)} %get-tuple-element.32.refs_2_.refs_4_, ...), custom_call_target="tpu_custom_call" | custom-call | flops 1 | bytes 1 | tf_op jit(solution)/shard_map/label_side/pallas_call | solution.py:201
  69.1 1.8 %convert_add_fusion = f32[512,1024]{1,0:T(8,128)} fusion(f32[512,1024]{1,0:T(8,128)S(1)} %label_side.9, bf16[512,1024]{1,0:T(8,128)(2,1)S(1)} %collective-permute-done.14), kind=kLoop, calls=%fused_computation | loop fusion | flops 1048576 | bytes 5242880 | tf_op jit(solution)/shard_map/add | solution.py:299
  (24 shorter events, 0.9 us)
Async XLA Ops:
  2.4 11.0 %collective-permute-start.2 = (bf16[136,1024]{1,0:T(8,128)(2,1)}, bf16[136,1024]{1,0:T(8,128)(2,1)S(1)}, u32[]{:S(2)}, u32[]{:S(2)}) collective-permute-start(bf16[136,1024]{1,0:T(8,128)(2,1)} %pack.1.refs_1_), channel_id=1, source_target_pairs={{0,8},{8,24},{24,16},{16,0},{1,9},{9,25},{25,17},{17,1},{2,10},{10... | collective-permute-start | bytes 835592 | tf_op jit(solution)/shard_map/ppermute | solution.py:258
  5.4 8.3 %collective-permute-start.1 = (bf16[136,1024]{1,0:T(8,128)(2,1)}, bf16[136,1024]{1,0:T(8,128)(2,1)S(1)}, u32[]{:S(2)}, u32[]{:S(2)}) collective-permute-start(bf16[136,1024]{1,0:T(8,128)(2,1)} %pack.1.refs_1_), channel_id=1, source_target_pairs={{0,4},{2,6},{4,0},{6,2},{1,5},{3,7},{5,1},{7,3},{8,12},{10,14},{12... | collective-permute-start | bytes 835592 | tf_op jit(solution)/shard_map/ppermute | solution.py:214
  6.9 8.0 %collective-permute-start = (bf16[136,1024]{1,0:T(8,128)(2,1)}, bf16[136,1024]{1,0:T(8,128)(2,1)S(1)}, u32[]{:S(2)}, u32[]{:S(2)}) collective-permute-start(bf16[136,1024]{1,0:T(8,128)(2,1)} %pack.1.refs_1_), channel_id=1, source_target_pairs={{0,2},{2,0},{4,6},{6,4},{1,3},{3,1},{5,7},{7,5},{8,10},{10,8},{12,... | collective-permute-start | bytes 835592 | tf_op jit(solution)/shard_map/ppermute | solution.py:214
  8.5 3.4 %copy-start = (bf16[32,128,1024]{2,1,0:T(8,128)(2,1)S(1)}, bf16[32,128,1024]{2,1,0:T(8,128)(2,1)}, u32[]{:S(2)}) copy-start(bf16[32,128,1024]{2,1,0:T(8,128)(2,1)} %refs_2_.3) | copy-start | bytes 25165828
  11.8 0.7 %copy-start.3 = (f32[32,128]{1,0:T(8,128)S(1)}, f32[32,128]{1,0:T(8,128)}, u32[]{:S(2)}) copy-start(f32[32,128]{1,0:T(8,128)} %refs_3_.3) | copy-start | bytes 49156
  12.6 7.1 %copy-start.1 = (bf16[32,128,1024]{2,1,0:T(8,128)(2,1)S(1)}, bf16[32,128,1024]{2,1,0:T(8,128)(2,1)}, u32[]{:S(2)}) copy-start(bf16[32,128,1024]{2,1,0:T(8,128)(2,1)} %refs_2_.3) | copy-start | bytes 25165828
  14.9 9.7 %copy-start.2 = (bf16[136,1024]{1,0:T(8,128)(2,1)S(1)}, bf16[136,1024]{1,0:T(8,128)(2,1)}, u32[]{:S(2)}) copy-start(bf16[136,1024]{1,0:T(8,128)(2,1)} %pack.1.refs_1_) | copy-start | bytes 835588
  14.9 9.7 %collective-permute-start.5 = (bf16[136,1024]{1,0:T(8,128)(2,1)}, bf16[136,1024]{1,0:T(8,128)(2,1)S(1)}, u32[]{:S(2)}, u32[]{:S(2)}) collective-permute-start(bf16[136,1024]{1,0:T(8,128)(2,1)} %pack.1.refs_1_), channel_id=1, source_target_pairs={{0,6},{2,4},{4,2},{6,0},{1,7},{3,5},{5,3},{7,1},{8,14},{10,12},{12... | collective-permute-start | bytes 835592 | tf_op jit(solution)/shard_map/ppermute | solution.py:214
  16.4 9.2 %collective-permute-start.4 = (bf16[136,1024]{1,0:T(8,128)(2,1)S(1)}, bf16[136,1024]{1,0:T(8,128)(2,1)S(1)}, u32[]{:S(2)}, u32[]{:S(2)}) collective-permute-start(bf16[136,1024]{1,0:T(8,128)(2,1)S(1)} %collective-permute-done.2), channel_id=1, source_target_pairs={{0,8},{8,24},{24,16},{16,0},{1,9},{9,25},{25,17},{17,1},{2,10},{10... | collective-permute-start | bytes 835592 | tf_op jit(solution)/shard_map/ppermute | solution.py:267
  19.0 6.6 %collective-permute-start.3 = (bf16[136,1024]{1,0:T(8,128)(2,1)S(1)}, bf16[136,1024]{1,0:T(8,128)(2,1)S(1)}, u32[]{:S(2)}, u32[]{:S(2)}) collective-permute-start(bf16[136,1024]{1,0:T(8,128)(2,1)S(1)} %collective-permute-done.2), channel_id=1, source_target_pairs={{0,0},{8,16},{16,8},{24,24},{1,1},{9,17},{17,9},{25,25},{2,2},{10,... | collective-permute-start | bytes 835592 | tf_op jit(solution)/shard_map/ppermute | solution.py:271
  25.6 34.9 %collective-permute-start.13 = (bf16[544,1024]{1,0:T(8,128)(2,1)S(1)}, bf16[544,1024]{1,0:T(8,128)(2,1)S(1)}, u32[]{:S(2)}, u32[]{:S(2)}) collective-permute-start(bf16[544,1024]{1,0:T(8,128)(2,1)S(1)} %pad_maximum_fusion.refs_0_), channel_id=1, source_target_pairs={{0,8},{8,0},{16,24},{24,16},{1,9},{9,1},{17,25},{25,17},{2,10},{10... | collective-permute-start | bytes 3342344 | tf_op jit(solution)/shard_map/ppermute | solution.py:277
  30.8 15.4 %collective-permute-start.8 = (bf16[272,1024]{1,0:T(8,128)(2,1)S(1)}, bf16[272,1024]{1,0:T(8,128)(2,1)S(1)}, u32[]{:S(2)}, u32[]{:S(2)}) collective-permute-start(bf16[272,1024]{1,0:T(8,128)(2,1)S(1)} %pad_maximum_fusion.1.refs_0_), channel_id=1, source_target_pairs={{0,2},{2,0},{4,6},{6,4},{1,3},{3,1},{5,7},{7,5},{8,10},{10,8},{12,... | collective-permute-start | bytes 1671176 | tf_op jit(solution)/shard_map/ppermute | solution.py:214
  31.4 17.9 %collective-permute-start.9 = (bf16[272,1024]{1,0:T(8,128)(2,1)S(1)}, bf16[272,1024]{1,0:T(8,128)(2,1)S(1)}, u32[]{:S(2)}, u32[]{:S(2)}) collective-permute-start(bf16[272,1024]{1,0:T(8,128)(2,1)S(1)} %pad_maximum_fusion.1.refs_0_), channel_id=1, source_target_pairs={{0,4},{2,6},{4,0},{6,2},{1,5},{3,7},{5,1},{7,3},{8,12},{10,14},{12... | collective-permute-start | bytes 1671176 | tf_op jit(solution)/shard_map/ppermute | solution.py:214
  32.6 16.5 %collective-permute-start.6 = (bf16[128,1024]{1,0:T(8,128)(2,1)S(1)}, bf16[128,1024]{1,0:T(8,128)(2,1)S(1)}, u32[]{:S(2)}, u32[]{:S(2)}) collective-permute-start(bf16[128,1024]{1,0:T(8,128)(2,1)S(1)} %get-tuple-element.41), channel_id=1, source_target_pairs={{0,2},{2,0},{4,6},{6,4},{1,3},{3,1},{5,7},{7,5},{8,10},{10,8},{12,... | collective-permute-start | bytes 786440 | tf_op jit(solution)/shard_map/ppermute | solution.py:214
  34.1 15.2 %collective-permute-start.7 = (bf16[128,1024]{1,0:T(8,128)(2,1)S(1)}, bf16[128,1024]{1,0:T(8,128)(2,1)S(1)}, u32[]{:S(2)}, u32[]{:S(2)}) collective-permute-start(bf16[128,1024]{1,0:T(8,128)(2,1)S(1)} %get-tuple-element.43), channel_id=1, source_target_pairs={{0,4},{2,6},{4,0},{6,2},{1,5},{3,7},{5,1},{7,3},{8,12},{10,14},{12... | collective-permute-start | bytes 786440 | tf_op jit(solution)/shard_map/ppermute | solution.py:214
  49.3 14.8 %collective-permute-start.11 = (bf16[136,1024]{1,0:T(8,128)(2,1)S(1)}, bf16[136,1024]{1,0:T(8,128)(2,1)S(1)}, u32[]{:S(2)}, u32[]{:S(2)}) collective-permute-start(bf16[136,1024]{1,0:T(8,128)(2,1)S(1)} %slice.8), channel_id=1, source_target_pairs={{0,2},{2,0},{4,6},{6,4},{1,3},{3,1},{5,7},{7,5},{8,10},{10,8},{12,... | collective-permute-start | bytes 835592 | tf_op jit(solution)/shard_map/ppermute | solution.py:214
  51.0 13.1 %collective-permute-start.12 = (bf16[136,1024]{1,0:T(8,128)(2,1)S(1)}, bf16[136,1024]{1,0:T(8,128)(2,1)S(1)}, u32[]{:S(2)}, u32[]{:S(2)}) collective-permute-start(bf16[136,1024]{1,0:T(8,128)(2,1)S(1)} %slice.9), channel_id=1, source_target_pairs={{0,4},{2,6},{4,0},{6,2},{1,5},{3,7},{5,1},{7,3},{8,12},{10,14},{12... | collective-permute-start | bytes 835592 | tf_op jit(solution)/shard_map/ppermute | solution.py:214
  51.4 9.1 %collective-permute-start.10 = (bf16[128,1024]{1,0:T(8,128)(2,1)S(1)}, bf16[128,1024]{1,0:T(8,128)(2,1)S(1)}, u32[]{:S(2)}, u32[]{:S(2)}) collective-permute-start(bf16[128,1024]{1,0:T(8,128)(2,1)S(1)} %get-tuple-element.49), channel_id=1, source_target_pairs={{0,6},{2,4},{4,2},{6,0},{1,7},{3,5},{5,3},{7,1},{8,14},{10,12},{12... | collective-permute-start | bytes 786440 | tf_op jit(solution)/shard_map/ppermute | solution.py:214
  66.0 3.0 %collective-permute-start.14 = (bf16[512,1024]{1,0:T(8,128)(2,1)S(1)}, bf16[512,1024]{1,0:T(8,128)(2,1)S(1)}, u32[]{:S(2)}, u32[]{:S(2)}) collective-permute-start(bf16[512,1024]{1,0:T(8,128)(2,1)S(1)} %label_side.8), channel_id=1, source_target_pairs={{0,1},{1,0},{2,3},{3,2},{4,5},{5,4},{6,7},{7,6},{8,9},{9,8},{10,11... | collective-permute-start | bytes 3145736 | tf_op jit(solution)/shard_map/ppermute | solution.py:214

commit v4 on v3

--- a/solution.py
+++ b/solution.py
@@ -190,7 +190,7 @@
         outs[side][...] = total.astype(outs[side].dtype)
 
 
-def b_call(xs, ws, invs, where, blocks, rows, extra, before, kind, pair=2):
+def b_call(xs, ws, invs, where, blocks, rows, extra, before, kinds, pair=2):
     n, sides = len(xs), len(ws)
     count = sum(x.shape[0] for x in xs) // (rows + extra)
     pair = min(pair, count)
@@ -200,7 +200,7 @@
     more = [x for side in before for x in side]
     return pl.pallas_call(
         functools.partial(b_body, n, sides, pair, len(more) // sides, blocks, rows, extra),
-        out_shape=[jax.ShapeDtypeStruct((labels, feats), kind)] * sides,
+        out_shape=[jax.ShapeDtypeStruct((labels, feats), kind) for kind in kinds],
         in_specs=[sm] + [vm] * (n + 2 * sides + len(more)), out_specs=[vm] * sides,
         scratch_shapes=[pltpu.VMEM((count * rows, feats), bf16), pltpu.VMEM((labels, count * rows), bf16)],
         compiler_params=pltpu.CompilerParams(vmem_limit_bytes=(16 << 20) + 8 * (count * rows + sides * labels) * feats),
@@ -239,6 +239,7 @@
     one = base.astype(i32).reshape(1)
     cut = label_count // 2 + 1
     first, second = list(range(1, cut)), list(range(cut, label_count)) + [0]
+
     ring = list(range(0, dp_count, 2))[:1] + list(range(1, dp_count, 2)) + list(range(0, dp_count, 2))[:0:-1]
     forward = [(a, ring[(i + 1) % dp_count]) for i, a in enumerate(ring)]
 
@@ -247,12 +248,13 @@
                      [f32 if k == 0 else bf16 for k in ks])
         return dict(zip(ks, out))
 
-    def label_call(xs, before, *done, kind=f32):
+    def label_call(xs, before, *done, kinds=None):
         pick = list(range(len(offs)))
         if len(before) < len(pick):
-            pick = pick[:1] if kind == bf16 else pick[1:]
+            pick = pick[:1] if kinds else pick[-1:]
         where = after(jnp.stack([base] + [offs[k] for k in pick]).astype(i32), *done)
-        out = b_call(xs, [ws[k] for k in pick], [invs[k] for k in pick], where, blocks, rows, extra, before, kind)
+        kinds = kinds or [f32] * len(pick)
+        out = b_call(xs, [ws[k] for k in pick], [invs[k] for k in pick], where, blocks, rows, extra, before, kinds)
         return [[x] for x in out]
 
     column = lax.ppermute(packed, "dp", forward)
@@ -270,15 +272,16 @@
         last_plane = [(a, a ^ 1) for a in range(dp_count)]
         columns[0] = lax.ppermute(after(column, *gate), "dp", [(0, 0), (1, 2), (2, 1), (3, 3)])
     parts = owner_call(first, after(one, *gate))
-    gate = [parts[1]] + columns + [here[k] for k in second[:-1]]
+    gate = [parts[1]] + [here[k] for k in second[:-1]]
     own_plane = after(jnp.concatenate([here[k] for k in range(label_count)], axis=0), *gate)
-    columns = after(jnp.concatenate(columns, axis=0), *gate)
-    spread = [swap(columns, "label", bit) for bit in bits[:2]]
     next_plane = lax.ppermute(own_plane, "dp", last_plane)
     back = {k: swap(after(parts[k], *gate), "label", k) for k in first}
     parts.update(owner_call(second, after(one, *gate)))
-    total = label_call([own_plane], [[]] * len(offs), parts[0])
-    gate = total[0] + spread + [back[k] for k in first]
+    gate = [parts[0]] + columns + [back[k] for k in first]
+    columns = after(jnp.concatenate(columns, axis=0), *gate)
+    spread = [swap(columns, "label", bit) for bit in bits[:2]]
+    total = label_call([own_plane, columns], [[]] * len(offs), *gate)
+    gate = total[0] + spread
     cut = columns.shape[0] // (rows + extra) // 2 * (rows + extra)
     corners = [
         swap(after(spread[1][:cut], *gate), "label", bits[0]),
@@ -286,19 +289,20 @@
     ]
     for k in second[:-1]:
         back[k] = swap(after(parts[k], *gate), "label", k)
-    total = label_call([columns] + spread, total, *gate)
-    total = label_call([next_plane], total)
     rest = []
     for bit in bits[2:]:
         rest += [swap(x, "label", bit) for x in [columns] + spread + corners + rest]
     for x in rest:
         total = label_call([x], total)
+    total = label_call(spread, total, *gate)
+    theirs = []
     if sections == 2:
-        theirs = label_call(corners, total[:1], *back.values(), kind=bf16)[0][0]
-        mine = label_call(corners, total[1:], theirs)[0][0]
-        total = [[mine + swap(theirs, "section", 1).astype(f32)]]
-    else:
-        total = label_call(corners, total, *back.values())
+        theirs = [label_call([next_plane], total[:1], kinds=[bf16])[0][0]]
+    mine = label_call([next_plane], total[-1:], *theirs)
+    if sections == 2:
+        mine = [mine[0] + [swap(after(theirs[0], *corners, *back.values()), "section", 1)]]
+        corners = sum([[x, swap(x, "section", 1)] for x in corners], [])
+    total = label_call(corners, mine)
     query_grad = parts[0]
     for k in range(1, label_count):
         query_grad = query_grad + back[k].astype(f32)

time: 71.1 us -> 66.1 us (0.930)
  starting transfers between devices: 23.6 us -> 21.4 us
  other arithmetic: 3.07 us -> 1.27 us
  waiting for transfers between devices: 11.2 us -> 9.83 us
    ppermute x1, starting transfers between devices: 5.13 us -> 0.75 us  [per_device(): next_plane = lax.ppermute(own_plane, 'dp', last_plane)]
    ppermute x11 -> x13, waiting for transfers between devices: 10.4 us -> 7.67 us  [swap(): return lax.ppermute(x, axis, [(i, i ^ bit) for i in range(size)])]
    ppermute x11 -> x13, starting transfers between devices: 12.2 us -> 14.8 us  [swap(): return lax.ppermute(x, axis, [(i, i ^ bit) for i in range(size)])]
    ppermute x1, waiting for transfers between devices: 0.01 us -> 2.16 us  [per_device(): column = lax.ppermute(packed, 'dp', forward)]
    add x1 -> x0, other arithmetic: 1.78 us -> none  [per_device(): total = [[mine + swap(theirs, 'section', 1).astype(f32)]]]
    ppermute x1, starting transfers between devices: 3.02 us -> 1.58 us  [per_device(): column = lax.ppermute(packed, 'dp', forward)]
    ppermute x1, starting transfers between devices: 2.59 us -> 3.56 us  [per_device(): columns.append(lax.ppermute(after(columns[-1], *gate), 'dp', forward))]
    ppermute x1, waiting for transfers between devices: 0.85 us -> 0.01 us  [per_device(): columns.append(lax.ppermute(after(columns[-1], *gate), 'dp', forward))]
  transfers between devices with their start and end apart: 15 -> 17, of which waited for: 7 -> 5; matrix products, arithmetic and copies ran while one was open for 2% -> 2% of each run, Pallas kernels for 34% -> 35%
where the time goes in v4:
time: 66.1 us; the launch traced here: 65.9 us
  Pallas kernels  28.4 us (43%)
  starting transfers between devices  21.4 us (32%)
  waiting for transfers between devices  9.83 us (15%)
  local copies, waits for them, and re-layouts  4.15 us (6%)
  other arithmetic  1.27 us (2%)
  between operations  0.83 us (1%)
    pallas_call x5, Pallas kernels, b_call(): pl.pallas_call(functools.partial(b_body, n, sides, pair, len(more) // sid...  15.9 us
    ppermute x13, starting transfers between devices, swap(): return lax.ppermute(x, axis, [(i, i ^ bit) for i in range(size)])  14.8 us
    pallas_call x2, Pallas kernels, a_call(): pl.pallas_call(functools.partial(a_body, n, group), out_shape=out_types,...  9.95 us
    ppermute x13, waiting for transfers between devices, swap(): return lax.ppermute(x, axis, [(i, i ^ bit) for i in range(size)])  7.67 us
    unnamed x10, local copies, waits for them, and re-layouts  4.11 us
    ppermute x1, starting transfers between devices, per_device(): columns.append(lax.ppermute(after(columns[-1], *gate), 'dp', forward))  3.56 us
    ppermute x1, waiting for transfers between devices, per_device(): column = lax.ppermute(packed, 'dp', forward)  2.16 us
    pallas_call x1, Pallas kernels, pack(): pl.pallas_call(pack_body, out_shape=jax.ShapeDtypeStruct((rows + positive...  1.72 us
  transfers between devices with their start and end apart: 17, of which 5 were waited for; matrix products, arithmetic and copies ran while one was open for 2% of the time, Pallas kernels for 35%

profile of v4, /device:TPU:0, one launch (start us, length us, event | category | flops | bytes accessed | tf_op | source)
XLA Modules:
  0.0 65.9 jit_solution(16948299660193186293)
XLA Ops:
  0.6 1.7 %pack.1.refs_1_ = bf16[136,1024]{1,0:T(8,128)(2,1)} custom-call(bf16[128,1024]{1,0:T(8,128)(2,1)} %queries.1, s32[8,128]{1,0:T(8,128)} %bitcast.6, s32[1,48]{1,0:T(1,128)} %shortlist.1, s32[128]{0:T(128)} %owner_map.1), custom_call_target="tpu_custom_call" | custom-call | tf_op jit(solution)/shard_map/pack/pallas_call | solution.py:43
  2.4 2.9 %collective-permute-start = (bf16[136,1024]{1,0:T(8,128)(2,1)}, bf16[136,1024]{1,0:T(8,128)(2,1)S(1)}, u32[]{:S(2)}, u32[]{:S(2)}) collective-permute-start(bf16[136,1024]{1,0:T(8,128)(2,1)} %pack.1.refs_1_), channel_id=1, source_target_pairs={{0,2},{2,0},{4,6},{6,4},{1,3},{3,1},{5,7},{7,5},{8,10},{10,8},{12,... | collective-permute-start | bytes 835592 | tf_op jit(solution)/shard_map/ppermute | solution.py:214
  5.3 1.5 %collective-permute-start.1 = (bf16[136,1024]{1,0:T(8,128)(2,1)}, bf16[136,1024]{1,0:T(8,128)(2,1)S(1)}, u32[]{:S(2)}, u32[]{:S(2)}) collective-permute-start(bf16[136,1024]{1,0:T(8,128)(2,1)} %pack.1.refs_1_), channel_id=1, source_target_pairs={{0,4},{2,6},{4,0},{6,2},{1,5},{3,7},{5,1},{7,3},{8,12},{10,14},{12... | collective-permute-start | bytes 835592 | tf_op jit(solution)/shard_map/ppermute | solution.py:214
  6.8 1.6 %collective-permute-start.2 = (bf16[136,1024]{1,0:T(8,128)(2,1)}, bf16[136,1024]{1,0:T(8,128)(2,1)S(1)}, u32[]{:S(2)}, u32[]{:S(2)}) collective-permute-start(bf16[136,1024]{1,0:T(8,128)(2,1)} %pack.1.refs_1_), channel_id=1, source_target_pairs={{0,8},{8,24},{24,16},{16,0},{1,9},{9,25},{25,17},{17,1},{2,10},{10... | collective-permute-start | bytes 835592 | tf_op jit(solution)/shard_map/ppermute | solution.py:260
  8.5 3.4 %copy-done = bf16[32,128,1024]{2,1,0:T(8,128)(2,1)S(1)} copy-done((bf16[32,128,1024]{2,1,0:T(8,128)(2,1)S(1)}, bf16[32,128,1024]{2,1,0:T(8,128)(2,1)}, u32[]{:S(2)}) %copy-start) | copy-done | bytes 8388632
  11.9 0.7 %copy-done.3 = f32[32,128]{1,0:T(8,128)S(1)} copy-done((f32[32,128]{1,0:T(8,128)S(1)}, f32[32,128]{1,0:T(8,128)}, u32[]{:S(2)}) %copy-start.3) | copy-done | bytes 16408
  12.6 0.8 %prepare.1 = (bf16[512,1024]{1,0:T(8,128)(2,1)S(1)}, bf16[512,1024]{1,0:T(8,128)(2,1)S(1)}, f32[512,128]{1,0:T(8,128)S(1)}, f32[512,128]{1,0:T(8,128)S(1)}) custom-call(s32[3]{0:T(128)S(1)} %pad_add_fusion.where, bf16[32,128,1024]{2,1,0:T(8,128)(2,1)S(1)} %copy-done, f32[32,128]{1,0:T(8,128)S(1)} %copy-done.3), custom_call_target="tpu_custom_call" | custom-call | flops 1 | bytes 134217728 | tf_op jit(solution)/shard_map/prepare/pallas_call | solution.py:71
  13.4 0.2 collective-permute-done.1.refs_1_
  13.6 2.2 %collective-permute-done.2 = bf16[136,1024]{1,0:T(8,128)(2,1)S(1)} collective-permute-done((bf16[136,1024]{1,0:T(8,128)(2,1)}, bf16[136,1024]{1,0:T(8,128)(2,1)S(1)}, u32[]{:S(2)}, u32[]{:S(2)}) %collective-permute-start.2) | collective-permute-done | bytes 278560 | tf_op jit(solution)/shard_map/ppermute | solution.py:260
  15.8 0.4 collective-permute-start.3
  16.2 0.7 %collective-permute-start.6 = (bf16[136,1024]{1,0:T(8,128)(2,1)S(1)}, bf16[136,1024]{1,0:T(8,128)(2,1)S(1)}, u32[]{:S(2)}, u32[]{:S(2)}) collective-permute-start(bf16[136,1024]{1,0:T(8,128)(2,1)S(1)} %collective-permute-done.2), channel_id=1, source_target_pairs={{0,0},{8,16},{16,8},{24,24},{1,1},{9,17},{17,9},{25,25},{2,2},{10,... | collective-permute-start | bytes 835592 | tf_op jit(solution)/shard_map/ppermute | solution.py:273
  16.9 3.6 %collective-permute-start.7 = (bf16[136,1024]{1,0:T(8,128)(2,1)S(1)}, bf16[136,1024]{1,0:T(8,128)(2,1)S(1)}, u32[]{:S(2)}, u32[]{:S(2)}) collective-permute-start(bf16[136,1024]{1,0:T(8,128)(2,1)S(1)} %collective-permute-done.2), channel_id=1, source_target_pairs={{0,8},{8,24},{24,16},{16,0},{1,9},{9,25},{25,17},{17,1},{2,10},{10... | collective-permute-start | bytes 835592 | tf_op jit(solution)/shard_map/ppermute | solution.py:269
  20.5 5.0 %owner_side.2 = (bf16[128,1024]{1,0:T(8,128)(2,1)S(1)}, bf16[128,1024]{1,0:T(8,128)(2,1)S(1)}) custom-call(s32[1]{0:T(128)} %bitcast.base, bf16[136,1024]{1,0:T(8,128)(2,1)S(1)} %collective-permute-done.refs_0_, bf16[136,1024]{1,0:T(8,128)(2,1)S(1)} %collective-permute-done.1.refs_1_, bf16[32,128,1024]{2,1,0:T(8,128)(2,1)S(1)} %copy-done.1, ...), custom_call_target="tpu_custom_call" | custom-call | flops 1 | bytes 1 | tf_op jit(solution)/shard_map/owner_side/pallas_call | solution.py:139
  25.6 0.7 %collective-permute-start.15 = (bf16[544,1024]{1,0:T(8,128)(2,1)S(1)}, bf16[544,1024]{1,0:T(8,128)(2,1)S(1)}, u32[]{:S(2)}, u32[]{:S(2)}) collective-permute-start(bf16[544,1024]{1,0:T(8,128)(2,1)S(1)} %pad_maximum_fusion.refs_0_), channel_id=1, source_target_pairs={{0,8},{8,0},{16,24},{24,16},{1,9},{9,1},{17,25},{25,17},{2,10},{10... | collective-permute-start | bytes 3342344 | tf_op jit(solution)/shard_map/ppermute | solution.py:277
  26.3 1.5 %collective-permute-start.5 = (bf16[128,1024]{1,0:T(8,128)(2,1)S(1)}, bf16[128,1024]{1,0:T(8,128)(2,1)S(1)}, u32[]{:S(2)}, u32[]{:S(2)}) collective-permute-start(bf16[128,1024]{1,0:T(8,128)(2,1)S(1)} %get-tuple-element.40), channel_id=1, source_target_pairs={{0,4},{2,6},{4,0},{6,2},{1,5},{3,7},{5,1},{7,3},{8,12},{10,14},{12... | collective-permute-start | bytes 786440 | tf_op jit(solution)/shard_map/ppermute | solution.py:214
  27.8 1.5 %collective-permute-start.4 = (bf16[128,1024]{1,0:T(8,128)(2,1)S(1)}, bf16[128,1024]{1,0:T(8,128)(2,1)S(1)}, u32[]{:S(2)}, u32[]{:S(2)}) collective-permute-start(bf16[128,1024]{1,0:T(8,128)(2,1)S(1)} %get-tuple-element.38), channel_id=1, source_target_pairs={{0,2},{2,0},{4,6},{6,4},{1,3},{3,1},{5,7},{7,5},{8,10},{10,8},{12,... | collective-permute-start | bytes 786440 | tf_op jit(solution)/shard_map/ppermute | solution.py:214
  29.3 5.0 %owner_side.3 = (bf16[128,1024]{1,0:T(8,128)(2,1)S(1)}, f32[128,1024]{1,0:T(8,128)S(1)}) custom-call(s32[1]{0:T(128)} %bitcast.base, bf16[136,1024]{1,0:T(8,128)(2,1)S(1)} %collective-permute-done.3.refs_0_, bf16[136,1024]{1,0:T(8,128)(2,1)S(1)} %copy-done.2, bf16[32,128,1024]{2,1,0:T(8,128)(2,1)S(1)} %copy-done.1, f32[32,128]{1,0:T(8,128)S(1)} %copy-done.4), custom_call_target="tpu_custom_call" | custom-call | flops 1 | bytes 1 | tf_op jit(solution)/shard_map/owner_side/pallas_call | solution.py:139
  34.4 2.3 %collective-permute-start.8 = (bf16[272,1024]{1,0:T(8,128)(2,1)S(1)}, bf16[272,1024]{1,0:T(8,128)(2,1)S(1)}, u32[]{:S(2)}, u32[]{:S(2)}) collective-permute-start(bf16[272,1024]{1,0:T(8,128)(2,1)S(1)} %pad_maximum_fusion.1.refs_1_), channel_id=1, source_target_pairs={{0,2},{2,0},{4,6},{6,4},{1,3},{3,1},{5,7},{7,5},{8,10},{10,8},{12,... | collective-permute-start | bytes 1671176 | tf_op jit(solution)/shard_map/ppermute | solution.py:214
  36.7 0.5 collective-permute-start.9
  37.2 4.6 %label_side.5 = (f32[512,1024]{1,0:T(8,128)S(1)}, f32[512,1024]{1,0:T(8,128)S(1)}) custom-call(s32[3]{0:T(128)S(1)} %pad_add_fusion.where, bf16[544,1024]{1,0:T(8,128)(2,1)S(1)} %pad_maximum_fusion.refs_0_, bf16[272,1024]{1,0:T(8,128)(2,1)S(1)} %pad_maximum_fusion.1.refs_1_, bf16[512,1024]{1,0:T(8,128)(2,1)S(1)} %get-tuple-element.29.refs_2_.refs_1_, ...), custom_call_target="tpu_custom_call" | custom-call | flops 1 | bytes 1 | tf_op jit(solution)/shard_map/label_side/pallas_call | solution.py:201
  41.8 5.3 %collective-permute-done.8.refs_0_ = bf16[272,1024]{1,0:T(8,128)(2,1)S(1)} collective-permute-done((bf16[272,1024]{1,0:T(8,128)(2,1)S(1)}, bf16[272,1024]{1,0:T(8,128)(2,1)S(1)}, u32[]{:S(2)}, u32[]{:S(2)}) %collective-permute-start.8) | collective-permute-done | bytes 557088 | tf_op jit(solution)/shard_map/ppermute | solution.py:214
  47.0 0.6 collective-permute-done.9.refs_1_
  47.7 0.5 collective-permute-start.13
  48.2 1.8 %collective-permute-start.11 = (bf16[136,1024]{1,0:T(8,128)(2,1)S(1)}, bf16[136,1024]{1,0:T(8,128)(2,1)S(1)}, u32[]{:S(2)}, u32[]{:S(2)}) collective-permute-start(bf16[136,1024]{1,0:T(8,128)(2,1)S(1)} %slice.8), channel_id=1, source_target_pairs={{0,2},{2,0},{4,6},{6,4},{1,3},{3,1},{5,7},{7,5},{8,10},{10,8},{12,... | collective-permute-start | bytes 835592 | tf_op jit(solution)/shard_map/ppermute | solution.py:214
  50.0 1.2 %collective-permute-start.10 = (bf16[128,1024]{1,0:T(8,128)(2,1)S(1)}, bf16[128,1024]{1,0:T(8,128)(2,1)S(1)}, u32[]{:S(2)}, u32[]{:S(2)}) collective-permute-start(bf16[128,1024]{1,0:T(8,128)(2,1)S(1)} %get-tuple-element.47), channel_id=1, source_target_pairs={{0,6},{2,4},{4,2},{6,0},{1,7},{3,5},{5,3},{7,1},{8,14},{10,12},{12... | collective-permute-start | bytes 786440 | tf_op jit(solution)/shard_map/ppermute | solution.py:214
  51.3 3.6 %label_side.6 = (f32[512,1024]{1,0:T(8,128)S(1)}, f32[512,1024]{1,0:T(8,128)S(1)}) custom-call(s32[3]{0:T(128)S(1)} %pad_add_fusion.where, bf16[272,1024]{1,0:T(8,128)(2,1)S(1)} %collective-permute-done.8.refs_0_, bf16[272,1024]{1,0:T(8,128)(2,1)S(1)} %collective-permute-done.9.refs_1_, bf16[512,1024]{1,0:T(8,128)(2,1)S(1)} %get-tuple-element.29.refs_2_.refs_1_, ...), custom_call_target="tpu_custom_call" | custom-call | flops 1 | bytes 1 | tf_op jit(solution)/shard_map/label_side/pallas_call | solution.py:201
  54.9 2.1 %label_side.7 = bf16[512,1024]{1,0:T(8,128)(2,1)S(1)} custom-call(s32[2]{0:T(128)S(1)} %pad_add_fusion.2.where, bf16[544,1024]{1,0:T(8,128)(2,1)S(1)} %collective-permute-done.15.refs_0_, bf16[512,1024]{1,0:T(8,128)(2,1)S(1)} %get-tuple-element.29.refs_2_.refs_1_, f32[512,128]{1,0:T(8,128)S(1)} %get-tuple-element.31.refs_4_.refs_2_, ...), custom_call_target="tpu_custom_call" | custom-call | flops 1 | bytes 1 | tf_op jit(solution)/shard_map/label_side/pallas_call | solution.py:201
  57.1 1.5 %collective-permute-done.10 = bf16[128,1024]{1,0:T(8,128)(2,1)S(1)} collective-permute-done((bf16[128,1024]{1,0:T(8,128)(2,1)S(1)}, bf16[128,1024]{1,0:T(8,128)(2,1)S(1)}, u32[]{:S(2)}, u32[]{:S(2)}) %collective-permute-start.10) | collective-permute-done | bytes 262176 | tf_op jit(solution)/shard_map/ppermute | solution.py:214
  58.6 0.5 collective-permute-start.14
  59.3 0.9 %convert_add_fusion = f32[128,1024]{1,0:T(8,128)} fusion(bf16[128,1024]{1,0:T(8,128)(2,1)S(1)} %collective-permute-done.10, bf16[128,1024]{1,0:T(8,128)(2,1)S(1)} %collective-permute-done.5, f32[128,1024]{1,0:T(8,128)S(1)} %get-tuple-element.37, bf16[128,1024]{1,0:T(8,128)(2,1)S(1)} %collective-permute-done.4), kind=kLoop, calls=%fused_computation.2 | loop fusion | flops 786432 | bytes 1835008 | tf_op jit(solution)/shard_map/add | solution.py:308
  60.2 2.1 %label_side.8.refs_6_ = f32[512,1024]{1,0:T(8,128)S(1)} custom-call(s32[2]{0:T(128)S(1)} %pad_add_fusion.1.where, bf16[544,1024]{1,0:T(8,128)(2,1)S(1)} %collective-permute-done.15.refs_0_, bf16[512,1024]{1,0:T(8,128)(2,1)S(1)} %get-tuple-element.30.refs_3_.refs_1_.refs_4_, f32[512,128]{1,0:T(8,128)S(1)} %get-tuple-element.32.refs_5_.refs_2_, ...), custom_call_target="tpu_custom_call" | custom-call | flops 1 | bytes 1 | tf_op jit(solution)/shard_map/label_side/pallas_call | solution.py:201
  62.4 3.5 %label_side.9 = f32[512,1024]{1,0:T(8,128)} custom-call(s32[2]{0:T(128)S(1)} %pad_add_fusion.1.where, bf16[136,1024]{1,0:T(8,128)(2,1)S(1)} %collective-permute-done.11.refs_0_, bf16[136,1024]{1,0:T(8,128)(2,1)S(1)} %collective-permute-done.12.refs_1_, bf16[136,1024]{1,0:T(8,128)(2,1)S(1)} %collective-permute-done.13.refs_2_, ...), custom_call_target="tpu_custom_call" | custom-call | flops 1 | bytes 1 | tf_op jit(solution)/shard_map/label_side/pallas_call | solution.py:201
  (29 shorter events, 0.5 us)
Async XLA Ops:
  2.4 11.0 %collective-permute-start = (bf16[136,1024]{1,0:T(8,128)(2,1)}, bf16[136,1024]{1,0:T(8,128)(2,1)S(1)}, u32[]{:S(2)}, u32[]{:S(2)}) collective-permute-start(bf16[136,1024]{1,0:T(8,128)(2,1)} %pack.1.refs_1_), channel_id=1, source_target_pairs={{0,2},{2,0},{4,6},{6,4},{1,3},{3,1},{5,7},{7,5},{8,10},{10,8},{12,... | collective-permute-start | bytes 835592 | tf_op jit(solution)/shard_map/ppermute | solution.py:214
  5.3 8.3 %collective-permute-start.1 = (bf16[136,1024]{1,0:T(8,128)(2,1)}, bf16[136,1024]{1,0:T(8,128)(2,1)S(1)}, u32[]{:S(2)}, u32[]{:S(2)}) collective-permute-start(bf16[136,1024]{1,0:T(8,128)(2,1)} %pack.1.refs_1_), channel_id=1, source_target_pairs={{0,4},{2,6},{4,0},{6,2},{1,5},{3,7},{5,1},{7,3},{8,12},{10,14},{12... | collective-permute-start | bytes 835592 | tf_op jit(solution)/shard_map/ppermute | solution.py:214
  6.8 9.0 %collective-permute-start.2 = (bf16[136,1024]{1,0:T(8,128)(2,1)}, bf16[136,1024]{1,0:T(8,128)(2,1)S(1)}, u32[]{:S(2)}, u32[]{:S(2)}) collective-permute-start(bf16[136,1024]{1,0:T(8,128)(2,1)} %pack.1.refs_1_), channel_id=1, source_target_pairs={{0,8},{8,24},{24,16},{16,0},{1,9},{9,25},{25,17},{17,1},{2,10},{10... | collective-permute-start | bytes 835592 | tf_op jit(solution)/shard_map/ppermute | solution.py:260
  8.5 3.4 %copy-start = (bf16[32,128,1024]{2,1,0:T(8,128)(2,1)S(1)}, bf16[32,128,1024]{2,1,0:T(8,128)(2,1)}, u32[]{:S(2)}) copy-start(bf16[32,128,1024]{2,1,0:T(8,128)(2,1)} %refs_2_.3) | copy-start | bytes 25165828
  11.8 0.7 %copy-start.3 = (f32[32,128]{1,0:T(8,128)S(1)}, f32[32,128]{1,0:T(8,128)}, u32[]{:S(2)}) copy-start(f32[32,128]{1,0:T(8,128)} %refs_3_.3) | copy-start | bytes 49156
  12.6 7.9 %copy-start.1 = (bf16[32,128,1024]{2,1,0:T(8,128)(2,1)S(1)}, bf16[32,128,1024]{2,1,0:T(8,128)(2,1)}, u32[]{:S(2)}) copy-start(bf16[32,128,1024]{2,1,0:T(8,128)(2,1)} %refs_2_.3) | copy-start | bytes 25165828
  15.8 9.7 %copy-start.2 = (bf16[136,1024]{1,0:T(8,128)(2,1)S(1)}, bf16[136,1024]{1,0:T(8,128)(2,1)}, u32[]{:S(2)}) copy-start(bf16[136,1024]{1,0:T(8,128)(2,1)} %pack.1.refs_1_) | copy-start | bytes 835588
  15.8 9.7 %collective-permute-start.3 = (bf16[136,1024]{1,0:T(8,128)(2,1)}, bf16[136,1024]{1,0:T(8,128)(2,1)S(1)}, u32[]{:S(2)}, u32[]{:S(2)}) collective-permute-start(bf16[136,1024]{1,0:T(8,128)(2,1)} %pack.1.refs_1_), channel_id=1, source_target_pairs={{0,6},{2,4},{4,2},{6,0},{1,7},{3,5},{5,3},{7,1},{8,14},{10,12},{12... | collective-permute-start | bytes 835592 | tf_op jit(solution)/shard_map/ppermute | solution.py:214
  16.2 18.1 %collective-permute-start.6 = (bf16[136,1024]{1,0:T(8,128)(2,1)S(1)}, bf16[136,1024]{1,0:T(8,128)(2,1)S(1)}, u32[]{:S(2)}, u32[]{:S(2)}) collective-permute-start(bf16[136,1024]{1,0:T(8,128)(2,1)S(1)} %collective-permute-done.2), channel_id=1, source_target_pairs={{0,0},{8,16},{16,8},{24,24},{1,1},{9,17},{17,9},{25,25},{2,2},{10,... | collective-permute-start | bytes 835592 | tf_op jit(solution)/shard_map/ppermute | solution.py:273
  16.9 17.4 %collective-permute-start.7 = (bf16[136,1024]{1,0:T(8,128)(2,1)S(1)}, bf16[136,1024]{1,0:T(8,128)(2,1)S(1)}, u32[]{:S(2)}, u32[]{:S(2)}) collective-permute-start(bf16[136,1024]{1,0:T(8,128)(2,1)S(1)} %collective-permute-done.2), channel_id=1, source_target_pairs={{0,8},{8,24},{24,16},{16,0},{1,9},{9,25},{25,17},{17,1},{2,10},{10... | collective-permute-start | bytes 835592 | tf_op jit(solution)/shard_map/ppermute | solution.py:269
  25.4 3.9 %copy-start.4 = (f32[32,128]{1,0:T(8,128)S(1)}, f32[32,128]{1,0:T(8,128)}, u32[]{:S(2)}) copy-start(f32[32,128]{1,0:T(8,128)} %refs_3_.3) | copy-start | bytes 49156
  25.6 29.4 %collective-permute-start.15 = (bf16[544,1024]{1,0:T(8,128)(2,1)S(1)}, bf16[544,1024]{1,0:T(8,128)(2,1)S(1)}, u32[]{:S(2)}, u32[]{:S(2)}) collective-permute-start(bf16[544,1024]{1,0:T(8,128)(2,1)S(1)} %pad_maximum_fusion.refs_0_), channel_id=1, source_target_pairs={{0,8},{8,0},{16,24},{24,16},{1,9},{9,1},{17,25},{25,17},{2,10},{10... | collective-permute-start | bytes 3342344 | tf_op jit(solution)/shard_map/ppermute | solution.py:277
  26.3 8.1 %collective-permute-start.5 = (bf16[128,1024]{1,0:T(8,128)(2,1)S(1)}, bf16[128,1024]{1,0:T(8,128)(2,1)S(1)}, u32[]{:S(2)}, u32[]{:S(2)}) collective-permute-start(bf16[128,1024]{1,0:T(8,128)(2,1)S(1)} %get-tuple-element.40), channel_id=1, source_target_pairs={{0,4},{2,6},{4,0},{6,2},{1,5},{3,7},{5,1},{7,3},{8,12},{10,14},{12... | collective-permute-start | bytes 786440 | tf_op jit(solution)/shard_map/ppermute | solution.py:214
  27.8 6.6 %collective-permute-start.4 = (bf16[128,1024]{1,0:T(8,128)(2,1)S(1)}, bf16[128,1024]{1,0:T(8,128)(2,1)S(1)}, u32[]{:S(2)}, u32[]{:S(2)}) collective-permute-start(bf16[128,1024]{1,0:T(8,128)(2,1)S(1)} %get-tuple-element.38), channel_id=1, source_target_pairs={{0,2},{2,0},{4,6},{6,4},{1,3},{3,1},{5,7},{7,5},{8,10},{10,8},{12,... | collective-permute-start | bytes 786440 | tf_op jit(solution)/shard_map/ppermute | solution.py:214
  34.4 12.6 %collective-permute-start.8 = (bf16[272,1024]{1,0:T(8,128)(2,1)S(1)}, bf16[272,1024]{1,0:T(8,128)(2,1)S(1)}, u32[]{:S(2)}, u32[]{:S(2)}) collective-permute-start(bf16[272,1024]{1,0:T(8,128)(2,1)S(1)} %pad_maximum_fusion.1.refs_1_), channel_id=1, source_target_pairs={{0,2},{2,0},{4,6},{6,4},{1,3},{3,1},{5,7},{7,5},{8,10},{10,8},{12,... | collective-permute-start | bytes 1671176 | tf_op jit(solution)/shard_map/ppermute | solution.py:214
  36.7 11.0 %collective-permute-start.9 = (bf16[272,1024]{1,0:T(8,128)(2,1)S(1)}, bf16[272,1024]{1,0:T(8,128)(2,1)S(1)}, u32[]{:S(2)}, u32[]{:S(2)}) collective-permute-start(bf16[272,1024]{1,0:T(8,128)(2,1)S(1)} %pad_maximum_fusion.1.refs_1_), channel_id=1, source_target_pairs={{0,4},{2,6},{4,0},{6,2},{1,5},{3,7},{5,1},{7,3},{8,12},{10,14},{12... | collective-permute-start | bytes 1671176 | tf_op jit(solution)/shard_map/ppermute | solution.py:214
  47.7 10.9 %collective-permute-start.13 = (bf16[136,1024]{1,0:T(8,128)(2,1)S(1)}, bf16[136,1024]{1,0:T(8,128)(2,1)S(1)}, u32[]{:S(2)}, u32[]{:S(2)}) collective-permute-start(bf16[136,1024]{1,0:T(8,128)(2,1)S(1)} %slice.9), channel_id=1, source_target_pairs={{0,4},{2,6},{4,0},{6,2},{1,5},{3,7},{5,1},{7,3},{8,12},{10,14},{12... | collective-permute-start | bytes 835592 | tf_op jit(solution)/shard_map/ppermute | solution.py:214
  48.2 10.4 %collective-permute-start.11 = (bf16[136,1024]{1,0:T(8,128)(2,1)S(1)}, bf16[136,1024]{1,0:T(8,128)(2,1)S(1)}, u32[]{:S(2)}, u32[]{:S(2)}) collective-permute-start(bf16[136,1024]{1,0:T(8,128)(2,1)S(1)} %slice.8), channel_id=1, source_target_pairs={{0,2},{2,0},{4,6},{6,4},{1,3},{3,1},{5,7},{7,5},{8,10},{10,8},{12,... | collective-permute-start | bytes 835592 | tf_op jit(solution)/shard_map/ppermute | solution.py:214
  50.0 8.6 %collective-permute-start.10 = (bf16[128,1024]{1,0:T(8,128)(2,1)S(1)}, bf16[128,1024]{1,0:T(8,128)(2,1)S(1)}, u32[]{:S(2)}, u32[]{:S(2)}) collective-permute-start(bf16[128,1024]{1,0:T(8,128)(2,1)S(1)} %get-tuple-element.47), channel_id=1, source_target_pairs={{0,6},{2,4},{4,2},{6,0},{1,7},{3,5},{5,3},{7,1},{8,14},{10,12},{12... | collective-permute-start | bytes 786440 | tf_op jit(solution)/shard_map/ppermute | solution.py:214
  58.6 3.8 %collective-permute-start.16 = (bf16[512,1024]{1,0:T(8,128)(2,1)S(1)}, bf16[512,1024]{1,0:T(8,128)(2,1)S(1)}, u32[]{:S(2)}, u32[]{:S(2)}) collective-permute-start(bf16[512,1024]{1,0:T(8,128)(2,1)S(1)} %label_side.7), channel_id=1, source_target_pairs={{0,1},{1,0},{2,3},{3,2},{4,5},{5,4},{6,7},{7,6},{8,9},{9,8},{10,11... | collective-permute-start | bytes 3145736 | tf_op jit(solution)/shard_map/ppermute | solution.py:214
  58.6 3.7 %collective-permute-start.14 = (bf16[136,1024]{1,0:T(8,128)(2,1)S(1)}, bf16[136,1024]{1,0:T(8,128)(2,1)S(1)}, u32[]{:S(2)}, u32[]{:S(2)}) collective-permute-start(bf16[136,1024]{1,0:T(8,128)(2,1)S(1)} %collective-permute-done.13.refs_2_), channel_id=1, source_target_pairs={{0,1},{1,0},{2,3},{3,2},{4,5},{5,4},{6,7},{7,6},{8,9},{9,8},{10,11... | collective-permute-start | bytes 835592 | tf_op jit(solution)/shard_map/ppermute | solution.py:214
  59.1 3.2 %collective-permute-start.12 = (bf16[136,1024]{1,0:T(8,128)(2,1)S(1)}, bf16[136,1024]{1,0:T(8,128)(2,1)S(1)}, u32[]{:S(2)}, u32[]{:S(2)}) collective-permute-start(bf16[136,1024]{1,0:T(8,128)(2,1)S(1)} %collective-permute-done.11.refs_0_), channel_id=1, source_target_pairs={{0,1},{1,0},{2,3},{3,2},{4,5},{5,4},{6,7},{7,6},{8,9},{9,8},{10,11... | collective-permute-start | bytes 835592 | tf_op jit(solution)/shard_map/ppermute | solution.py:214

commit v5 on v4

--- a/solution.py
+++ b/solution.py
@@ -150,10 +150,10 @@
     )(base, *xs, w, prop)
 
 
-def b_body(n, sides, pair, adds, blocks, rows, extra, where, *refs):
+def b_body(n, sides, pair, adds, blocks, rows, extra, pieces, where, *refs):
     xs, ws, invs, rest = refs[:n], refs[n:n + sides], refs[n + sides:n + 2 * sides], refs[n + 2 * sides:]
     before, rest = rest[:adds * sides], rest[adds * sides:]
-    outs, (x_all, grads) = rest[:sides], rest[sides:]
+    outs, (x_all, grads), stage = rest[:sides], rest[sides:sides + 2], rest[sides + 2:]
     labels = ws[0].shape[0]
     each = labels // blocks
     base = where[0]
@@ -184,13 +184,25 @@
                 s = scores[:, (k - k0) * rows:(k - k0 + 1) * rows]
                 g = half * jnp.tanh(0.5 * s) + (half - jnp.where(got, invs[side][...], 0.0))
                 grads[:, k * rows:(k + 1) * rows] = g.astype(bf16)
-        total = lax.dot_general(grads[...], x_all[...], NN, preferred_element_type=f32)
-        for old in before[side * adds:(side + 1) * adds]:
-            total = total + old[...]
-        outs[side][...] = total.astype(outs[side].dtype)
-
-
-def b_call(xs, ws, invs, where, blocks, rows, extra, before, kinds, pair=2):
+        part = labels // pieces
+        copies = []
+        for piece in range(pieces):
+            span = slice(piece * part, (piece + 1) * part)
+            total = lax.dot_general(grads[span, :], x_all[...], NN, preferred_element_type=f32)
+            for old in before[side * adds:(side + 1) * adds]:
+                total = total + old[span, :]
+            if pieces == 1:
+                outs[side][...] = total.astype(outs[side].dtype)
+                continue
+            stage[0][span, :] = total
+            copies.append(pltpu.make_async_copy(
+                stage[0].at[pl.ds(piece * part, part)], outs[side].at[pl.ds(piece * part, part)], stage[1].at[piece]))
+            copies[-1].start()
+        for copy in copies:
+            copy.wait()
+
+
+def b_call(xs, ws, invs, where, blocks, rows, extra, before, kinds, pieces=1, pair=2):
     n, sides = len(xs), len(ws)
     count = sum(x.shape[0] for x in xs) // (rows + extra)
     pair = min(pair, count)
@@ -199,10 +211,12 @@
     sm = pl.BlockSpec(memory_space=pltpu.SMEM)
     more = [x for side in before for x in side]
     return pl.pallas_call(
-        functools.partial(b_body, n, sides, pair, len(more) // sides, blocks, rows, extra),
+        functools.partial(b_body, n, sides, pair, len(more) // sides, blocks, rows, extra, pieces),
         out_shape=[jax.ShapeDtypeStruct((labels, feats), kind) for kind in kinds],
-        in_specs=[sm] + [vm] * (n + 2 * sides + len(more)), out_specs=[vm] * sides,
-        scratch_shapes=[pltpu.VMEM((count * rows, feats), bf16), pltpu.VMEM((labels, count * rows), bf16)],
+        in_specs=[sm] + [vm] * (n + 2 * sides + len(more)),
+        out_specs=[vm if pieces == 1 else pl.BlockSpec(memory_space=pl.ANY)] * sides,
+        scratch_shapes=[pltpu.VMEM((count * rows, feats), bf16), pltpu.VMEM((labels, count * rows), bf16)]
+        + [pltpu.VMEM((labels, feats), f32), pltpu.SemaphoreType.DMA((pieces,))] * (pieces > 1),
         compiler_params=pltpu.CompilerParams(vmem_limit_bytes=(16 << 20) + 8 * (count * rows + sides * labels) * feats),
         cost_estimate=pl.CostEstimate(flops=1, bytes_accessed=1, transcendentals=0),
         name="label_side",
@@ -248,13 +262,13 @@
                      [f32 if k == 0 else bf16 for k in ks])
         return dict(zip(ks, out))
 
-    def label_call(xs, before, *done, kinds=None):
+    def label_call(xs, before, *done, kinds=None, pieces=1):
         pick = list(range(len(offs)))
         if len(before) < len(pick):
             pick = pick[:1] if kinds else pick[-1:]
         where = after(jnp.stack([base] + [offs[k] for k in pick]).astype(i32), *done)
         kinds = kinds or [f32] * len(pick)
-        out = b_call(xs, [ws[k] for k in pick], [invs[k] for k in pick], where, blocks, rows, extra, before, kinds)
+        out = b_call(xs, [ws[k] for k in pick], [invs[k] for k in pick], where, blocks, rows, extra, before, kinds, pieces)
         return [[x] for x in out]
 
     column = lax.ppermute(packed, "dp", forward)
@@ -263,7 +277,7 @@
         here[k] = swap(packed, "label", k)
     gate = [here[k] for k in first] + [column] + list(ws) + list(invs)
     for k in second[:-1]:
-        here[k] = swap(after(packed, *gate), "label", k)
+        here[k] = swap(after(packed, *[x for x in gate if x is not column]), "label", k)
     columns = [column]
     for _ in range(dp_count - 3):
         columns.append(lax.ppermute(after(columns[-1], *gate), "dp", forward))
@@ -271,7 +285,7 @@
     if dp_count == 4:
         last_plane = [(a, a ^ 1) for a in range(dp_count)]
         columns[0] = lax.ppermute(after(column, *gate), "dp", [(0, 0), (1, 2), (2, 1), (3, 3)])
-    parts = owner_call(first, after(one, *gate))
+    parts = owner_call(first, after(one, *[x for x in gate if x is not column]))
     gate = [parts[1]] + [here[k] for k in second[:-1]]
     own_plane = after(jnp.concatenate([here[k] for k in range(label_count)], axis=0), *gate)
     next_plane = lax.ppermute(own_plane, "dp", last_plane)
@@ -302,7 +316,7 @@
     if sections == 2:
         mine = [mine[0] + [swap(after(theirs[0], *corners, *back.values()), "section", 1)]]
         corners = sum([[x, swap(x, "section", 1)] for x in corners], [])
-    total = label_call(corners, mine)
+    total = label_call(corners, mine, pieces=2 if blocks * each % 32 == 0 else 1)
     query_grad = parts[0]
     for k in range(1, label_count):
         query_grad = query_grad + back[k].astype(f32)

time: 66.1 us -> 64.5 us (0.976)
  waiting for transfers between devices: 9.83 us -> 8.62 us
    ppermute x1, waiting for transfers between devices: 2.16 us -> 0.66 us  [per_device(): column = lax.ppermute(packed, 'dp', forward)]
    ppermute x1, waiting for transfers between devices: 0.01 us -> 0.77 us  [per_device(): next_plane = lax.ppermute(own_plane, 'dp', last_plane)]
  transfers between devices with their start and end apart: 17 -> 17, of which waited for: 5 -> 7; matrix products, arithmetic and copies ran while one was open for 2% -> 2% of each run, Pallas kernels for 35% -> 36%
where the time goes in v5:
time: 64.5 us; the launch traced here: 64.3 us
  Pallas kernels  28 us (43%)
  starting transfers between devices  21.2 us (33%)
  waiting for transfers between devices  8.62 us (13%)
  local copies, waits for them, and re-layouts  4.15 us (6%)
  other arithmetic  1.27 us (2%)
  between operations  0.97 us (2%)
    pallas_call x5, Pallas kernels, b_call(): pl.pallas_call(functools.partial(b_body, n, sides, pair, len(more) // sid...  15.6 us
    ppermute x13, starting transfers between devices, swap(): return lax.ppermute(x, axis, [(i, i ^ bit) for i in range(size)])  14.7 us
    pallas_call x2, Pallas kernels, a_call(): pl.pallas_call(functools.partial(a_body, n, group), out_shape=out_types,...  9.94 us
    ppermute x13, waiting for transfers between devices, swap(): return lax.ppermute(x, axis, [(i, i ^ bit) for i in range(size)])  7.18 us
    unnamed x10, local copies, waits for them, and re-layouts  4.11 us
    ppermute x1, starting transfers between devices, per_device(): columns.append(lax.ppermute(after(columns[-1], *gate), 'dp', forward))  3.78 us
    pallas_call x1, Pallas kernels, pack(): pl.pallas_call(pack_body, out_shape=jax.ShapeDtypeStruct((rows + positive...  1.72 us
    ppermute x1, starting transfers between devices, per_device(): column = lax.ppermute(packed, 'dp', forward)  1.58 us
  transfers between devices with their start and end apart: 17, of which 7 were waited for; matrix products, arithmetic and copies ran while one was open for 2% of the time, Pallas kernels for 36%

profile of v5, /device:TPU:0, one launch (start us, length us, event | category | flops | bytes accessed | tf_op | source)
XLA Modules:
  0.0 64.3 jit_solution(11352842011616953078)
XLA Ops:
  0.6 1.7 %pack.1.refs_1_ = bf16[136,1024]{1,0:T(8,128)(2,1)} custom-call(bf16[128,1024]{1,0:T(8,128)(2,1)} %queries.1, s32[8,128]{1,0:T(8,128)} %bitcast.6, s32[1,48]{1,0:T(1,128)} %shortlist.1, s32[128]{0:T(128)} %owner_map.1), custom_call_target="tpu_custom_call" | custom-call | tf_op jit(solution)/shard_map/pack/pallas_call | solution.py:43
  2.4 2.9 %collective-permute-start = (bf16[136,1024]{1,0:T(8,128)(2,1)}, bf16[136,1024]{1,0:T(8,128)(2,1)S(1)}, u32[]{:S(2)}, u32[]{:S(2)}) collective-permute-start(bf16[136,1024]{1,0:T(8,128)(2,1)} %pack.1.refs_1_), channel_id=1, source_target_pairs={{0,2},{2,0},{4,6},{6,4},{1,3},{3,1},{5,7},{7,5},{8,10},{10,8},{12,... | collective-permute-start | bytes 835592 | tf_op jit(solution)/shard_map/ppermute | solution.py:228
  5.3 1.5 %collective-permute-start.1 = (bf16[136,1024]{1,0:T(8,128)(2,1)}, bf16[136,1024]{1,0:T(8,128)(2,1)S(1)}, u32[]{:S(2)}, u32[]{:S(2)}) collective-permute-start(bf16[136,1024]{1,0:T(8,128)(2,1)} %pack.1.refs_1_), channel_id=1, source_target_pairs={{0,4},{2,6},{4,0},{6,2},{1,5},{3,7},{5,1},{7,3},{8,12},{10,14},{12... | collective-permute-start | bytes 835592 | tf_op jit(solution)/shard_map/ppermute | solution.py:228
  6.8 1.6 %collective-permute-start.5 = (bf16[136,1024]{1,0:T(8,128)(2,1)}, bf16[136,1024]{1,0:T(8,128)(2,1)S(1)}, u32[]{:S(2)}, u32[]{:S(2)}) collective-permute-start(bf16[136,1024]{1,0:T(8,128)(2,1)} %pack.1.refs_1_), channel_id=1, source_target_pairs={{0,8},{8,24},{24,16},{16,0},{1,9},{9,25},{25,17},{17,1},{2,10},{10... | collective-permute-start | bytes 835592 | tf_op jit(solution)/shard_map/ppermute | solution.py:274
  8.5 3.4 %copy-done = bf16[32,128,1024]{2,1,0:T(8,128)(2,1)S(1)} copy-done((bf16[32,128,1024]{2,1,0:T(8,128)(2,1)S(1)}, bf16[32,128,1024]{2,1,0:T(8,128)(2,1)}, u32[]{:S(2)}) %copy-start) | copy-done | bytes 8388632
  11.9 0.7 %copy-done.3 = f32[32,128]{1,0:T(8,128)S(1)} copy-done((f32[32,128]{1,0:T(8,128)S(1)}, f32[32,128]{1,0:T(8,128)}, u32[]{:S(2)}) %copy-start.3) | copy-done | bytes 16408
  12.6 0.8 %prepare.1 = (bf16[512,1024]{1,0:T(8,128)(2,1)S(1)}, bf16[512,1024]{1,0:T(8,128)(2,1)S(1)}, f32[512,128]{1,0:T(8,128)S(1)}, f32[512,128]{1,0:T(8,128)S(1)}) custom-call(s32[3]{0:T(128)S(1)} %pad_add_fusion.where, bf16[32,128,1024]{2,1,0:T(8,128)(2,1)S(1)} %copy-done, f32[32,128]{1,0:T(8,128)S(1)} %copy-done.3), custom_call_target="tpu_custom_call" | custom-call | flops 1 | bytes 134217728 | tf_op jit(solution)/shard_map/prepare/pallas_call | solution.py:71
  13.6 1.5 %collective-permute-start.2 = (bf16[136,1024]{1,0:T(8,128)(2,1)}, bf16[136,1024]{1,0:T(8,128)(2,1)S(1)}, u32[]{:S(2)}, u32[]{:S(2)}) collective-permute-start(bf16[136,1024]{1,0:T(8,128)(2,1)} %pack.1.refs_1_), channel_id=1, source_target_pairs={{0,6},{2,4},{4,2},{6,0},{1,7},{3,5},{5,3},{7,1},{8,14},{10,12},{12... | collective-permute-start | bytes 835592 | tf_op jit(solution)/shard_map/ppermute | solution.py:228
  15.1 0.7 %collective-permute-done.5 = bf16[136,1024]{1,0:T(8,128)(2,1)S(1)} collective-permute-done((bf16[136,1024]{1,0:T(8,128)(2,1)}, bf16[136,1024]{1,0:T(8,128)(2,1)S(1)}, u32[]{:S(2)}, u32[]{:S(2)}) %collective-permute-start.5) | collective-permute-done | bytes 278560 | tf_op jit(solution)/shard_map/ppermute | solution.py:274
  15.8 0.7 %collective-permute-start.6 = (bf16[136,1024]{1,0:T(8,128)(2,1)S(1)}, bf16[136,1024]{1,0:T(8,128)(2,1)S(1)}, u32[]{:S(2)}, u32[]{:S(2)}) collective-permute-start(bf16[136,1024]{1,0:T(8,128)(2,1)S(1)} %collective-permute-done.5), channel_id=1, source_target_pairs={{0,0},{8,16},{16,8},{24,24},{1,1},{9,17},{17,9},{25,25},{2,2},{10,... | collective-permute-start | bytes 835592 | tf_op jit(solution)/shard_map/ppermute | solution.py:287
  16.5 3.8 %collective-permute-start.7 = (bf16[136,1024]{1,0:T(8,128)(2,1)S(1)}, bf16[136,1024]{1,0:T(8,128)(2,1)S(1)}, u32[]{:S(2)}, u32[]{:S(2)}) collective-permute-start(bf16[136,1024]{1,0:T(8,128)(2,1)S(1)} %collective-permute-done.5), channel_id=1, source_target_pairs={{0,8},{8,24},{24,16},{16,0},{1,9},{9,25},{25,17},{17,1},{2,10},{10... | collective-permute-start | bytes 835592 | tf_op jit(solution)/shard_map/ppermute | solution.py:283
  20.2 5.0 %owner_side.2 = (bf16[128,1024]{1,0:T(8,128)(2,1)S(1)}, bf16[128,1024]{1,0:T(8,128)(2,1)S(1)}) custom-call(s32[1]{0:T(128)} %bitcast.base, bf16[136,1024]{1,0:T(8,128)(2,1)S(1)} %collective-permute-done.refs_0_, bf16[136,1024]{1,0:T(8,128)(2,1)S(1)} %collective-permute-done.1.refs_1_, bf16[32,128,1024]{2,1,0:T(8,128)(2,1)S(1)} %copy-done.1, ...), custom_call_target="tpu_custom_call" | custom-call | flops 1 | bytes 1 | tf_op jit(solution)/shard_map/owner_side/pallas_call | solution.py:139
  25.3 0.5 collective-permute-start.15
  25.8 0.5 collective-permute-start.4
  26.3 1.1 %collective-permute-start.3 = (bf16[128,1024]{1,0:T(8,128)(2,1)S(1)}, bf16[128,1024]{1,0:T(8,128)(2,1)S(1)}, u32[]{:S(2)}, u32[]{:S(2)}) collective-permute-start(bf16[128,1024]{1,0:T(8,128)(2,1)S(1)} %get-tuple-element.38), channel_id=1, source_target_pairs={{0,2},{2,0},{4,6},{6,4},{1,3},{3,1},{5,7},{7,5},{8,10},{10,8},{12,... | collective-permute-start | bytes 786440 | tf_op jit(solution)/shard_map/ppermute | solution.py:228
  27.5 5.0 %owner_side.3 = (bf16[128,1024]{1,0:T(8,128)(2,1)S(1)}, f32[128,1024]{1,0:T(8,128)S(1)}) custom-call(s32[1]{0:T(128)} %bitcast.base, bf16[136,1024]{1,0:T(8,128)(2,1)S(1)} %collective-permute-done.2.refs_0_, bf16[136,1024]{1,0:T(8,128)(2,1)S(1)} %copy-done.2, bf16[32,128,1024]{2,1,0:T(8,128)(2,1)S(1)} %copy-done.1, f32[32,128]{1,0:T(8,128)S(1)} %copy-done.4), custom_call_target="tpu_custom_call" | custom-call | flops 1 | bytes 1 | tf_op jit(solution)/shard_map/owner_side/pallas_call | solution.py:139
  32.9 1.4 %collective-permute-start.8 = (bf16[272,1024]{1,0:T(8,128)(2,1)S(1)}, bf16[272,1024]{1,0:T(8,128)(2,1)S(1)}, u32[]{:S(2)}, u32[]{:S(2)}) collective-permute-start(bf16[272,1024]{1,0:T(8,128)(2,1)S(1)} %pad_maximum_fusion.1.refs_1_), channel_id=1, source_target_pairs={{0,2},{2,0},{4,6},{6,4},{1,3},{3,1},{5,7},{7,5},{8,10},{10,8},{12,... | collective-permute-start | bytes 1671176 | tf_op jit(solution)/shard_map/ppermute | solution.py:228
  34.3 1.5 %collective-permute-start.9 = (bf16[272,1024]{1,0:T(8,128)(2,1)S(1)}, bf16[272,1024]{1,0:T(8,128)(2,1)S(1)}, u32[]{:S(2)}, u32[]{:S(2)}) collective-permute-start(bf16[272,1024]{1,0:T(8,128)(2,1)S(1)} %pad_maximum_fusion.1.refs_1_), channel_id=1, source_target_pairs={{0,4},{2,6},{4,0},{6,2},{1,5},{3,7},{5,1},{7,3},{8,12},{10,14},{12... | collective-permute-start | bytes 1671176 | tf_op jit(solution)/shard_map/ppermute | solution.py:228
  35.9 4.6 %label_side.5 = (f32[512,1024]{1,0:T(8,128)S(1)}, f32[512,1024]{1,0:T(8,128)S(1)}) custom-call(s32[3]{0:T(128)S(1)} %pad_add_fusion.where, bf16[544,1024]{1,0:T(8,128)(2,1)S(1)} %pad_maximum_fusion.refs_0_, bf16[272,1024]{1,0:T(8,128)(2,1)S(1)} %pad_maximum_fusion.1.refs_1_, bf16[512,1024]{1,0:T(8,128)(2,1)S(1)} %get-tuple-element.29.refs_2_.refs_1_, ...), custom_call_target="tpu_custom_call" | custom-call | flops 1 | bytes 1 | tf_op jit(solution)/shard_map/label_side/pallas_call | solution.py:213
  40.5 4.2 %collective-permute-done.8.refs_0_ = bf16[272,1024]{1,0:T(8,128)(2,1)S(1)} collective-permute-done((bf16[272,1024]{1,0:T(8,128)(2,1)S(1)}, bf16[272,1024]{1,0:T(8,128)(2,1)S(1)}, u32[]{:S(2)}, u32[]{:S(2)}) %collective-permute-start.8) | collective-permute-done | bytes 557088 | tf_op jit(solution)/shard_map/ppermute | solution.py:228
  44.7 1.6 %collective-permute-done.9.refs_1_ = bf16[272,1024]{1,0:T(8,128)(2,1)S(1)} collective-permute-done((bf16[272,1024]{1,0:T(8,128)(2,1)S(1)}, bf16[272,1024]{1,0:T(8,128)(2,1)S(1)}, u32[]{:S(2)}, u32[]{:S(2)}) %collective-permute-start.9) | collective-permute-done | bytes 557088 | tf_op jit(solution)/shard_map/ppermute | solution.py:228
  46.2 1.5 %collective-permute-start.13 = (bf16[136,1024]{1,0:T(8,128)(2,1)S(1)}, bf16[136,1024]{1,0:T(8,128)(2,1)S(1)}, u32[]{:S(2)}, u32[]{:S(2)}) collective-permute-start(bf16[136,1024]{1,0:T(8,128)(2,1)S(1)} %slice.9), channel_id=1, source_target_pairs={{0,4},{2,6},{4,0},{6,2},{1,5},{3,7},{5,1},{7,3},{8,12},{10,14},{12... | collective-permute-start | bytes 835592 | tf_op jit(solution)/shard_map/ppermute | solution.py:228
  47.8 1.6 %collective-permute-start.11 = (bf16[136,1024]{1,0:T(8,128)(2,1)S(1)}, bf16[136,1024]{1,0:T(8,128)(2,1)S(1)}, u32[]{:S(2)}, u32[]{:S(2)}) collective-permute-start(bf16[136,1024]{1,0:T(8,128)(2,1)S(1)} %slice.8), channel_id=1, source_target_pairs={{0,2},{2,0},{4,6},{6,4},{1,3},{3,1},{5,7},{7,5},{8,10},{10,8},{12,... | collective-permute-start | bytes 835592 | tf_op jit(solution)/shard_map/ppermute | solution.py:228
  49.3 0.5 collective-permute-start.10
  49.9 3.6 %label_side.6 = (f32[512,1024]{1,0:T(8,128)S(1)}, f32[512,1024]{1,0:T(8,128)S(1)}) custom-call(s32[3]{0:T(128)S(1)} %pad_add_fusion.where, bf16[272,1024]{1,0:T(8,128)(2,1)S(1)} %collective-permute-done.8.refs_0_, bf16[272,1024]{1,0:T(8,128)(2,1)S(1)} %collective-permute-done.9.refs_1_, bf16[512,1024]{1,0:T(8,128)(2,1)S(1)} %get-tuple-element.29.refs_2_.refs_1_, ...), custom_call_target="tpu_custom_call" | custom-call | flops 1 | bytes 1 | tf_op jit(solution)/shard_map/label_side/pallas_call | solution.py:213
  53.5 0.8 %collective-permute-done.15.refs_0_ = bf16[544,1024]{1,0:T(8,128)(2,1)S(1)} collective-permute-done((bf16[544,1024]{1,0:T(8,128)(2,1)S(1)}, bf16[544,1024]{1,0:T(8,128)(2,1)S(1)}, u32[]{:S(2)}, u32[]{:S(2)}) %collective-permute-start.15) | collective-permute-done | bytes 1114144 | tf_op jit(solution)/shard_map/ppermute | solution.py:291
  54.2 2.1 %label_side.7 = bf16[512,1024]{1,0:T(8,128)(2,1)S(1)} custom-call(s32[2]{0:T(128)S(1)} %pad_add_fusion.2.where, bf16[544,1024]{1,0:T(8,128)(2,1)S(1)} %collective-permute-done.15.refs_0_, bf16[512,1024]{1,0:T(8,128)(2,1)S(1)} %get-tuple-element.29.refs_2_.refs_1_, f32[512,128]{1,0:T(8,128)S(1)} %get-tuple-element.31.refs_4_.refs_2_, ...), custom_call_target="tpu_custom_call" | custom-call | flops 1 | bytes 1 | tf_op jit(solution)/shard_map/label_side/pallas_call | solution.py:213
  56.4 0.8 %collective-permute-done.10 = bf16[128,1024]{1,0:T(8,128)(2,1)S(1)} collective-permute-done((bf16[128,1024]{1,0:T(8,128)(2,1)S(1)}, bf16[128,1024]{1,0:T(8,128)(2,1)S(1)}, u32[]{:S(2)}, u32[]{:S(2)}) %collective-permute-start.10) | collective-permute-done | bytes 262176 | tf_op jit(solution)/shard_map/ppermute | solution.py:228
  57.2 0.5 collective-permute-start.14
  57.9 0.9 %convert_add_fusion = f32[128,1024]{1,0:T(8,128)} fusion(bf16[128,1024]{1,0:T(8,128)(2,1)S(1)} %collective-permute-done.10, bf16[128,1024]{1,0:T(8,128)(2,1)S(1)} %collective-permute-done.4, f32[128,1024]{1,0:T(8,128)S(1)} %get-tuple-element.37, bf16[128,1024]{1,0:T(8,128)(2,1)S(1)} %collective-permute-done.3), kind=kLoop, calls=%fused_computation.2 | loop fusion | flops 786432 | bytes 1835008 | tf_op jit(solution)/shard_map/add | solution.py:322
  58.8 2.1 %label_side.8.refs_6_ = f32[512,1024]{1,0:T(8,128)S(1)} custom-call(s32[2]{0:T(128)S(1)} %pad_add_fusion.1.where, bf16[544,1024]{1,0:T(8,128)(2,1)S(1)} %collective-permute-done.15.refs_0_, bf16[512,1024]{1,0:T(8,128)(2,1)S(1)} %get-tuple-element.30.refs_3_.refs_1_.refs_4_, f32[512,128]{1,0:T(8,128)S(1)} %get-tuple-element.32.refs_5_.refs_2_, ...), custom_call_target="tpu_custom_call" | custom-call | flops 1 | bytes 1 | tf_op jit(solution)/shard_map/label_side/pallas_call | solution.py:213
  61.0 3.1 %label_side.9 = f32[512,1024]{1,0:T(8,128)} custom-call(s32[2]{0:T(128)S(1)} %pad_add_fusion.1.where, bf16[136,1024]{1,0:T(8,128)(2,1)S(1)} %collective-permute-done.11.refs_0_, bf16[136,1024]{1,0:T(8,128)(2,1)S(1)} %collective-permute-done.12.refs_1_, bf16[136,1024]{1,0:T(8,128)(2,1)S(1)} %collective-permute-done.13.refs_2_, ...), custom_call_target="tpu_custom_call" | custom-call | flops 1 | bytes 1 | tf_op jit(solution)/shard_map/label_side/pallas_call | solution.py:213
  (29 shorter events, 1.1 us)
Async XLA Ops:
  2.4 11.0 %collective-permute-start = (bf16[136,1024]{1,0:T(8,128)(2,1)}, bf16[136,1024]{1,0:T(8,128)(2,1)S(1)}, u32[]{:S(2)}, u32[]{:S(2)}) collective-permute-start(bf16[136,1024]{1,0:T(8,128)(2,1)} %pack.1.refs_1_), channel_id=1, source_target_pairs={{0,2},{2,0},{4,6},{6,4},{1,3},{3,1},{5,7},{7,5},{8,10},{10,8},{12,... | collective-permute-start | bytes 835592 | tf_op jit(solution)/shard_map/ppermute | solution.py:228
  5.3 8.3 %collective-permute-start.1 = (bf16[136,1024]{1,0:T(8,128)(2,1)}, bf16[136,1024]{1,0:T(8,128)(2,1)S(1)}, u32[]{:S(2)}, u32[]{:S(2)}) collective-permute-start(bf16[136,1024]{1,0:T(8,128)(2,1)} %pack.1.refs_1_), channel_id=1, source_target_pairs={{0,4},{2,6},{4,0},{6,2},{1,5},{3,7},{5,1},{7,3},{8,12},{10,14},{12... | collective-permute-start | bytes 835592 | tf_op jit(solution)/shard_map/ppermute | solution.py:228
  6.8 9.0 %collective-permute-start.5 = (bf16[136,1024]{1,0:T(8,128)(2,1)}, bf16[136,1024]{1,0:T(8,128)(2,1)S(1)}, u32[]{:S(2)}, u32[]{:S(2)}) collective-permute-start(bf16[136,1024]{1,0:T(8,128)(2,1)} %pack.1.refs_1_), channel_id=1, source_target_pairs={{0,8},{8,24},{24,16},{16,0},{1,9},{9,25},{25,17},{17,1},{2,10},{10... | collective-permute-start | bytes 835592 | tf_op jit(solution)/shard_map/ppermute | solution.py:274
  8.5 3.4 %copy-start = (bf16[32,128,1024]{2,1,0:T(8,128)(2,1)S(1)}, bf16[32,128,1024]{2,1,0:T(8,128)(2,1)}, u32[]{:S(2)}) copy-start(bf16[32,128,1024]{2,1,0:T(8,128)(2,1)} %refs_2_.3) | copy-start | bytes 25165828
  11.8 0.7 %copy-start.3 = (f32[32,128]{1,0:T(8,128)S(1)}, f32[32,128]{1,0:T(8,128)}, u32[]{:S(2)}) copy-start(f32[32,128]{1,0:T(8,128)} %refs_3_.3) | copy-start | bytes 49156
  12.6 7.7 %copy-start.1 = (bf16[32,128,1024]{2,1,0:T(8,128)(2,1)S(1)}, bf16[32,128,1024]{2,1,0:T(8,128)(2,1)}, u32[]{:S(2)}) copy-start(bf16[32,128,1024]{2,1,0:T(8,128)(2,1)} %refs_2_.3) | copy-start | bytes 25165828
  13.6 11.6 %copy-start.2 = (bf16[136,1024]{1,0:T(8,128)(2,1)S(1)}, bf16[136,1024]{1,0:T(8,128)(2,1)}, u32[]{:S(2)}) copy-start(bf16[136,1024]{1,0:T(8,128)(2,1)} %pack.1.refs_1_) | copy-start | bytes 835588
  13.6 11.6 %collective-permute-start.2 = (bf16[136,1024]{1,0:T(8,128)(2,1)}, bf16[136,1024]{1,0:T(8,128)(2,1)S(1)}, u32[]{:S(2)}, u32[]{:S(2)}) collective-permute-start(bf16[136,1024]{1,0:T(8,128)(2,1)} %pack.1.refs_1_), channel_id=1, source_target_pairs={{0,6},{2,4},{4,2},{6,0},{1,7},{3,5},{5,3},{7,1},{8,14},{10,12},{12... | collective-permute-start | bytes 835592 | tf_op jit(solution)/shard_map/ppermute | solution.py:228
  15.8 16.7 %collective-permute-start.6 = (bf16[136,1024]{1,0:T(8,128)(2,1)S(1)}, bf16[136,1024]{1,0:T(8,128)(2,1)S(1)}, u32[]{:S(2)}, u32[]{:S(2)}) collective-permute-start(bf16[136,1024]{1,0:T(8,128)(2,1)S(1)} %collective-permute-done.5), channel_id=1, source_target_pairs={{0,0},{8,16},{16,8},{24,24},{1,1},{9,17},{17,9},{25,25},{2,2},{10,... | collective-permute-start | bytes 835592 | tf_op jit(solution)/shard_map/ppermute | solution.py:287
  16.5 16.0 %collective-permute-start.7 = (bf16[136,1024]{1,0:T(8,128)(2,1)S(1)}, bf16[136,1024]{1,0:T(8,128)(2,1)S(1)}, u32[]{:S(2)}, u32[]{:S(2)}) collective-permute-start(bf16[136,1024]{1,0:T(8,128)(2,1)S(1)} %collective-permute-done.5), channel_id=1, source_target_pairs={{0,8},{8,24},{24,16},{16,0},{1,9},{9,25},{25,17},{17,1},{2,10},{10... | collective-permute-start | bytes 835592 | tf_op jit(solution)/shard_map/ppermute | solution.py:283
  25.2 2.3 %copy-start.4 = (f32[32,128]{1,0:T(8,128)S(1)}, f32[32,128]{1,0:T(8,128)}, u32[]{:S(2)}) copy-start(f32[32,128]{1,0:T(8,128)} %refs_3_.3) | copy-start | bytes 49156
  25.3 28.9 %collective-permute-start.15 = (bf16[544,1024]{1,0:T(8,128)(2,1)S(1)}, bf16[544,1024]{1,0:T(8,128)(2,1)S(1)}, u32[]{:S(2)}, u32[]{:S(2)}) collective-permute-start(bf16[544,1024]{1,0:T(8,128)(2,1)S(1)} %pad_maximum_fusion.refs_0_), channel_id=1, source_target_pairs={{0,8},{8,0},{16,24},{24,16},{1,9},{9,1},{17,25},{25,17},{2,10},{10... | collective-permute-start | bytes 3342344 | tf_op jit(solution)/shard_map/ppermute | solution.py:291
  25.8 6.7 %collective-permute-start.4 = (bf16[128,1024]{1,0:T(8,128)(2,1)S(1)}, bf16[128,1024]{1,0:T(8,128)(2,1)S(1)}, u32[]{:S(2)}, u32[]{:S(2)}) collective-permute-start(bf16[128,1024]{1,0:T(8,128)(2,1)S(1)} %get-tuple-element.40), channel_id=1, source_target_pairs={{0,4},{2,6},{4,0},{6,2},{1,5},{3,7},{5,1},{7,3},{8,12},{10,14},{12... | collective-permute-start | bytes 786440 | tf_op jit(solution)/shard_map/ppermute | solution.py:228
  26.3 6.6 %collective-permute-start.3 = (bf16[128,1024]{1,0:T(8,128)(2,1)S(1)}, bf16[128,1024]{1,0:T(8,128)(2,1)S(1)}, u32[]{:S(2)}, u32[]{:S(2)}) collective-permute-start(bf16[128,1024]{1,0:T(8,128)(2,1)S(1)} %get-tuple-element.38), channel_id=1, source_target_pairs={{0,2},{2,0},{4,6},{6,4},{1,3},{3,1},{5,7},{7,5},{8,10},{10,8},{12,... | collective-permute-start | bytes 786440 | tf_op jit(solution)/shard_map/ppermute | solution.py:228
  32.9 11.8 %collective-permute-start.8 = (bf16[272,1024]{1,0:T(8,128)(2,1)S(1)}, bf16[272,1024]{1,0:T(8,128)(2,1)S(1)}, u32[]{:S(2)}, u32[]{:S(2)}) collective-permute-start(bf16[272,1024]{1,0:T(8,128)(2,1)S(1)} %pad_maximum_fusion.1.refs_1_), channel_id=1, source_target_pairs={{0,2},{2,0},{4,6},{6,4},{1,3},{3,1},{5,7},{7,5},{8,10},{10,8},{12,... | collective-permute-start | bytes 1671176 | tf_op jit(solution)/shard_map/ppermute | solution.py:228
  34.3 11.9 %collective-permute-start.9 = (bf16[272,1024]{1,0:T(8,128)(2,1)S(1)}, bf16[272,1024]{1,0:T(8,128)(2,1)S(1)}, u32[]{:S(2)}, u32[]{:S(2)}) collective-permute-start(bf16[272,1024]{1,0:T(8,128)(2,1)S(1)} %pad_maximum_fusion.1.refs_1_), channel_id=1, source_target_pairs={{0,4},{2,6},{4,0},{6,2},{1,5},{3,7},{5,1},{7,3},{8,12},{10,14},{12... | collective-permute-start | bytes 1671176 | tf_op jit(solution)/shard_map/ppermute | solution.py:228
  46.2 11.0 %collective-permute-start.13 = (bf16[136,1024]{1,0:T(8,128)(2,1)S(1)}, bf16[136,1024]{1,0:T(8,128)(2,1)S(1)}, u32[]{:S(2)}, u32[]{:S(2)}) collective-permute-start(bf16[136,1024]{1,0:T(8,128)(2,1)S(1)} %slice.9), channel_id=1, source_target_pairs={{0,4},{2,6},{4,0},{6,2},{1,5},{3,7},{5,1},{7,3},{8,12},{10,14},{12... | collective-permute-start | bytes 835592 | tf_op jit(solution)/shard_map/ppermute | solution.py:228
  47.8 9.4 %collective-permute-start.11 = (bf16[136,1024]{1,0:T(8,128)(2,1)S(1)}, bf16[136,1024]{1,0:T(8,128)(2,1)S(1)}, u32[]{:S(2)}, u32[]{:S(2)}) collective-permute-start(bf16[136,1024]{1,0:T(8,128)(2,1)S(1)} %slice.8), channel_id=1, source_target_pairs={{0,2},{2,0},{4,6},{6,4},{1,3},{3,1},{5,7},{7,5},{8,10},{10,8},{12,... | collective-permute-start | bytes 835592 | tf_op jit(solution)/shard_map/ppermute | solution.py:228
  49.3 7.9 %collective-permute-start.10 = (bf16[128,1024]{1,0:T(8,128)(2,1)S(1)}, bf16[128,1024]{1,0:T(8,128)(2,1)S(1)}, u32[]{:S(2)}, u32[]{:S(2)}) collective-permute-start(bf16[128,1024]{1,0:T(8,128)(2,1)S(1)} %get-tuple-element.47), channel_id=1, source_target_pairs={{0,6},{2,4},{4,2},{6,0},{1,7},{3,5},{5,3},{7,1},{8,14},{10,12},{12... | collective-permute-start | bytes 786440 | tf_op jit(solution)/shard_map/ppermute | solution.py:228
  57.2 3.8 %collective-permute-start.16 = (bf16[512,1024]{1,0:T(8,128)(2,1)S(1)}, bf16[512,1024]{1,0:T(8,128)(2,1)S(1)}, u32[]{:S(2)}, u32[]{:S(2)}) collective-permute-start(bf16[512,1024]{1,0:T(8,128)(2,1)S(1)} %label_side.7), channel_id=1, source_target_pairs={{0,1},{1,0},{2,3},{3,2},{4,5},{5,4},{6,7},{7,6},{8,9},{9,8},{10,11... | collective-permute-start | bytes 3145736 | tf_op jit(solution)/shard_map/ppermute | solution.py:228
  57.2 3.7 %collective-permute-start.14 = (bf16[136,1024]{1,0:T(8,128)(2,1)S(1)}, bf16[136,1024]{1,0:T(8,128)(2,1)S(1)}, u32[]{:S(2)}, u32[]{:S(2)}) collective-permute-start(bf16[136,1024]{1,0:T(8,128)(2,1)S(1)} %collective-permute-done.13.refs_2_), channel_id=1, source_target_pairs={{0,1},{1,0},{2,3},{3,2},{4,5},{5,4},{6,7},{7,6},{8,9},{9,8},{10,11... | collective-permute-start | bytes 835592 | tf_op jit(solution)/shard_map/ppermute | solution.py:228
  57.7 3.2 %collective-permute-start.12 = (bf16[136,1024]{1,0:T(8,128)(2,1)S(1)}, bf16[136,1024]{1,0:T(8,128)(2,1)S(1)}, u32[]{:S(2)}, u32[]{:S(2)}) collective-permute-start(bf16[136,1024]{1,0:T(8,128)(2,1)S(1)} %collective-permute-done.11.refs_0_), channel_id=1, source_target_pairs={{0,1},{1,0},{2,3},{3,2},{4,5},{5,4},{6,7},{7,6},{8,9},{9,8},{10,11... | collective-permute-start | bytes 835592 | tf_op jit(solution)/shard_map/ppermute | solution.py:228

commit v6 on v5

--- a/solution.py
+++ b/solution.py
@@ -277,7 +277,7 @@
         here[k] = swap(packed, "label", k)
     gate = [here[k] for k in first] + [column] + list(ws) + list(invs)
     for k in second[:-1]:
-        here[k] = swap(after(packed, *[x for x in gate if x is not column]), "label", k)
+        here[k] = swap(after(packed, *ws, *invs), "label", k)
     columns = [column]
     for _ in range(dp_count - 3):
         columns.append(lax.ppermute(after(columns[-1], *gate), "dp", forward))
@@ -298,8 +298,8 @@
     gate = total[0] + spread
     cut = columns.shape[0] // (rows + extra) // 2 * (rows + extra)
     corners = [
-        swap(after(spread[1][:cut], *gate), "label", bits[0]),
-        swap(after(spread[0][cut:], *gate), "label", bits[1]),
+        swap(after(spread[1][:cut], *total[0]), "label", bits[0]),
+        swap(after(spread[0][cut:], *total[0]), "label", bits[1]),
     ]
     for k in second[:-1]:
         back[k] = swap(after(parts[k], *gate), "label", k)
@@ -312,9 +312,9 @@
     theirs = []
     if sections == 2:
         theirs = [label_call([next_plane], total[:1], kinds=[bf16])[0][0]]
-    mine = label_call([next_plane], total[-1:], *theirs)
+    mine = label_call([next_plane], total[-1:], *theirs, *back.values())
     if sections == 2:
-        mine = [mine[0] + [swap(after(theirs[0], *corners, *back.values()), "section", 1)]]
+        mine = [mine[0] + [jnp.concatenate([swap(x, "section", 1) for x in jnp.split(after(theirs[0], *corners), 2)], axis=0)]]
         corners = sum([[x, swap(x, "section", 1)] for x in corners], [])
     total = label_call(corners, mine, pieces=2 if blocks * each % 32 == 0 else 1)
     query_grad = parts[0]

time: 64.5 us -> 64.2 us (level)
    ppermute x1, waiting for transfers between devices: 0.66 us -> 1.84 us  [per_device(): column = lax.ppermute(packed, 'dp', forward)]
    ppermute x13 -> x14, waiting for transfers between devices: 7.18 us -> 6.21 us  [swap(): return lax.ppermute(x, axis, [(i, i ^ bit) for i in range(size)])]
    ppermute x13 -> x14, starting transfers between devices: 14.7 us -> 14.2 us  [swap(): return lax.ppermute(x, axis, [(i, i ^ bit) for i in range(size)])]
  transfers between devices with their start and end apart: 17 -> 18, of which waited for: 7 -> 5; matrix products, arithmetic and copies ran while one was open for 2% -> 2% of each run, Pallas kernels for 36% -> 36%
where the time goes in v6:
time: 64.2 us; the launch traced here: 64 us
  Pallas kernels  28 us (44%)
  starting transfers between devices  20.7 us (32%)
  waiting for transfers between devices  8.69 us (14%)
  local copies, waits for them, and re-layouts  4.22 us (7%)
  other arithmetic  1.34 us (2%)
  between operations  1.01 us (2%)
    pallas_call x5, Pallas kernels, b_call(): pl.pallas_call(functools.partial(b_body, n, sides, pair, len(more) // sid...  15.5 us
    ppermute x14, starting transfers between devices, swap(): return lax.ppermute(x, axis, [(i, i ^ bit) for i in range(size)])  14.2 us
    pallas_call x2, Pallas kernels, a_call(): pl.pallas_call(functools.partial(a_body, n, group), out_shape=out_types,...  9.95 us
    ppermute x14, waiting for transfers between devices, swap(): return lax.ppermute(x, axis, [(i, i ^ bit) for i in range(size)])  6.21 us
    unnamed x10, local copies, waits for them, and re-layouts  4.12 us
    ppermute x1, starting transfers between devices, per_device(): columns.append(lax.ppermute(after(columns[-1], *gate), 'dp', forward))  3.52 us
    ppermute x1, waiting for transfers between devices, per_device(): column = lax.ppermute(packed, 'dp', forward)  1.84 us
    pallas_call x1, Pallas kernels, pack(): pl.pallas_call(pack_body, out_shape=jax.ShapeDtypeStruct((rows + positive...  1.72 us
  transfers between devices with their start and end apart: 18, of which 5 were waited for; matrix products, arithmetic and copies ran while one was open for 2% of the time, Pallas kernels for 36%

profile of v6, /device:TPU:0, one launch (start us, length us, event | category | flops | bytes accessed | tf_op | source)
XLA Modules:
  0.0 64.0 jit_solution(1933987156120881392)
XLA Ops:
  0.6 1.7 %pack.1.refs_1_ = bf16[136,1024]{1,0:T(8,128)(2,1)} custom-call(bf16[128,1024]{1,0:T(8,128)(2,1)} %queries.1, s32[8,128]{1,0:T(8,128)} %bitcast.6, s32[1,48]{1,0:T(1,128)} %shortlist.1, s32[128]{0:T(128)} %owner_map.1), custom_call_target="tpu_custom_call" | custom-call | tf_op jit(solution)/shard_map/pack/pallas_call | solution.py:43
  2.4 2.9 %collective-permute-start = (bf16[136,1024]{1,0:T(8,128)(2,1)}, bf16[136,1024]{1,0:T(8,128)(2,1)S(1)}, u32[]{:S(2)}, u32[]{:S(2)}) collective-permute-start(bf16[136,1024]{1,0:T(8,128)(2,1)} %pack.1.refs_1_), channel_id=1, source_target_pairs={{0,2},{2,0},{4,6},{6,4},{1,3},{3,1},{5,7},{7,5},{8,10},{10,8},{12,... | collective-permute-start | bytes 835592 | tf_op jit(solution)/shard_map/ppermute | solution.py:228
  5.3 1.5 %collective-permute-start.1 = (bf16[136,1024]{1,0:T(8,128)(2,1)}, bf16[136,1024]{1,0:T(8,128)(2,1)S(1)}, u32[]{:S(2)}, u32[]{:S(2)}) collective-permute-start(bf16[136,1024]{1,0:T(8,128)(2,1)} %pack.1.refs_1_), channel_id=1, source_target_pairs={{0,4},{2,6},{4,0},{6,2},{1,5},{3,7},{5,1},{7,3},{8,12},{10,14},{12... | collective-permute-start | bytes 835592 | tf_op jit(solution)/shard_map/ppermute | solution.py:228
  6.8 1.6 %collective-permute-start.5 = (bf16[136,1024]{1,0:T(8,128)(2,1)}, bf16[136,1024]{1,0:T(8,128)(2,1)S(1)}, u32[]{:S(2)}, u32[]{:S(2)}) collective-permute-start(bf16[136,1024]{1,0:T(8,128)(2,1)} %pack.1.refs_1_), channel_id=1, source_target_pairs={{0,8},{8,24},{24,16},{16,0},{1,9},{9,25},{25,17},{17,1},{2,10},{10... | collective-permute-start | bytes 835592 | tf_op jit(solution)/shard_map/ppermute | solution.py:274
  8.5 3.4 %copy-done = bf16[32,128,1024]{2,1,0:T(8,128)(2,1)S(1)} copy-done((bf16[32,128,1024]{2,1,0:T(8,128)(2,1)S(1)}, bf16[32,128,1024]{2,1,0:T(8,128)(2,1)}, u32[]{:S(2)}) %copy-start) | copy-done | bytes 8388632
  11.9 0.7 %copy-done.3 = f32[32,128]{1,0:T(8,128)S(1)} copy-done((f32[32,128]{1,0:T(8,128)S(1)}, f32[32,128]{1,0:T(8,128)}, u32[]{:S(2)}) %copy-start.3) | copy-done | bytes 16408
  12.6 0.8 %prepare.1 = (bf16[512,1024]{1,0:T(8,128)(2,1)S(1)}, bf16[512,1024]{1,0:T(8,128)(2,1)S(1)}, f32[512,128]{1,0:T(8,128)S(1)}, f32[512,128]{1,0:T(8,128)S(1)}) custom-call(s32[3]{0:T(128)S(1)} %pad_add_fusion.where, bf16[32,128,1024]{2,1,0:T(8,128)(2,1)S(1)} %copy-done, f32[32,128]{1,0:T(8,128)S(1)} %copy-done.3), custom_call_target="tpu_custom_call" | custom-call | flops 1 | bytes 134217728 | tf_op jit(solution)/shard_map/prepare/pallas_call | solution.py:71
  13.4 0.5 collective-permute-start.2
  13.9 1.8 %collective-permute-done.5 = bf16[136,1024]{1,0:T(8,128)(2,1)S(1)} collective-permute-done((bf16[136,1024]{1,0:T(8,128)(2,1)}, bf16[136,1024]{1,0:T(8,128)(2,1)S(1)}, u32[]{:S(2)}, u32[]{:S(2)}) %collective-permute-start.5) | collective-permute-done | bytes 278560 | tf_op jit(solution)/shard_map/ppermute | solution.py:274
  15.8 0.7 %collective-permute-start.6 = (bf16[136,1024]{1,0:T(8,128)(2,1)S(1)}, bf16[136,1024]{1,0:T(8,128)(2,1)S(1)}, u32[]{:S(2)}, u32[]{:S(2)}) collective-permute-start(bf16[136,1024]{1,0:T(8,128)(2,1)S(1)} %collective-permute-done.5), channel_id=1, source_target_pairs={{0,0},{8,16},{16,8},{24,24},{1,1},{9,17},{17,9},{25,25},{2,2},{10,... | collective-permute-start | bytes 835592 | tf_op jit(solution)/shard_map/ppermute | solution.py:287
  16.5 3.5 %collective-permute-start.7 = (bf16[136,1024]{1,0:T(8,128)(2,1)S(1)}, bf16[136,1024]{1,0:T(8,128)(2,1)S(1)}, u32[]{:S(2)}, u32[]{:S(2)}) collective-permute-start(bf16[136,1024]{1,0:T(8,128)(2,1)S(1)} %collective-permute-done.5), channel_id=1, source_target_pairs={{0,8},{8,24},{24,16},{16,0},{1,9},{9,25},{25,17},{17,1},{2,10},{10... | collective-permute-start | bytes 835592 | tf_op jit(solution)/shard_map/ppermute | solution.py:283
  20.0 5.0 %owner_side.2 = (bf16[128,1024]{1,0:T(8,128)(2,1)S(1)}, bf16[128,1024]{1,0:T(8,128)(2,1)S(1)}) custom-call(s32[1]{0:T(128)} %bitcast.base, bf16[136,1024]{1,0:T(8,128)(2,1)S(1)} %collective-permute-done.refs_0_, bf16[136,1024]{1,0:T(8,128)(2,1)S(1)} %collective-permute-done.1.refs_1_, bf16[32,128,1024]{2,1,0:T(8,128)(2,1)S(1)} %copy-done.1, ...), custom_call_target="tpu_custom_call" | custom-call | flops 1 | bytes 1 | tf_op jit(solution)/shard_map/owner_side/pallas_call | solution.py:139
  25.1 0.7 %collective-permute-start.15 = (bf16[544,1024]{1,0:T(8,128)(2,1)S(1)}, bf16[544,1024]{1,0:T(8,128)(2,1)S(1)}, u32[]{:S(2)}, u32[]{:S(2)}) collective-permute-start(bf16[544,1024]{1,0:T(8,128)(2,1)S(1)} %pad_maximum_fusion.refs_0_), channel_id=1, source_target_pairs={{0,8},{8,0},{16,24},{24,16},{1,9},{9,1},{17,25},{25,17},{2,10},{10... | collective-permute-start | bytes 3342344 | tf_op jit(solution)/shard_map/ppermute | solution.py:291
  25.8 0.5 collective-permute-start.4
  26.3 0.5 collective-permute-start.3
  26.9 5.0 %owner_side.3 = (bf16[128,1024]{1,0:T(8,128)(2,1)S(1)}, f32[128,1024]{1,0:T(8,128)S(1)}) custom-call(s32[1]{0:T(128)} %bitcast.base, bf16[136,1024]{1,0:T(8,128)(2,1)S(1)} %collective-permute-done.2.refs_0_, bf16[136,1024]{1,0:T(8,128)(2,1)S(1)} %copy-done.2, bf16[32,128,1024]{2,1,0:T(8,128)(2,1)S(1)} %copy-done.1, f32[32,128]{1,0:T(8,128)S(1)} %copy-done.4), custom_call_target="tpu_custom_call" | custom-call | flops 1 | bytes 1 | tf_op jit(solution)/shard_map/owner_side/pallas_call | solution.py:139
  32.2 0.8 %collective-permute-done.3 = bf16[128,1024]{1,0:T(8,128)(2,1)S(1)} collective-permute-done((bf16[128,1024]{1,0:T(8,128)(2,1)S(1)}, bf16[128,1024]{1,0:T(8,128)(2,1)S(1)}, u32[]{:S(2)}, u32[]{:S(2)}) %collective-permute-start.3) | collective-permute-done | bytes 262176 | tf_op jit(solution)/shard_map/ppermute | solution.py:228
  33.0 0.5 collective-permute-start.8
  33.5 1.5 %collective-permute-start.9 = (bf16[272,1024]{1,0:T(8,128)(2,1)S(1)}, bf16[272,1024]{1,0:T(8,128)(2,1)S(1)}, u32[]{:S(2)}, u32[]{:S(2)}) collective-permute-start(bf16[272,1024]{1,0:T(8,128)(2,1)S(1)} %pad_maximum_fusion.2.refs_1_), channel_id=1, source_target_pairs={{0,4},{2,6},{4,0},{6,2},{1,5},{3,7},{5,1},{7,3},{8,12},{10,14},{12... | collective-permute-start | bytes 1671176 | tf_op jit(solution)/shard_map/ppermute | solution.py:228
  35.0 4.6 %label_side.5 = (f32[512,1024]{1,0:T(8,128)S(1)}, f32[512,1024]{1,0:T(8,128)S(1)}) custom-call(s32[3]{0:T(128)S(1)} %pad_add_fusion.where, bf16[544,1024]{1,0:T(8,128)(2,1)S(1)} %pad_maximum_fusion.refs_0_, bf16[272,1024]{1,0:T(8,128)(2,1)S(1)} %pad_maximum_fusion.2.refs_1_, bf16[512,1024]{1,0:T(8,128)(2,1)S(1)} %get-tuple-element.29.refs_2_.refs_1_, ...), custom_call_target="tpu_custom_call" | custom-call | flops 1 | bytes 1 | tf_op jit(solution)/shard_map/label_side/pallas_call | solution.py:213
  39.6 5.1 %collective-permute-done.8.refs_0_ = bf16[272,1024]{1,0:T(8,128)(2,1)S(1)} collective-permute-done((bf16[272,1024]{1,0:T(8,128)(2,1)S(1)}, bf16[272,1024]{1,0:T(8,128)(2,1)S(1)}, u32[]{:S(2)}, u32[]{:S(2)}) %collective-permute-start.8) | collective-permute-done | bytes 557088 | tf_op jit(solution)/shard_map/ppermute | solution.py:228
  44.8 2.2 %collective-permute-start.13 = (bf16[136,1024]{1,0:T(8,128)(2,1)S(1)}, bf16[136,1024]{1,0:T(8,128)(2,1)S(1)}, u32[]{:S(2)}, u32[]{:S(2)}) collective-permute-start(bf16[136,1024]{1,0:T(8,128)(2,1)S(1)} %slice.9), channel_id=1, source_target_pairs={{0,4},{2,6},{4,0},{6,2},{1,5},{3,7},{5,1},{7,3},{8,12},{10,14},{12... | collective-permute-start | bytes 835592 | tf_op jit(solution)/shard_map/ppermute | solution.py:228
  47.0 0.9 %collective-permute-start.11 = (bf16[136,1024]{1,0:T(8,128)(2,1)S(1)}, bf16[136,1024]{1,0:T(8,128)(2,1)S(1)}, u32[]{:S(2)}, u32[]{:S(2)}) collective-permute-start(bf16[136,1024]{1,0:T(8,128)(2,1)S(1)} %slice.8), channel_id=1, source_target_pairs={{0,2},{2,0},{4,6},{6,4},{1,3},{3,1},{5,7},{7,5},{8,10},{10,8},{12,... | collective-permute-start | bytes 835592 | tf_op jit(solution)/shard_map/ppermute | solution.py:228
  48.0 1.9 %collective-permute-start.10 = (bf16[128,1024]{1,0:T(8,128)(2,1)S(1)}, bf16[128,1024]{1,0:T(8,128)(2,1)S(1)}, u32[]{:S(2)}, u32[]{:S(2)}) collective-permute-start(bf16[128,1024]{1,0:T(8,128)(2,1)S(1)} %get-tuple-element.47), channel_id=1, source_target_pairs={{0,6},{2,4},{4,2},{6,0},{1,7},{3,5},{5,3},{7,1},{8,14},{10,12},{12... | collective-permute-start | bytes 786440 | tf_op jit(solution)/shard_map/ppermute | solution.py:228
  49.9 3.6 %label_side.6 = (f32[512,1024]{1,0:T(8,128)S(1)}, f32[512,1024]{1,0:T(8,128)S(1)}) custom-call(s32[3]{0:T(128)S(1)} %pad_add_fusion.where, bf16[272,1024]{1,0:T(8,128)(2,1)S(1)} %collective-permute-done.8.refs_0_, bf16[272,1024]{1,0:T(8,128)(2,1)S(1)} %collective-permute-done.9.refs_1_, bf16[512,1024]{1,0:T(8,128)(2,1)S(1)} %get-tuple-element.29.refs_2_.refs_1_, ...), custom_call_target="tpu_custom_call" | custom-call | flops 1 | bytes 1 | tf_op jit(solution)/shard_map/label_side/pallas_call | solution.py:213
  53.5 0.6 collective-permute-done.15.refs_0_
  54.1 2.1 %label_side.7 = bf16[512,1024]{1,0:T(8,128)(2,1)S(1)} custom-call(s32[2]{0:T(128)S(1)} %pad_add_fusion.2.where, bf16[544,1024]{1,0:T(8,128)(2,1)S(1)} %collective-permute-done.15.refs_0_, bf16[512,1024]{1,0:T(8,128)(2,1)S(1)} %get-tuple-element.29.refs_2_.refs_1_, f32[512,128]{1,0:T(8,128)S(1)} %get-tuple-element.31.refs_4_.refs_2_, ...), custom_call_target="tpu_custom_call" | custom-call | flops 1 | bytes 1 | tf_op jit(solution)/shard_map/label_side/pallas_call | solution.py:213
  56.4 0.5 collective-permute-start.17
  57.1 0.4 collective-permute-start.12
  57.5 0.9 %convert_add_fusion = f32[128,1024]{1,0:T(8,128)} fusion(bf16[128,1024]{1,0:T(8,128)(2,1)S(1)} %collective-permute-done.10, bf16[128,1024]{1,0:T(8,128)(2,1)S(1)} %collective-permute-done.4, f32[128,1024]{1,0:T(8,128)S(1)} %get-tuple-element.37, bf16[128,1024]{1,0:T(8,128)(2,1)S(1)} %collective-permute-done.3), kind=kLoop, calls=%fused_computation.3 | loop fusion | flops 786432 | bytes 1835008 | tf_op jit(solution)/shard_map/add | solution.py:322
  58.4 2.1 %label_side.8.refs_6_ = f32[512,1024]{1,0:T(8,128)S(1)} custom-call(s32[2]{0:T(128)S(1)} %pad_add_fusion.1.where, bf16[544,1024]{1,0:T(8,128)(2,1)S(1)} %collective-permute-done.15.refs_0_, bf16[512,1024]{1,0:T(8,128)(2,1)S(1)} %get-tuple-element.30.refs_3_.refs_1_.refs_4_, f32[512,128]{1,0:T(8,128)S(1)} %get-tuple-element.32.refs_5_.refs_2_, ...), custom_call_target="tpu_custom_call" | custom-call | flops 1 | bytes 1 | tf_op jit(solution)/shard_map/label_side/pallas_call | solution.py:213
  60.7 3.1 %label_side.9 = f32[512,1024]{1,0:T(8,128)} custom-call(s32[2]{0:T(128)S(1)} %pad_add_fusion.1.where, bf16[136,1024]{1,0:T(8,128)(2,1)S(1)} %collective-permute-done.11.refs_0_, bf16[136,1024]{1,0:T(8,128)(2,1)S(1)} %collective-permute-done.12.refs_1_, bf16[136,1024]{1,0:T(8,128)(2,1)S(1)} %collective-permute-done.13.refs_2_, ...), custom_call_target="tpu_custom_call" | custom-call | flops 1 | bytes 1 | tf_op jit(solution)/shard_map/label_side/pallas_call | solution.py:213
  (33 shorter events, 1.0 us)
Async XLA Ops:
  2.4 11.6 %collective-permute-start = (bf16[136,1024]{1,0:T(8,128)(2,1)}, bf16[136,1024]{1,0:T(8,128)(2,1)S(1)}, u32[]{:S(2)}, u32[]{:S(2)}) collective-permute-start(bf16[136,1024]{1,0:T(8,128)(2,1)} %pack.1.refs_1_), channel_id=1, source_target_pairs={{0,2},{2,0},{4,6},{6,4},{1,3},{3,1},{5,7},{7,5},{8,10},{10,8},{12,... | collective-permute-start | bytes 835592 | tf_op jit(solution)/shard_map/ppermute | solution.py:228
  5.3 8.6 %collective-permute-start.1 = (bf16[136,1024]{1,0:T(8,128)(2,1)}, bf16[136,1024]{1,0:T(8,128)(2,1)S(1)}, u32[]{:S(2)}, u32[]{:S(2)}) collective-permute-start(bf16[136,1024]{1,0:T(8,128)(2,1)} %pack.1.refs_1_), channel_id=1, source_target_pairs={{0,4},{2,6},{4,0},{6,2},{1,5},{3,7},{5,1},{7,3},{8,12},{10,14},{12... | collective-permute-start | bytes 835592 | tf_op jit(solution)/shard_map/ppermute | solution.py:228
  6.8 9.0 %collective-permute-start.5 = (bf16[136,1024]{1,0:T(8,128)(2,1)}, bf16[136,1024]{1,0:T(8,128)(2,1)S(1)}, u32[]{:S(2)}, u32[]{:S(2)}) collective-permute-start(bf16[136,1024]{1,0:T(8,128)(2,1)} %pack.1.refs_1_), channel_id=1, source_target_pairs={{0,8},{8,24},{24,16},{16,0},{1,9},{9,25},{25,17},{17,1},{2,10},{10... | collective-permute-start | bytes 835592 | tf_op jit(solution)/shard_map/ppermute | solution.py:274
  8.5 3.4 %copy-start = (bf16[32,128,1024]{2,1,0:T(8,128)(2,1)S(1)}, bf16[32,128,1024]{2,1,0:T(8,128)(2,1)}, u32[]{:S(2)}) copy-start(bf16[32,128,1024]{2,1,0:T(8,128)(2,1)} %refs_2_.3) | copy-start | bytes 25165828
  11.8 0.7 %copy-start.3 = (f32[32,128]{1,0:T(8,128)S(1)}, f32[32,128]{1,0:T(8,128)}, u32[]{:S(2)}) copy-start(f32[32,128]{1,0:T(8,128)} %refs_3_.3) | copy-start | bytes 49156
  12.6 7.4 %copy-start.1 = (bf16[32,128,1024]{2,1,0:T(8,128)(2,1)S(1)}, bf16[32,128,1024]{2,1,0:T(8,128)(2,1)}, u32[]{:S(2)}) copy-start(bf16[32,128,1024]{2,1,0:T(8,128)(2,1)} %refs_2_.3) | copy-start | bytes 25165828
  13.4 11.6 %copy-start.2 = (bf16[136,1024]{1,0:T(8,128)(2,1)S(1)}, bf16[136,1024]{1,0:T(8,128)(2,1)}, u32[]{:S(2)}) copy-start(bf16[136,1024]{1,0:T(8,128)(2,1)} %pack.1.refs_1_) | copy-start | bytes 835588
  13.4 11.6 %collective-permute-start.2 = (bf16[136,1024]{1,0:T(8,128)(2,1)}, bf16[136,1024]{1,0:T(8,128)(2,1)S(1)}, u32[]{:S(2)}, u32[]{:S(2)}) collective-permute-start(bf16[136,1024]{1,0:T(8,128)(2,1)} %pack.1.refs_1_), channel_id=1, source_target_pairs={{0,6},{2,4},{4,2},{6,0},{1,7},{3,5},{5,3},{7,1},{8,14},{10,12},{12... | collective-permute-start | bytes 835592 | tf_op jit(solution)/shard_map/ppermute | solution.py:228
  15.8 16.1 %collective-permute-start.6 = (bf16[136,1024]{1,0:T(8,128)(2,1)S(1)}, bf16[136,1024]{1,0:T(8,128)(2,1)S(1)}, u32[]{:S(2)}, u32[]{:S(2)}) collective-permute-start(bf16[136,1024]{1,0:T(8,128)(2,1)S(1)} %collective-permute-done.5), channel_id=1, source_target_pairs={{0,0},{8,16},{16,8},{24,24},{1,1},{9,17},{17,9},{25,25},{2,2},{10,... | collective-permute-start | bytes 835592 | tf_op jit(solution)/shard_map/ppermute | solution.py:287
  16.5 15.4 %collective-permute-start.7 = (bf16[136,1024]{1,0:T(8,128)(2,1)S(1)}, bf16[136,1024]{1,0:T(8,128)(2,1)S(1)}, u32[]{:S(2)}, u32[]{:S(2)}) collective-permute-start(bf16[136,1024]{1,0:T(8,128)(2,1)S(1)} %collective-permute-done.5), channel_id=1, source_target_pairs={{0,8},{8,24},{24,16},{16,0},{1,9},{9,25},{25,17},{17,1},{2,10},{10... | collective-permute-start | bytes 835592 | tf_op jit(solution)/shard_map/ppermute | solution.py:283
  25.0 1.9 %copy-start.4 = (f32[32,128]{1,0:T(8,128)S(1)}, f32[32,128]{1,0:T(8,128)}, u32[]{:S(2)}) copy-start(f32[32,128]{1,0:T(8,128)} %refs_3_.3) | copy-start | bytes 49156
  25.1 29.0 %collective-permute-start.15 = (bf16[544,1024]{1,0:T(8,128)(2,1)S(1)}, bf16[544,1024]{1,0:T(8,128)(2,1)S(1)}, u32[]{:S(2)}, u32[]{:S(2)}) collective-permute-start(bf16[544,1024]{1,0:T(8,128)(2,1)S(1)} %pad_maximum_fusion.refs_0_), channel_id=1, source_target_pairs={{0,8},{8,0},{16,24},{24,16},{1,9},{9,1},{17,25},{25,17},{2,10},{10... | collective-permute-start | bytes 3342344 | tf_op jit(solution)/shard_map/ppermute | solution.py:291
  25.8 6.4 %collective-permute-start.4 = (bf16[128,1024]{1,0:T(8,128)(2,1)S(1)}, bf16[128,1024]{1,0:T(8,128)(2,1)S(1)}, u32[]{:S(2)}, u32[]{:S(2)}) collective-permute-start(bf16[128,1024]{1,0:T(8,128)(2,1)S(1)} %get-tuple-element.40), channel_id=1, source_target_pairs={{0,4},{2,6},{4,0},{6,2},{1,5},{3,7},{5,1},{7,3},{8,12},{10,14},{12... | collective-permute-start | bytes 786440 | tf_op jit(solution)/shard_map/ppermute | solution.py:228
  26.3 6.6 %collective-permute-start.3 = (bf16[128,1024]{1,0:T(8,128)(2,1)S(1)}, bf16[128,1024]{1,0:T(8,128)(2,1)S(1)}, u32[]{:S(2)}, u32[]{:S(2)}) collective-permute-start(bf16[128,1024]{1,0:T(8,128)(2,1)S(1)} %get-tuple-element.38), channel_id=1, source_target_pairs={{0,2},{2,0},{4,6},{6,4},{1,3},{3,1},{5,7},{7,5},{8,10},{10,8},{12,... | collective-permute-start | bytes 786440 | tf_op jit(solution)/shard_map/ppermute | solution.py:228
  33.0 11.8 %collective-permute-start.8 = (bf16[272,1024]{1,0:T(8,128)(2,1)S(1)}, bf16[272,1024]{1,0:T(8,128)(2,1)S(1)}, u32[]{:S(2)}, u32[]{:S(2)}) collective-permute-start(bf16[272,1024]{1,0:T(8,128)(2,1)S(1)} %pad_maximum_fusion.2.refs_1_), channel_id=1, source_target_pairs={{0,2},{2,0},{4,6},{6,4},{1,3},{3,1},{5,7},{7,5},{8,10},{10,8},{12,... | collective-permute-start | bytes 1671176 | tf_op jit(solution)/shard_map/ppermute | solution.py:228
  33.5 13.5 %collective-permute-start.9 = (bf16[272,1024]{1,0:T(8,128)(2,1)S(1)}, bf16[272,1024]{1,0:T(8,128)(2,1)S(1)}, u32[]{:S(2)}, u32[]{:S(2)}) collective-permute-start(bf16[272,1024]{1,0:T(8,128)(2,1)S(1)} %pad_maximum_fusion.2.refs_1_), channel_id=1, source_target_pairs={{0,4},{2,6},{4,0},{6,2},{1,5},{3,7},{5,1},{7,3},{8,12},{10,14},{12... | collective-permute-start | bytes 1671176 | tf_op jit(solution)/shard_map/ppermute | solution.py:228
  44.8 11.5 %collective-permute-start.13 = (bf16[136,1024]{1,0:T(8,128)(2,1)S(1)}, bf16[136,1024]{1,0:T(8,128)(2,1)S(1)}, u32[]{:S(2)}, u32[]{:S(2)}) collective-permute-start(bf16[136,1024]{1,0:T(8,128)(2,1)S(1)} %slice.9), channel_id=1, source_target_pairs={{0,4},{2,6},{4,0},{6,2},{1,5},{3,7},{5,1},{7,3},{8,12},{10,14},{12... | collective-permute-start | bytes 835592 | tf_op jit(solution)/shard_map/ppermute | solution.py:228
  47.0 9.3 %collective-permute-start.11 = (bf16[136,1024]{1,0:T(8,128)(2,1)S(1)}, bf16[136,1024]{1,0:T(8,128)(2,1)S(1)}, u32[]{:S(2)}, u32[]{:S(2)}) collective-permute-start(bf16[136,1024]{1,0:T(8,128)(2,1)S(1)} %slice.8), channel_id=1, source_target_pairs={{0,2},{2,0},{4,6},{6,4},{1,3},{3,1},{5,7},{7,5},{8,10},{10,8},{12,... | collective-permute-start | bytes 835592 | tf_op jit(solution)/shard_map/ppermute | solution.py:228
  48.0 9.5 %collective-permute-start.10 = (bf16[128,1024]{1,0:T(8,128)(2,1)S(1)}, bf16[128,1024]{1,0:T(8,128)(2,1)S(1)}, u32[]{:S(2)}, u32[]{:S(2)}) collective-permute-start(bf16[128,1024]{1,0:T(8,128)(2,1)S(1)} %get-tuple-element.47), channel_id=1, source_target_pairs={{0,6},{2,4},{4,2},{6,0},{1,7},{3,5},{5,3},{7,1},{8,14},{10,12},{12... | collective-permute-start | bytes 786440 | tf_op jit(solution)/shard_map/ppermute | solution.py:228
  56.3 4.2 %collective-permute-start.16 = (bf16[256,1024]{1,0:T(8,128)(2,1)S(1)}, bf16[256,1024]{1,0:T(8,128)(2,1)S(1)}, u32[]{:S(2)}, u32[]{:S(2)}) collective-permute-start(bf16[256,1024]{1,0:T(8,128)(2,1)S(1)} %get-tuple-element.56), channel_id=1, source_target_pairs={{0,1},{1,0},{2,3},{3,2},{4,5},{5,4},{6,7},{7,6},{8,9},{9,8},{10,11... | collective-permute-start | bytes 1572872 | tf_op jit(solution)/shard_map/ppermute | solution.py:228
  56.4 4.2 %collective-permute-start.17 = (bf16[256,1024]{1,0:T(8,128)(2,1)S(1)}, bf16[256,1024]{1,0:T(8,128)(2,1)S(1)}, u32[]{:S(2)}, u32[]{:S(2)}) collective-permute-start(bf16[256,1024]{1,0:T(8,128)(2,1)S(1)} %get-tuple-element.57), channel_id=1, source_target_pairs={{0,1},{1,0},{2,3},{3,2},{4,5},{5,4},{6,7},{7,6},{8,9},{9,8},{10,11... | collective-permute-start | bytes 1572872 | tf_op jit(solution)/shard_map/ppermute | solution.py:228
  57.0 3.7 %collective-permute-start.14 = (bf16[136,1024]{1,0:T(8,128)(2,1)S(1)}, bf16[136,1024]{1,0:T(8,128)(2,1)S(1)}, u32[]{:S(2)}, u32[]{:S(2)}) collective-permute-start(bf16[136,1024]{1,0:T(8,128)(2,1)S(1)} %collective-permute-done.13.refs_2_), channel_id=1, source_target_pairs={{0,1},{1,0},{2,3},{3,2},{4,5},{5,4},{6,7},{7,6},{8,9},{9,8},{10,11... | collective-permute-start | bytes 835592 | tf_op jit(solution)/shard_map/ppermute | solution.py:228
  57.1 3.6 %collective-permute-start.12 = (bf16[136,1024]{1,0:T(8,128)(2,1)S(1)}, bf16[136,1024]{1,0:T(8,128)(2,1)S(1)}, u32[]{:S(2)}, u32[]{:S(2)}) collective-permute-start(bf16[136,1024]{1,0:T(8,128)(2,1)S(1)} %collective-permute-done.11.refs_0_), channel_id=1, source_target_pairs={{0,1},{1,0},{2,3},{3,2},{4,5},{5,4},{6,7},{7,6},{8,9},{9,8},{10,11... | collective-permute-start | bytes 835592 | tf_op jit(solution)/shard_map/ppermute | solution.py:228

commit v7 on v6

--- a/solution.py
+++ b/solution.py
@@ -202,7 +202,7 @@
             copy.wait()
 
 
-def b_call(xs, ws, invs, where, blocks, rows, extra, before, kinds, pieces=1, pair=2):
+def b_call(xs, ws, invs, where, blocks, rows, extra, before, kinds, pieces=1, pair=4):
     n, sides = len(xs), len(ws)
     count = sum(x.shape[0] for x in xs) // (rows + extra)
     pair = min(pair, count)

time: 64.2 us -> 64.2 us (level)
  no operation moved by 1% of the time
where the time goes in v7:
time: 64.2 us; the launch traced here: 64 us
  Pallas kernels  28 us (44%)
  starting transfers between devices  20.7 us (32%)
  waiting for transfers between devices  8.68 us (14%)
  local copies, waits for them, and re-layouts  4.22 us (7%)
  other arithmetic  1.34 us (2%)
  between operations  1.01 us (2%)
    pallas_call x5, Pallas kernels, b_call(): pl.pallas_call(functools.partial(b_body, n, sides, pair, len(more) // sid...  15.5 us
    ppermute x14, starting transfers between devices, swap(): return lax.ppermute(x, axis, [(i, i ^ bit) for i in range(size)])  14.2 us
    pallas_call x2, Pallas kernels, a_call(): pl.pallas_call(functools.partial(a_body, n, group), out_shape=out_types,...  9.95 us
    ppermute x14, waiting for transfers between devices, swap(): return lax.ppermute(x, axis, [(i, i ^ bit) for i in range(size)])  6.2 us
    unnamed x10, local copies, waits for them, and re-layouts  4.12 us
    ppermute x1, starting transfers between devices, per_device(): columns.append(lax.ppermute(after(columns[-1], *gate), 'dp', forward))  3.52 us
    ppermute x1, waiting for transfers between devices, per_device(): column = lax.ppermute(packed, 'dp', forward)  1.84 us
    pallas_call x1, Pallas kernels, pack(): pl.pallas_call(pack_body, out_shape=jax.ShapeDtypeStruct((rows + positive...  1.72 us
  transfers between devices with their start and end apart: 18, of which 5 were waited for; matrix products, arithmetic and copies ran while one was open for 2% of the time, Pallas kernels for 36%

profile of v7, /device:TPU:0, one launch (start us, length us, event | category | flops | bytes accessed | tf_op | source)
XLA Modules:
  0.0 64.0 jit_solution(17542794228049455652)
XLA Ops:
  0.6 1.7 %pack.1.refs_1_ = bf16[136,1024]{1,0:T(8,128)(2,1)} custom-call(bf16[128,1024]{1,0:T(8,128)(2,1)} %queries.1, s32[8,128]{1,0:T(8,128)} %bitcast.6, s32[1,48]{1,0:T(1,128)} %shortlist.1, s32[128]{0:T(128)} %owner_map.1), custom_call_target="tpu_custom_call" | custom-call | tf_op jit(solution)/shard_map/pack/pallas_call | solution.py:43
  2.4 2.9 %collective-permute-start = (bf16[136,1024]{1,0:T(8,128)(2,1)}, bf16[136,1024]{1,0:T(8,128)(2,1)S(1)}, u32[]{:S(2)}, u32[]{:S(2)}) collective-permute-start(bf16[136,1024]{1,0:T(8,128)(2,1)} %pack.1.refs_1_), channel_id=1, source_target_pairs={{0,2},{2,0},{4,6},{6,4},{1,3},{3,1},{5,7},{7,5},{8,10},{10,8},{12,... | collective-permute-start | bytes 835592 | tf_op jit(solution)/shard_map/ppermute | solution.py:228
  5.3 1.5 %collective-permute-start.1 = (bf16[136,1024]{1,0:T(8,128)(2,1)}, bf16[136,1024]{1,0:T(8,128)(2,1)S(1)}, u32[]{:S(2)}, u32[]{:S(2)}) collective-permute-start(bf16[136,1024]{1,0:T(8,128)(2,1)} %pack.1.refs_1_), channel_id=1, source_target_pairs={{0,4},{2,6},{4,0},{6,2},{1,5},{3,7},{5,1},{7,3},{8,12},{10,14},{12... | collective-permute-start | bytes 835592 | tf_op jit(solution)/shard_map/ppermute | solution.py:228
  6.8 1.6 %collective-permute-start.5 = (bf16[136,1024]{1,0:T(8,128)(2,1)}, bf16[136,1024]{1,0:T(8,128)(2,1)S(1)}, u32[]{:S(2)}, u32[]{:S(2)}) collective-permute-start(bf16[136,1024]{1,0:T(8,128)(2,1)} %pack.1.refs_1_), channel_id=1, source_target_pairs={{0,8},{8,24},{24,16},{16,0},{1,9},{9,25},{25,17},{17,1},{2,10},{10... | collective-permute-start | bytes 835592 | tf_op jit(solution)/shard_map/ppermute | solution.py:274
  8.5 3.4 %copy-done = bf16[32,128,1024]{2,1,0:T(8,128)(2,1)S(1)} copy-done((bf16[32,128,1024]{2,1,0:T(8,128)(2,1)S(1)}, bf16[32,128,1024]{2,1,0:T(8,128)(2,1)}, u32[]{:S(2)}) %copy-start) | copy-done | bytes 8388632
  11.9 0.7 %copy-done.3 = f32[32,128]{1,0:T(8,128)S(1)} copy-done((f32[32,128]{1,0:T(8,128)S(1)}, f32[32,128]{1,0:T(8,128)}, u32[]{:S(2)}) %copy-start.3) | copy-done | bytes 16408
  12.6 0.8 %prepare.1 = (bf16[512,1024]{1,0:T(8,128)(2,1)S(1)}, bf16[512,1024]{1,0:T(8,128)(2,1)S(1)}, f32[512,128]{1,0:T(8,128)S(1)}, f32[512,128]{1,0:T(8,128)S(1)}) custom-call(s32[3]{0:T(128)S(1)} %pad_add_fusion.where, bf16[32,128,1024]{2,1,0:T(8,128)(2,1)S(1)} %copy-done, f32[32,128]{1,0:T(8,128)S(1)} %copy-done.3), custom_call_target="tpu_custom_call" | custom-call | flops 1 | bytes 134217728 | tf_op jit(solution)/shard_map/prepare/pallas_call | solution.py:71
  13.4 0.5 collective-permute-start.2
  13.9 1.8 %collective-permute-done.5 = bf16[136,1024]{1,0:T(8,128)(2,1)S(1)} collective-permute-done((bf16[136,1024]{1,0:T(8,128)(2,1)}, bf16[136,1024]{1,0:T(8,128)(2,1)S(1)}, u32[]{:S(2)}, u32[]{:S(2)}) %collective-permute-start.5) | collective-permute-done | bytes 278560 | tf_op jit(solution)/shard_map/ppermute | solution.py:274
  15.8 0.7 %collective-permute-start.6 = (bf16[136,1024]{1,0:T(8,128)(2,1)S(1)}, bf16[136,1024]{1,0:T(8,128)(2,1)S(1)}, u32[]{:S(2)}, u32[]{:S(2)}) collective-permute-start(bf16[136,1024]{1,0:T(8,128)(2,1)S(1)} %collective-permute-done.5), channel_id=1, source_target_pairs={{0,0},{8,16},{16,8},{24,24},{1,1},{9,17},{17,9},{25,25},{2,2},{10,... | collective-permute-start | bytes 835592 | tf_op jit(solution)/shard_map/ppermute | solution.py:287
  16.5 3.5 %collective-permute-start.7 = (bf16[136,1024]{1,0:T(8,128)(2,1)S(1)}, bf16[136,1024]{1,0:T(8,128)(2,1)S(1)}, u32[]{:S(2)}, u32[]{:S(2)}) collective-permute-start(bf16[136,1024]{1,0:T(8,128)(2,1)S(1)} %collective-permute-done.5), channel_id=1, source_target_pairs={{0,8},{8,24},{24,16},{16,0},{1,9},{9,25},{25,17},{17,1},{2,10},{10... | collective-permute-start | bytes 835592 | tf_op jit(solution)/shard_map/ppermute | solution.py:283
  20.0 5.0 %owner_side.2 = (bf16[128,1024]{1,0:T(8,128)(2,1)S(1)}, bf16[128,1024]{1,0:T(8,128)(2,1)S(1)}) custom-call(s32[1]{0:T(128)} %bitcast.base, bf16[136,1024]{1,0:T(8,128)(2,1)S(1)} %collective-permute-done.refs_0_, bf16[136,1024]{1,0:T(8,128)(2,1)S(1)} %collective-permute-done.1.refs_1_, bf16[32,128,1024]{2,1,0:T(8,128)(2,1)S(1)} %copy-done.1, ...), custom_call_target="tpu_custom_call" | custom-call | flops 1 | bytes 1 | tf_op jit(solution)/shard_map/owner_side/pallas_call | solution.py:139
  25.1 0.7 %collective-permute-start.15 = (bf16[544,1024]{1,0:T(8,128)(2,1)S(1)}, bf16[544,1024]{1,0:T(8,128)(2,1)S(1)}, u32[]{:S(2)}, u32[]{:S(2)}) collective-permute-start(bf16[544,1024]{1,0:T(8,128)(2,1)S(1)} %pad_maximum_fusion.refs_0_), channel_id=1, source_target_pairs={{0,8},{8,0},{16,24},{24,16},{1,9},{9,1},{17,25},{25,17},{2,10},{10... | collective-permute-start | bytes 3342344 | tf_op jit(solution)/shard_map/ppermute | solution.py:291
  25.8 0.5 collective-permute-start.4
  26.3 0.5 collective-permute-start.3
  26.9 5.0 %owner_side.3 = (bf16[128,1024]{1,0:T(8,128)(2,1)S(1)}, f32[128,1024]{1,0:T(8,128)S(1)}) custom-call(s32[1]{0:T(128)} %bitcast.base, bf16[136,1024]{1,0:T(8,128)(2,1)S(1)} %collective-permute-done.2.refs_0_, bf16[136,1024]{1,0:T(8,128)(2,1)S(1)} %copy-done.2, bf16[32,128,1024]{2,1,0:T(8,128)(2,1)S(1)} %copy-done.1, f32[32,128]{1,0:T(8,128)S(1)} %copy-done.4), custom_call_target="tpu_custom_call" | custom-call | flops 1 | bytes 1 | tf_op jit(solution)/shard_map/owner_side/pallas_call | solution.py:139
  32.2 0.8 %collective-permute-done.3 = bf16[128,1024]{1,0:T(8,128)(2,1)S(1)} collective-permute-done((bf16[128,1024]{1,0:T(8,128)(2,1)S(1)}, bf16[128,1024]{1,0:T(8,128)(2,1)S(1)}, u32[]{:S(2)}, u32[]{:S(2)}) %collective-permute-start.3) | collective-permute-done | bytes 262176 | tf_op jit(solution)/shard_map/ppermute | solution.py:228
  33.0 0.5 collective-permute-start.8
  33.5 1.5 %collective-permute-start.9 = (bf16[272,1024]{1,0:T(8,128)(2,1)S(1)}, bf16[272,1024]{1,0:T(8,128)(2,1)S(1)}, u32[]{:S(2)}, u32[]{:S(2)}) collective-permute-start(bf16[272,1024]{1,0:T(8,128)(2,1)S(1)} %pad_maximum_fusion.2.refs_1_), channel_id=1, source_target_pairs={{0,4},{2,6},{4,0},{6,2},{1,5},{3,7},{5,1},{7,3},{8,12},{10,14},{12... | collective-permute-start | bytes 1671176 | tf_op jit(solution)/shard_map/ppermute | solution.py:228
  35.0 4.6 %label_side.5 = (f32[512,1024]{1,0:T(8,128)S(1)}, f32[512,1024]{1,0:T(8,128)S(1)}) custom-call(s32[3]{0:T(128)S(1)} %pad_add_fusion.where, bf16[544,1024]{1,0:T(8,128)(2,1)S(1)} %pad_maximum_fusion.refs_0_, bf16[272,1024]{1,0:T(8,128)(2,1)S(1)} %pad_maximum_fusion.2.refs_1_, bf16[512,1024]{1,0:T(8,128)(2,1)S(1)} %get-tuple-element.29.refs_2_.refs_1_, ...), custom_call_target="tpu_custom_call" | custom-call | flops 1 | bytes 1 | tf_op jit(solution)/shard_map/label_side/pallas_call | solution.py:213
  39.6 5.1 %collective-permute-done.8.refs_0_ = bf16[272,1024]{1,0:T(8,128)(2,1)S(1)} collective-permute-done((bf16[272,1024]{1,0:T(8,128)(2,1)S(1)}, bf16[272,1024]{1,0:T(8,128)(2,1)S(1)}, u32[]{:S(2)}, u32[]{:S(2)}) %collective-permute-start.8) | collective-permute-done | bytes 557088 | tf_op jit(solution)/shard_map/ppermute | solution.py:228
  44.8 2.2 %collective-permute-start.13 = (bf16[136,1024]{1,0:T(8,128)(2,1)S(1)}, bf16[136,1024]{1,0:T(8,128)(2,1)S(1)}, u32[]{:S(2)}, u32[]{:S(2)}) collective-permute-start(bf16[136,1024]{1,0:T(8,128)(2,1)S(1)} %slice.9), channel_id=1, source_target_pairs={{0,4},{2,6},{4,0},{6,2},{1,5},{3,7},{5,1},{7,3},{8,12},{10,14},{12... | collective-permute-start | bytes 835592 | tf_op jit(solution)/shard_map/ppermute | solution.py:228
  47.0 0.9 %collective-permute-start.11 = (bf16[136,1024]{1,0:T(8,128)(2,1)S(1)}, bf16[136,1024]{1,0:T(8,128)(2,1)S(1)}, u32[]{:S(2)}, u32[]{:S(2)}) collective-permute-start(bf16[136,1024]{1,0:T(8,128)(2,1)S(1)} %slice.8), channel_id=1, source_target_pairs={{0,2},{2,0},{4,6},{6,4},{1,3},{3,1},{5,7},{7,5},{8,10},{10,8},{12,... | collective-permute-start | bytes 835592 | tf_op jit(solution)/shard_map/ppermute | solution.py:228
  48.0 1.9 %collective-permute-start.10 = (bf16[128,1024]{1,0:T(8,128)(2,1)S(1)}, bf16[128,1024]{1,0:T(8,128)(2,1)S(1)}, u32[]{:S(2)}, u32[]{:S(2)}) collective-permute-start(bf16[128,1024]{1,0:T(8,128)(2,1)S(1)} %get-tuple-element.47), channel_id=1, source_target_pairs={{0,6},{2,4},{4,2},{6,0},{1,7},{3,5},{5,3},{7,1},{8,14},{10,12},{12... | collective-permute-start | bytes 786440 | tf_op jit(solution)/shard_map/ppermute | solution.py:228
  49.9 3.6 %label_side.6 = (f32[512,1024]{1,0:T(8,128)S(1)}, f32[512,1024]{1,0:T(8,128)S(1)}) custom-call(s32[3]{0:T(128)S(1)} %pad_add_fusion.where, bf16[272,1024]{1,0:T(8,128)(2,1)S(1)} %collective-permute-done.8.refs_0_, bf16[272,1024]{1,0:T(8,128)(2,1)S(1)} %collective-permute-done.9.refs_1_, bf16[512,1024]{1,0:T(8,128)(2,1)S(1)} %get-tuple-element.29.refs_2_.refs_1_, ...), custom_call_target="tpu_custom_call" | custom-call | flops 1 | bytes 1 | tf_op jit(solution)/shard_map/label_side/pallas_call | solution.py:213
  53.5 0.6 collective-permute-done.15.refs_0_
  54.1 2.1 %label_side.7 = bf16[512,1024]{1,0:T(8,128)(2,1)S(1)} custom-call(s32[2]{0:T(128)S(1)} %pad_add_fusion.2.where, bf16[544,1024]{1,0:T(8,128)(2,1)S(1)} %collective-permute-done.15.refs_0_, bf16[512,1024]{1,0:T(8,128)(2,1)S(1)} %get-tuple-element.29.refs_2_.refs_1_, f32[512,128]{1,0:T(8,128)S(1)} %get-tuple-element.31.refs_4_.refs_2_, ...), custom_call_target="tpu_custom_call" | custom-call | flops 1 | bytes 1 | tf_op jit(solution)/shard_map/label_side/pallas_call | solution.py:213
  56.4 0.5 collective-permute-start.17
  57.1 0.4 collective-permute-start.12
  57.5 0.9 %convert_add_fusion = f32[128,1024]{1,0:T(8,128)} fusion(bf16[128,1024]{1,0:T(8,128)(2,1)S(1)} %collective-permute-done.10, bf16[128,1024]{1,0:T(8,128)(2,1)S(1)} %collective-permute-done.4, f32[128,1024]{1,0:T(8,128)S(1)} %get-tuple-element.37, bf16[128,1024]{1,0:T(8,128)(2,1)S(1)} %collective-permute-done.3), kind=kLoop, calls=%fused_computation.3 | loop fusion | flops 786432 | bytes 1835008 | tf_op jit(solution)/shard_map/add | solution.py:322
  58.4 2.1 %label_side.8.refs_6_ = f32[512,1024]{1,0:T(8,128)S(1)} custom-call(s32[2]{0:T(128)S(1)} %pad_add_fusion.1.where, bf16[544,1024]{1,0:T(8,128)(2,1)S(1)} %collective-permute-done.15.refs_0_, bf16[512,1024]{1,0:T(8,128)(2,1)S(1)} %get-tuple-element.30.refs_3_.refs_1_.refs_4_, f32[512,128]{1,0:T(8,128)S(1)} %get-tuple-element.32.refs_5_.refs_2_, ...), custom_call_target="tpu_custom_call" | custom-call | flops 1 | bytes 1 | tf_op jit(solution)/shard_map/label_side/pallas_call | solution.py:213
  60.7 3.1 %label_side.9 = f32[512,1024]{1,0:T(8,128)} custom-call(s32[2]{0:T(128)S(1)} %pad_add_fusion.1.where, bf16[136,1024]{1,0:T(8,128)(2,1)S(1)} %collective-permute-done.11.refs_0_, bf16[136,1024]{1,0:T(8,128)(2,1)S(1)} %collective-permute-done.12.refs_1_, bf16[136,1024]{1,0:T(8,128)(2,1)S(1)} %collective-permute-done.13.refs_2_, ...), custom_call_target="tpu_custom_call" | custom-call | flops 1 | bytes 1 | tf_op jit(solution)/shard_map/label_side/pallas_call | solution.py:213
  (33 shorter events, 1.0 us)
Async XLA Ops:
  2.4 11.6 %collective-permute-start = (bf16[136,1024]{1,0:T(8,128)(2,1)}, bf16[136,1024]{1,0:T(8,128)(2,1)S(1)}, u32[]{:S(2)}, u32[]{:S(2)}) collective-permute-start(bf16[136,1024]{1,0:T(8,128)(2,1)} %pack.1.refs_1_), channel_id=1, source_target_pairs={{0,2},{2,0},{4,6},{6,4},{1,3},{3,1},{5,7},{7,5},{8,10},{10,8},{12,... | collective-permute-start | bytes 835592 | tf_op jit(solution)/shard_map/ppermute | solution.py:228
  5.3 8.6 %collective-permute-start.1 = (bf16[136,1024]{1,0:T(8,128)(2,1)}, bf16[136,1024]{1,0:T(8,128)(2,1)S(1)}, u32[]{:S(2)}, u32[]{:S(2)}) collective-permute-start(bf16[136,1024]{1,0:T(8,128)(2,1)} %pack.1.refs_1_), channel_id=1, source_target_pairs={{0,4},{2,6},{4,0},{6,2},{1,5},{3,7},{5,1},{7,3},{8,12},{10,14},{12... | collective-permute-start | bytes 835592 | tf_op jit(solution)/shard_map/ppermute | solution.py:228
  6.8 9.0 %collective-permute-start.5 = (bf16[136,1024]{1,0:T(8,128)(2,1)}, bf16[136,1024]{1,0:T(8,128)(2,1)S(1)}, u32[]{:S(2)}, u32[]{:S(2)}) collective-permute-start(bf16[136,1024]{1,0:T(8,128)(2,1)} %pack.1.refs_1_), channel_id=1, source_target_pairs={{0,8},{8,24},{24,16},{16,0},{1,9},{9,25},{25,17},{17,1},{2,10},{10... | collective-permute-start | bytes 835592 | tf_op jit(solution)/shard_map/ppermute | solution.py:274
  8.5 3.4 %copy-start = (bf16[32,128,1024]{2,1,0:T(8,128)(2,1)S(1)}, bf16[32,128,1024]{2,1,0:T(8,128)(2,1)}, u32[]{:S(2)}) copy-start(bf16[32,128,1024]{2,1,0:T(8,128)(2,1)} %refs_2_.3) | copy-start | bytes 25165828
  11.8 0.7 %copy-start.3 = (f32[32,128]{1,0:T(8,128)S(1)}, f32[32,128]{1,0:T(8,128)}, u32[]{:S(2)}) copy-start(f32[32,128]{1,0:T(8,128)} %refs_3_.3) | copy-start | bytes 49156
  12.6 7.4 %copy-start.1 = (bf16[32,128,1024]{2,1,0:T(8,128)(2,1)S(1)}, bf16[32,128,1024]{2,1,0:T(8,128)(2,1)}, u32[]{:S(2)}) copy-start(bf16[32,128,1024]{2,1,0:T(8,128)(2,1)} %refs_2_.3) | copy-start | bytes 25165828
  13.4 11.6 %copy-start.2 = (bf16[136,1024]{1,0:T(8,128)(2,1)S(1)}, bf16[136,1024]{1,0:T(8,128)(2,1)}, u32[]{:S(2)}) copy-start(bf16[136,1024]{1,0:T(8,128)(2,1)} %pack.1.refs_1_) | copy-start | bytes 835588
  13.4 11.6 %collective-permute-start.2 = (bf16[136,1024]{1,0:T(8,128)(2,1)}, bf16[136,1024]{1,0:T(8,128)(2,1)S(1)}, u32[]{:S(2)}, u32[]{:S(2)}) collective-permute-start(bf16[136,1024]{1,0:T(8,128)(2,1)} %pack.1.refs_1_), channel_id=1, source_target_pairs={{0,6},{2,4},{4,2},{6,0},{1,7},{3,5},{5,3},{7,1},{8,14},{10,12},{12... | collective-permute-start | bytes 835592 | tf_op jit(solution)/shard_map/ppermute | solution.py:228
  15.8 16.1 %collective-permute-start.6 = (bf16[136,1024]{1,0:T(8,128)(2,1)S(1)}, bf16[136,1024]{1,0:T(8,128)(2,1)S(1)}, u32[]{:S(2)}, u32[]{:S(2)}) collective-permute-start(bf16[136,1024]{1,0:T(8,128)(2,1)S(1)} %collective-permute-done.5), channel_id=1, source_target_pairs={{0,0},{8,16},{16,8},{24,24},{1,1},{9,17},{17,9},{25,25},{2,2},{10,... | collective-permute-start | bytes 835592 | tf_op jit(solution)/shard_map/ppermute | solution.py:287
  16.5 15.4 %collective-permute-start.7 = (bf16[136,1024]{1,0:T(8,128)(2,1)S(1)}, bf16[136,1024]{1,0:T(8,128)(2,1)S(1)}, u32[]{:S(2)}, u32[]{:S(2)}) collective-permute-start(bf16[136,1024]{1,0:T(8,128)(2,1)S(1)} %collective-permute-done.5), channel_id=1, source_target_pairs={{0,8},{8,24},{24,16},{16,0},{1,9},{9,25},{25,17},{17,1},{2,10},{10... | collective-permute-start | bytes 835592 | tf_op jit(solution)/shard_map/ppermute | solution.py:283
  25.0 1.9 %copy-start.4 = (f32[32,128]{1,0:T(8,128)S(1)}, f32[32,128]{1,0:T(8,128)}, u32[]{:S(2)}) copy-start(f32[32,128]{1,0:T(8,128)} %refs_3_.3) | copy-start | bytes 49156
  25.1 29.0 %collective-permute-start.15 = (bf16[544,1024]{1,0:T(8,128)(2,1)S(1)}, bf16[544,1024]{1,0:T(8,128)(2,1)S(1)}, u32[]{:S(2)}, u32[]{:S(2)}) collective-permute-start(bf16[544,1024]{1,0:T(8,128)(2,1)S(1)} %pad_maximum_fusion.refs_0_), channel_id=1, source_target_pairs={{0,8},{8,0},{16,24},{24,16},{1,9},{9,1},{17,25},{25,17},{2,10},{10... | collective-permute-start | bytes 3342344 | tf_op jit(solution)/shard_map/ppermute | solution.py:291
  25.8 6.4 %collective-permute-start.4 = (bf16[128,1024]{1,0:T(8,128)(2,1)S(1)}, bf16[128,1024]{1,0:T(8,128)(2,1)S(1)}, u32[]{:S(2)}, u32[]{:S(2)}) collective-permute-start(bf16[128,1024]{1,0:T(8,128)(2,1)S(1)} %get-tuple-element.40), channel_id=1, source_target_pairs={{0,4},{2,6},{4,0},{6,2},{1,5},{3,7},{5,1},{7,3},{8,12},{10,14},{12... | collective-permute-start | bytes 786440 | tf_op jit(solution)/shard_map/ppermute | solution.py:228
  26.3 6.6 %collective-permute-start.3 = (bf16[128,1024]{1,0:T(8,128)(2,1)S(1)}, bf16[128,1024]{1,0:T(8,128)(2,1)S(1)}, u32[]{:S(2)}, u32[]{:S(2)}) collective-permute-start(bf16[128,1024]{1,0:T(8,128)(2,1)S(1)} %get-tuple-element.38), channel_id=1, source_target_pairs={{0,2},{2,0},{4,6},{6,4},{1,3},{3,1},{5,7},{7,5},{8,10},{10,8},{12,... | collective-permute-start | bytes 786440 | tf_op jit(solution)/shard_map/ppermute | solution.py:228
  33.0 11.8 %collective-permute-start.8 = (bf16[272,1024]{1,0:T(8,128)(2,1)S(1)}, bf16[272,1024]{1,0:T(8,128)(2,1)S(1)}, u32[]{:S(2)}, u32[]{:S(2)}) collective-permute-start(bf16[272,1024]{1,0:T(8,128)(2,1)S(1)} %pad_maximum_fusion.2.refs_1_), channel_id=1, source_target_pairs={{0,2},{2,0},{4,6},{6,4},{1,3},{3,1},{5,7},{7,5},{8,10},{10,8},{12,... | collective-permute-start | bytes 1671176 | tf_op jit(solution)/shard_map/ppermute | solution.py:228
  33.5 13.5 %collective-permute-start.9 = (bf16[272,1024]{1,0:T(8,128)(2,1)S(1)}, bf16[272,1024]{1,0:T(8,128)(2,1)S(1)}, u32[]{:S(2)}, u32[]{:S(2)}) collective-permute-start(bf16[272,1024]{1,0:T(8,128)(2,1)S(1)} %pad_maximum_fusion.2.refs_1_), channel_id=1, source_target_pairs={{0,4},{2,6},{4,0},{6,2},{1,5},{3,7},{5,1},{7,3},{8,12},{10,14},{12... | collective-permute-start | bytes 1671176 | tf_op jit(solution)/shard_map/ppermute | solution.py:228
  44.8 11.5 %collective-permute-start.13 = (bf16[136,1024]{1,0:T(8,128)(2,1)S(1)}, bf16[136,1024]{1,0:T(8,128)(2,1)S(1)}, u32[]{:S(2)}, u32[]{:S(2)}) collective-permute-start(bf16[136,1024]{1,0:T(8,128)(2,1)S(1)} %slice.9), channel_id=1, source_target_pairs={{0,4},{2,6},{4,0},{6,2},{1,5},{3,7},{5,1},{7,3},{8,12},{10,14},{12... | collective-permute-start | bytes 835592 | tf_op jit(solution)/shard_map/ppermute | solution.py:228
  47.0 9.3 %collective-permute-start.11 = (bf16[136,1024]{1,0:T(8,128)(2,1)S(1)}, bf16[136,1024]{1,0:T(8,128)(2,1)S(1)}, u32[]{:S(2)}, u32[]{:S(2)}) collective-permute-start(bf16[136,1024]{1,0:T(8,128)(2,1)S(1)} %slice.8), channel_id=1, source_target_pairs={{0,2},{2,0},{4,6},{6,4},{1,3},{3,1},{5,7},{7,5},{8,10},{10,8},{12,... | collective-permute-start | bytes 835592 | tf_op jit(solution)/shard_map/ppermute | solution.py:228
  48.0 9.5 %collective-permute-start.10 = (bf16[128,1024]{1,0:T(8,128)(2,1)S(1)}, bf16[128,1024]{1,0:T(8,128)(2,1)S(1)}, u32[]{:S(2)}, u32[]{:S(2)}) collective-permute-start(bf16[128,1024]{1,0:T(8,128)(2,1)S(1)} %get-tuple-element.47), channel_id=1, source_target_pairs={{0,6},{2,4},{4,2},{6,0},{1,7},{3,5},{5,3},{7,1},{8,14},{10,12},{12... | collective-permute-start | bytes 786440 | tf_op jit(solution)/shard_map/ppermute | solution.py:228
  56.3 4.2 %collective-permute-start.16 = (bf16[256,1024]{1,0:T(8,128)(2,1)S(1)}, bf16[256,1024]{1,0:T(8,128)(2,1)S(1)}, u32[]{:S(2)}, u32[]{:S(2)}) collective-permute-start(bf16[256,1024]{1,0:T(8,128)(2,1)S(1)} %get-tuple-element.56), channel_id=1, source_target_pairs={{0,1},{1,0},{2,3},{3,2},{4,5},{5,4},{6,7},{7,6},{8,9},{9,8},{10,11... | collective-permute-start | bytes 1572872 | tf_op jit(solution)/shard_map/ppermute | solution.py:228
  56.4 4.2 %collective-permute-start.17 = (bf16[256,1024]{1,0:T(8,128)(2,1)S(1)}, bf16[256,1024]{1,0:T(8,128)(2,1)S(1)}, u32[]{:S(2)}, u32[]{:S(2)}) collective-permute-start(bf16[256,1024]{1,0:T(8,128)(2,1)S(1)} %get-tuple-element.57), channel_id=1, source_target_pairs={{0,1},{1,0},{2,3},{3,2},{4,5},{5,4},{6,7},{7,6},{8,9},{9,8},{10,11... | collective-permute-start | bytes 1572872 | tf_op jit(solution)/shard_map/ppermute | solution.py:228
  57.0 3.7 %collective-permute-start.14 = (bf16[136,1024]{1,0:T(8,128)(2,1)S(1)}, bf16[136,1024]{1,0:T(8,128)(2,1)S(1)}, u32[]{:S(2)}, u32[]{:S(2)}) collective-permute-start(bf16[136,1024]{1,0:T(8,128)(2,1)S(1)} %collective-permute-done.13.refs_2_), channel_id=1, source_target_pairs={{0,1},{1,0},{2,3},{3,2},{4,5},{5,4},{6,7},{7,6},{8,9},{9,8},{10,11... | collective-permute-start | bytes 835592 | tf_op jit(solution)/shard_map/ppermute | solution.py:228
  57.1 3.6 %collective-permute-start.12 = (bf16[136,1024]{1,0:T(8,128)(2,1)S(1)}, bf16[136,1024]{1,0:T(8,128)(2,1)S(1)}, u32[]{:S(2)}, u32[]{:S(2)}) collective-permute-start(bf16[136,1024]{1,0:T(8,128)(2,1)S(1)} %collective-permute-done.11.refs_0_), channel_id=1, source_target_pairs={{0,1},{1,0},{2,3},{3,2},{4,5},{5,4},{6,7},{7,6},{8,9},{9,8},{10,11... | collective-permute-start | bytes 835592 | tf_op jit(solution)/shard_map/ppermute | solution.py:228

commit v8 on v7

--- a/solution.py
+++ b/solution.py
@@ -316,7 +316,7 @@
     if sections == 2:
         mine = [mine[0] + [jnp.concatenate([swap(x, "section", 1) for x in jnp.split(after(theirs[0], *corners), 2)], axis=0)]]
         corners = sum([[x, swap(x, "section", 1)] for x in corners], [])
-    total = label_call(corners, mine, pieces=2 if blocks * each % 32 == 0 else 1)
+    total = label_call(corners, mine, pieces=4 if blocks * each % 64 == 0 else 1)
     query_grad = parts[0]
     for k in range(1, label_count):
         query_grad = query_grad + back[k].astype(f32)

time: 64.2 us -> 64.2 us (level)
  no operation moved by 1% of the time
where the time goes in v8:
time: 64.2 us; the launch traced here: 63.9 us
  Pallas kernels  28 us (44%)
  starting transfers between devices  20.7 us (32%)
  waiting for transfers between devices  8.68 us (14%)
  local copies, waits for them, and re-layouts  4.22 us (7%)
  other arithmetic  1.34 us (2%)
  between operations  1.01 us (2%)
    pallas_call x5, Pallas kernels, b_call(): pl.pallas_call(functools.partial(b_body, n, sides, pair, len(more) // sid...  15.5 us
    ppermute x14, starting transfers between devices, swap(): return lax.ppermute(x, axis, [(i, i ^ bit) for i in range(size)])  14.2 us
    pallas_call x2, Pallas kernels, a_call(): pl.pallas_call(functools.partial(a_body, n, group), out_shape=out_types,...  9.95 us
    ppermute x14, waiting for transfers between devices, swap(): return lax.ppermute(x, axis, [(i, i ^ bit) for i in range(size)])  6.2 us
    unnamed x10, local copies, waits for them, and re-layouts  4.12 us
    ppermute x1, starting transfers between devices, per_device(): columns.append(lax.ppermute(after(columns[-1], *gate), 'dp', forward))  3.52 us
    ppermute x1, waiting for transfers between devices, per_device(): column = lax.ppermute(packed, 'dp', forward)  1.84 us
    pallas_call x1, Pallas kernels, pack(): pl.pallas_call(pack_body, out_shape=jax.ShapeDtypeStruct((rows + positive...  1.72 us
  transfers between devices with their start and end apart: 18, of which 5 were waited for; matrix products, arithmetic and copies ran while one was open for 2% of the time, Pallas kernels for 36%

profile of v8, /device:TPU:0, one launch (start us, length us, event | category | flops | bytes accessed | tf_op | source)
XLA Modules:
  0.0 63.9 jit_solution(9586335877584937109)
XLA Ops:
  0.6 1.7 %pack.1.refs_1_ = bf16[136,1024]{1,0:T(8,128)(2,1)} custom-call(bf16[128,1024]{1,0:T(8,128)(2,1)} %queries.1, s32[8,128]{1,0:T(8,128)} %bitcast.6, s32[1,48]{1,0:T(1,128)} %shortlist.1, s32[128]{0:T(128)} %owner_map.1), custom_call_target="tpu_custom_call" | custom-call | tf_op jit(solution)/shard_map/pack/pallas_call | solution.py:43
  2.4 2.9 %collective-permute-start = (bf16[136,1024]{1,0:T(8,128)(2,1)}, bf16[136,1024]{1,0:T(8,128)(2,1)S(1)}, u32[]{:S(2)}, u32[]{:S(2)}) collective-permute-start(bf16[136,1024]{1,0:T(8,128)(2,1)} %pack.1.refs_1_), channel_id=1, source_target_pairs={{0,2},{2,0},{4,6},{6,4},{1,3},{3,1},{5,7},{7,5},{8,10},{10,8},{12,... | collective-permute-start | bytes 835592 | tf_op jit(solution)/shard_map/ppermute | solution.py:228
  5.3 1.5 %collective-permute-start.1 = (bf16[136,1024]{1,0:T(8,128)(2,1)}, bf16[136,1024]{1,0:T(8,128)(2,1)S(1)}, u32[]{:S(2)}, u32[]{:S(2)}) collective-permute-start(bf16[136,1024]{1,0:T(8,128)(2,1)} %pack.1.refs_1_), channel_id=1, source_target_pairs={{0,4},{2,6},{4,0},{6,2},{1,5},{3,7},{5,1},{7,3},{8,12},{10,14},{12... | collective-permute-start | bytes 835592 | tf_op jit(solution)/shard_map/ppermute | solution.py:228
  6.8 1.6 %collective-permute-start.5 = (bf16[136,1024]{1,0:T(8,128)(2,1)}, bf16[136,1024]{1,0:T(8,128)(2,1)S(1)}, u32[]{:S(2)}, u32[]{:S(2)}) collective-permute-start(bf16[136,1024]{1,0:T(8,128)(2,1)} %pack.1.refs_1_), channel_id=1, source_target_pairs={{0,8},{8,24},{24,16},{16,0},{1,9},{9,25},{25,17},{17,1},{2,10},{10... | collective-permute-start | bytes 835592 | tf_op jit(solution)/shard_map/ppermute | solution.py:274
  8.5 3.4 %copy-done = bf16[32,128,1024]{2,1,0:T(8,128)(2,1)S(1)} copy-done((bf16[32,128,1024]{2,1,0:T(8,128)(2,1)S(1)}, bf16[32,128,1024]{2,1,0:T(8,128)(2,1)}, u32[]{:S(2)}) %copy-start) | copy-done | bytes 8388632
  11.9 0.7 %copy-done.3 = f32[32,128]{1,0:T(8,128)S(1)} copy-done((f32[32,128]{1,0:T(8,128)S(1)}, f32[32,128]{1,0:T(8,128)}, u32[]{:S(2)}) %copy-start.3) | copy-done | bytes 16408
  12.6 0.8 %prepare.1 = (bf16[512,1024]{1,0:T(8,128)(2,1)S(1)}, bf16[512,1024]{1,0:T(8,128)(2,1)S(1)}, f32[512,128]{1,0:T(8,128)S(1)}, f32[512,128]{1,0:T(8,128)S(1)}) custom-call(s32[3]{0:T(128)S(1)} %pad_add_fusion.where, bf16[32,128,1024]{2,1,0:T(8,128)(2,1)S(1)} %copy-done, f32[32,128]{1,0:T(8,128)S(1)} %copy-done.3), custom_call_target="tpu_custom_call" | custom-call | flops 1 | bytes 134217728 | tf_op jit(solution)/shard_map/prepare/pallas_call | solution.py:71
  13.4 0.5 collective-permute-start.2
  13.9 1.8 %collective-permute-done.5 = bf16[136,1024]{1,0:T(8,128)(2,1)S(1)} collective-permute-done((bf16[136,1024]{1,0:T(8,128)(2,1)}, bf16[136,1024]{1,0:T(8,128)(2,1)S(1)}, u32[]{:S(2)}, u32[]{:S(2)}) %collective-permute-start.5) | collective-permute-done | bytes 278560 | tf_op jit(solution)/shard_map/ppermute | solution.py:274
  15.8 0.7 %collective-permute-start.6 = (bf16[136,1024]{1,0:T(8,128)(2,1)S(1)}, bf16[136,1024]{1,0:T(8,128)(2,1)S(1)}, u32[]{:S(2)}, u32[]{:S(2)}) collective-permute-start(bf16[136,1024]{1,0:T(8,128)(2,1)S(1)} %collective-permute-done.5), channel_id=1, source_target_pairs={{0,0},{8,16},{16,8},{24,24},{1,1},{9,17},{17,9},{25,25},{2,2},{10,... | collective-permute-start | bytes 835592 | tf_op jit(solution)/shard_map/ppermute | solution.py:287
  16.5 3.5 %collective-permute-start.7 = (bf16[136,1024]{1,0:T(8,128)(2,1)S(1)}, bf16[136,1024]{1,0:T(8,128)(2,1)S(1)}, u32[]{:S(2)}, u32[]{:S(2)}) collective-permute-start(bf16[136,1024]{1,0:T(8,128)(2,1)S(1)} %collective-permute-done.5), channel_id=1, source_target_pairs={{0,8},{8,24},{24,16},{16,0},{1,9},{9,25},{25,17},{17,1},{2,10},{10... | collective-permute-start | bytes 835592 | tf_op jit(solution)/shard_map/ppermute | solution.py:283
  20.0 5.0 %owner_side.2 = (bf16[128,1024]{1,0:T(8,128)(2,1)S(1)}, bf16[128,1024]{1,0:T(8,128)(2,1)S(1)}) custom-call(s32[1]{0:T(128)} %bitcast.base, bf16[136,1024]{1,0:T(8,128)(2,1)S(1)} %collective-permute-done.refs_0_, bf16[136,1024]{1,0:T(8,128)(2,1)S(1)} %collective-permute-done.1.refs_1_, bf16[32,128,1024]{2,1,0:T(8,128)(2,1)S(1)} %copy-done.1, ...), custom_call_target="tpu_custom_call" | custom-call | flops 1 | bytes 1 | tf_op jit(solution)/shard_map/owner_side/pallas_call | solution.py:139
  25.1 0.7 %collective-permute-start.15 = (bf16[544,1024]{1,0:T(8,128)(2,1)S(1)}, bf16[544,1024]{1,0:T(8,128)(2,1)S(1)}, u32[]{:S(2)}, u32[]{:S(2)}) collective-permute-start(bf16[544,1024]{1,0:T(8,128)(2,1)S(1)} %pad_maximum_fusion.refs_0_), channel_id=1, source_target_pairs={{0,8},{8,0},{16,24},{24,16},{1,9},{9,1},{17,25},{25,17},{2,10},{10... | collective-permute-start | bytes 3342344 | tf_op jit(solution)/shard_map/ppermute | solution.py:291
  25.8 0.5 collective-permute-start.4
  26.3 0.5 collective-permute-start.3
  26.9 5.0 %owner_side.3 = (bf16[128,1024]{1,0:T(8,128)(2,1)S(1)}, f32[128,1024]{1,0:T(8,128)S(1)}) custom-call(s32[1]{0:T(128)} %bitcast.base, bf16[136,1024]{1,0:T(8,128)(2,1)S(1)} %collective-permute-done.2.refs_0_, bf16[136,1024]{1,0:T(8,128)(2,1)S(1)} %copy-done.2, bf16[32,128,1024]{2,1,0:T(8,128)(2,1)S(1)} %copy-done.1, f32[32,128]{1,0:T(8,128)S(1)} %copy-done.4), custom_call_target="tpu_custom_call" | custom-call | flops 1 | bytes 1 | tf_op jit(solution)/shard_map/owner_side/pallas_call | solution.py:139
  32.2 0.8 %collective-permute-done.3 = bf16[128,1024]{1,0:T(8,128)(2,1)S(1)} collective-permute-done((bf16[128,1024]{1,0:T(8,128)(2,1)S(1)}, bf16[128,1024]{1,0:T(8,128)(2,1)S(1)}, u32[]{:S(2)}, u32[]{:S(2)}) %collective-permute-start.3) | collective-permute-done | bytes 262176 | tf_op jit(solution)/shard_map/ppermute | solution.py:228
  33.0 0.5 collective-permute-start.8
  33.5 1.5 %collective-permute-start.9 = (bf16[272,1024]{1,0:T(8,128)(2,1)S(1)}, bf16[272,1024]{1,0:T(8,128)(2,1)S(1)}, u32[]{:S(2)}, u32[]{:S(2)}) collective-permute-start(bf16[272,1024]{1,0:T(8,128)(2,1)S(1)} %pad_maximum_fusion.2.refs_1_), channel_id=1, source_target_pairs={{0,4},{2,6},{4,0},{6,2},{1,5},{3,7},{5,1},{7,3},{8,12},{10,14},{12... | collective-permute-start | bytes 1671176 | tf_op jit(solution)/shard_map/ppermute | solution.py:228
  35.0 4.6 %label_side.5 = (f32[512,1024]{1,0:T(8,128)S(1)}, f32[512,1024]{1,0:T(8,128)S(1)}) custom-call(s32[3]{0:T(128)S(1)} %pad_add_fusion.where, bf16[544,1024]{1,0:T(8,128)(2,1)S(1)} %pad_maximum_fusion.refs_0_, bf16[272,1024]{1,0:T(8,128)(2,1)S(1)} %pad_maximum_fusion.2.refs_1_, bf16[512,1024]{1,0:T(8,128)(2,1)S(1)} %get-tuple-element.29.refs_2_.refs_1_, ...), custom_call_target="tpu_custom_call" | custom-call | flops 1 | bytes 1 | tf_op jit(solution)/shard_map/label_side/pallas_call | solution.py:213
  39.6 5.1 %collective-permute-done.8.refs_0_ = bf16[272,1024]{1,0:T(8,128)(2,1)S(1)} collective-permute-done((bf16[272,1024]{1,0:T(8,128)(2,1)S(1)}, bf16[272,1024]{1,0:T(8,128)(2,1)S(1)}, u32[]{:S(2)}, u32[]{:S(2)}) %collective-permute-start.8) | collective-permute-done | bytes 557088 | tf_op jit(solution)/shard_map/ppermute | solution.py:228
  44.8 2.2 %collective-permute-start.13 = (bf16[136,1024]{1,0:T(8,128)(2,1)S(1)}, bf16[136,1024]{1,0:T(8,128)(2,1)S(1)}, u32[]{:S(2)}, u32[]{:S(2)}) collective-permute-start(bf16[136,1024]{1,0:T(8,128)(2,1)S(1)} %slice.9), channel_id=1, source_target_pairs={{0,4},{2,6},{4,0},{6,2},{1,5},{3,7},{5,1},{7,3},{8,12},{10,14},{12... | collective-permute-start | bytes 835592 | tf_op jit(solution)/shard_map/ppermute | solution.py:228
  47.0 0.9 %collective-permute-start.11 = (bf16[136,1024]{1,0:T(8,128)(2,1)S(1)}, bf16[136,1024]{1,0:T(8,128)(2,1)S(1)}, u32[]{:S(2)}, u32[]{:S(2)}) collective-permute-start(bf16[136,1024]{1,0:T(8,128)(2,1)S(1)} %slice.8), channel_id=1, source_target_pairs={{0,2},{2,0},{4,6},{6,4},{1,3},{3,1},{5,7},{7,5},{8,10},{10,8},{12,... | collective-permute-start | bytes 835592 | tf_op jit(solution)/shard_map/ppermute | solution.py:228
  48.0 1.9 %collective-permute-start.10 = (bf16[128,1024]{1,0:T(8,128)(2,1)S(1)}, bf16[128,1024]{1,0:T(8,128)(2,1)S(1)}, u32[]{:S(2)}, u32[]{:S(2)}) collective-permute-start(bf16[128,1024]{1,0:T(8,128)(2,1)S(1)} %get-tuple-element.47), channel_id=1, source_target_pairs={{0,6},{2,4},{4,2},{6,0},{1,7},{3,5},{5,3},{7,1},{8,14},{10,12},{12... | collective-permute-start | bytes 786440 | tf_op jit(solution)/shard_map/ppermute | solution.py:228
  49.9 3.6 %label_side.6 = (f32[512,1024]{1,0:T(8,128)S(1)}, f32[512,1024]{1,0:T(8,128)S(1)}) custom-call(s32[3]{0:T(128)S(1)} %pad_add_fusion.where, bf16[272,1024]{1,0:T(8,128)(2,1)S(1)} %collective-permute-done.8.refs_0_, bf16[272,1024]{1,0:T(8,128)(2,1)S(1)} %collective-permute-done.9.refs_1_, bf16[512,1024]{1,0:T(8,128)(2,1)S(1)} %get-tuple-element.29.refs_2_.refs_1_, ...), custom_call_target="tpu_custom_call" | custom-call | flops 1 | bytes 1 | tf_op jit(solution)/shard_map/label_side/pallas_call | solution.py:213
  53.5 0.6 collective-permute-done.15.refs_0_
  54.1 2.1 %label_side.7 = bf16[512,1024]{1,0:T(8,128)(2,1)S(1)} custom-call(s32[2]{0:T(128)S(1)} %pad_add_fusion.2.where, bf16[544,1024]{1,0:T(8,128)(2,1)S(1)} %collective-permute-done.15.refs_0_, bf16[512,1024]{1,0:T(8,128)(2,1)S(1)} %get-tuple-element.29.refs_2_.refs_1_, f32[512,128]{1,0:T(8,128)S(1)} %get-tuple-element.31.refs_4_.refs_2_, ...), custom_call_target="tpu_custom_call" | custom-call | flops 1 | bytes 1 | tf_op jit(solution)/shard_map/label_side/pallas_call | solution.py:213
  56.4 0.5 collective-permute-start.17
  57.1 0.4 collective-permute-start.12
  57.5 0.9 %convert_add_fusion = f32[128,1024]{1,0:T(8,128)} fusion(bf16[128,1024]{1,0:T(8,128)(2,1)S(1)} %collective-permute-done.10, bf16[128,1024]{1,0:T(8,128)(2,1)S(1)} %collective-permute-done.4, f32[128,1024]{1,0:T(8,128)S(1)} %get-tuple-element.37, bf16[128,1024]{1,0:T(8,128)(2,1)S(1)} %collective-permute-done.3), kind=kLoop, calls=%fused_computation.3 | loop fusion | flops 786432 | bytes 1835008 | tf_op jit(solution)/shard_map/add | solution.py:322
  58.4 2.1 %label_side.8.refs_6_ = f32[512,1024]{1,0:T(8,128)S(1)} custom-call(s32[2]{0:T(128)S(1)} %pad_add_fusion.1.where, bf16[544,1024]{1,0:T(8,128)(2,1)S(1)} %collective-permute-done.15.refs_0_, bf16[512,1024]{1,0:T(8,128)(2,1)S(1)} %get-tuple-element.30.refs_3_.refs_1_.refs_4_, f32[512,128]{1,0:T(8,128)S(1)} %get-tuple-element.32.refs_5_.refs_2_, ...), custom_call_target="tpu_custom_call" | custom-call | flops 1 | bytes 1 | tf_op jit(solution)/shard_map/label_side/pallas_call | solution.py:213
  60.7 3.0 %label_side.9 = f32[512,1024]{1,0:T(8,128)} custom-call(s32[2]{0:T(128)S(1)} %pad_add_fusion.1.where, bf16[136,1024]{1,0:T(8,128)(2,1)S(1)} %collective-permute-done.11.refs_0_, bf16[136,1024]{1,0:T(8,128)(2,1)S(1)} %collective-permute-done.12.refs_1_, bf16[136,1024]{1,0:T(8,128)(2,1)S(1)} %collective-permute-done.13.refs_2_, ...), custom_call_target="tpu_custom_call" | custom-call | flops 1 | bytes 1 | tf_op jit(solution)/shard_map/label_side/pallas_call | solution.py:213
  (33 shorter events, 1.0 us)
Async XLA Ops:
  2.4 11.6 %collective-permute-start = (bf16[136,1024]{1,0:T(8,128)(2,1)}, bf16[136,1024]{1,0:T(8,128)(2,1)S(1)}, u32[]{:S(2)}, u32[]{:S(2)}) collective-permute-start(bf16[136,1024]{1,0:T(8,128)(2,1)} %pack.1.refs_1_), channel_id=1, source_target_pairs={{0,2},{2,0},{4,6},{6,4},{1,3},{3,1},{5,7},{7,5},{8,10},{10,8},{12,... | collective-permute-start | bytes 835592 | tf_op jit(solution)/shard_map/ppermute | solution.py:228
  5.3 8.6 %collective-permute-start.1 = (bf16[136,1024]{1,0:T(8,128)(2,1)}, bf16[136,1024]{1,0:T(8,128)(2,1)S(1)}, u32[]{:S(2)}, u32[]{:S(2)}) collective-permute-start(bf16[136,1024]{1,0:T(8,128)(2,1)} %pack.1.refs_1_), channel_id=1, source_target_pairs={{0,4},{2,6},{4,0},{6,2},{1,5},{3,7},{5,1},{7,3},{8,12},{10,14},{12... | collective-permute-start | bytes 835592 | tf_op jit(solution)/shard_map/ppermute | solution.py:228
  6.8 9.0 %collective-permute-start.5 = (bf16[136,1024]{1,0:T(8,128)(2,1)}, bf16[136,1024]{1,0:T(8,128)(2,1)S(1)}, u32[]{:S(2)}, u32[]{:S(2)}) collective-permute-start(bf16[136,1024]{1,0:T(8,128)(2,1)} %pack.1.refs_1_), channel_id=1, source_target_pairs={{0,8},{8,24},{24,16},{16,0},{1,9},{9,25},{25,17},{17,1},{2,10},{10... | collective-permute-start | bytes 835592 | tf_op jit(solution)/shard_map/ppermute | solution.py:274
  8.5 3.4 %copy-start = (bf16[32,128,1024]{2,1,0:T(8,128)(2,1)S(1)}, bf16[32,128,1024]{2,1,0:T(8,128)(2,1)}, u32[]{:S(2)}) copy-start(bf16[32,128,1024]{2,1,0:T(8,128)(2,1)} %refs_2_.3) | copy-start | bytes 25165828
  11.8 0.7 %copy-start.3 = (f32[32,128]{1,0:T(8,128)S(1)}, f32[32,128]{1,0:T(8,128)}, u32[]{:S(2)}) copy-start(f32[32,128]{1,0:T(8,128)} %refs_3_.3) | copy-start | bytes 49156
  12.6 7.4 %copy-start.1 = (bf16[32,128,1024]{2,1,0:T(8,128)(2,1)S(1)}, bf16[32,128,1024]{2,1,0:T(8,128)(2,1)}, u32[]{:S(2)}) copy-start(bf16[32,128,1024]{2,1,0:T(8,128)(2,1)} %refs_2_.3) | copy-start | bytes 25165828
  13.4 11.6 %copy-start.2 = (bf16[136,1024]{1,0:T(8,128)(2,1)S(1)}, bf16[136,1024]{1,0:T(8,128)(2,1)}, u32[]{:S(2)}) copy-start(bf16[136,1024]{1,0:T(8,128)(2,1)} %pack.1.refs_1_) | copy-start | bytes 835588
  13.4 11.6 %collective-permute-start.2 = (bf16[136,1024]{1,0:T(8,128)(2,1)}, bf16[136,1024]{1,0:T(8,128)(2,1)S(1)}, u32[]{:S(2)}, u32[]{:S(2)}) collective-permute-start(bf16[136,1024]{1,0:T(8,128)(2,1)} %pack.1.refs_1_), channel_id=1, source_target_pairs={{0,6},{2,4},{4,2},{6,0},{1,7},{3,5},{5,3},{7,1},{8,14},{10,12},{12... | collective-permute-start | bytes 835592 | tf_op jit(solution)/shard_map/ppermute | solution.py:228
  15.8 16.1 %collective-permute-start.6 = (bf16[136,1024]{1,0:T(8,128)(2,1)S(1)}, bf16[136,1024]{1,0:T(8,128)(2,1)S(1)}, u32[]{:S(2)}, u32[]{:S(2)}) collective-permute-start(bf16[136,1024]{1,0:T(8,128)(2,1)S(1)} %collective-permute-done.5), channel_id=1, source_target_pairs={{0,0},{8,16},{16,8},{24,24},{1,1},{9,17},{17,9},{25,25},{2,2},{10,... | collective-permute-start | bytes 835592 | tf_op jit(solution)/shard_map/ppermute | solution.py:287
  16.5 15.4 %collective-permute-start.7 = (bf16[136,1024]{1,0:T(8,128)(2,1)S(1)}, bf16[136,1024]{1,0:T(8,128)(2,1)S(1)}, u32[]{:S(2)}, u32[]{:S(2)}) collective-permute-start(bf16[136,1024]{1,0:T(8,128)(2,1)S(1)} %collective-permute-done.5), channel_id=1, source_target_pairs={{0,8},{8,24},{24,16},{16,0},{1,9},{9,25},{25,17},{17,1},{2,10},{10... | collective-permute-start | bytes 835592 | tf_op jit(solution)/shard_map/ppermute | solution.py:283
  25.0 1.9 %copy-start.4 = (f32[32,128]{1,0:T(8,128)S(1)}, f32[32,128]{1,0:T(8,128)}, u32[]{:S(2)}) copy-start(f32[32,128]{1,0:T(8,128)} %refs_3_.3) | copy-start | bytes 49156
  25.1 29.0 %collective-permute-start.15 = (bf16[544,1024]{1,0:T(8,128)(2,1)S(1)}, bf16[544,1024]{1,0:T(8,128)(2,1)S(1)}, u32[]{:S(2)}, u32[]{:S(2)}) collective-permute-start(bf16[544,1024]{1,0:T(8,128)(2,1)S(1)} %pad_maximum_fusion.refs_0_), channel_id=1, source_target_pairs={{0,8},{8,0},{16,24},{24,16},{1,9},{9,1},{17,25},{25,17},{2,10},{10... | collective-permute-start | bytes 3342344 | tf_op jit(solution)/shard_map/ppermute | solution.py:291
  25.8 6.4 %collective-permute-start.4 = (bf16[128,1024]{1,0:T(8,128)(2,1)S(1)}, bf16[128,1024]{1,0:T(8,128)(2,1)S(1)}, u32[]{:S(2)}, u32[]{:S(2)}) collective-permute-start(bf16[128,1024]{1,0:T(8,128)(2,1)S(1)} %get-tuple-element.40), channel_id=1, source_target_pairs={{0,4},{2,6},{4,0},{6,2},{1,5},{3,7},{5,1},{7,3},{8,12},{10,14},{12... | collective-permute-start | bytes 786440 | tf_op jit(solution)/shard_map/ppermute | solution.py:228
  26.3 6.6 %collective-permute-start.3 = (bf16[128,1024]{1,0:T(8,128)(2,1)S(1)}, bf16[128,1024]{1,0:T(8,128)(2,1)S(1)}, u32[]{:S(2)}, u32[]{:S(2)}) collective-permute-start(bf16[128,1024]{1,0:T(8,128)(2,1)S(1)} %get-tuple-element.38), channel_id=1, source_target_pairs={{0,2},{2,0},{4,6},{6,4},{1,3},{3,1},{5,7},{7,5},{8,10},{10,8},{12,... | collective-permute-start | bytes 786440 | tf_op jit(solution)/shard_map/ppermute | solution.py:228
  33.0 11.8 %collective-permute-start.8 = (bf16[272,1024]{1,0:T(8,128)(2,1)S(1)}, bf16[272,1024]{1,0:T(8,128)(2,1)S(1)}, u32[]{:S(2)}, u32[]{:S(2)}) collective-permute-start(bf16[272,1024]{1,0:T(8,128)(2,1)S(1)} %pad_maximum_fusion.2.refs_1_), channel_id=1, source_target_pairs={{0,2},{2,0},{4,6},{6,4},{1,3},{3,1},{5,7},{7,5},{8,10},{10,8},{12,... | collective-permute-start | bytes 1671176 | tf_op jit(solution)/shard_map/ppermute | solution.py:228
  33.5 13.5 %collective-permute-start.9 = (bf16[272,1024]{1,0:T(8,128)(2,1)S(1)}, bf16[272,1024]{1,0:T(8,128)(2,1)S(1)}, u32[]{:S(2)}, u32[]{:S(2)}) collective-permute-start(bf16[272,1024]{1,0:T(8,128)(2,1)S(1)} %pad_maximum_fusion.2.refs_1_), channel_id=1, source_target_pairs={{0,4},{2,6},{4,0},{6,2},{1,5},{3,7},{5,1},{7,3},{8,12},{10,14},{12... | collective-permute-start | bytes 1671176 | tf_op jit(solution)/shard_map/ppermute | solution.py:228
  44.8 11.5 %collective-permute-start.13 = (bf16[136,1024]{1,0:T(8,128)(2,1)S(1)}, bf16[136,1024]{1,0:T(8,128)(2,1)S(1)}, u32[]{:S(2)}, u32[]{:S(2)}) collective-permute-start(bf16[136,1024]{1,0:T(8,128)(2,1)S(1)} %slice.9), channel_id=1, source_target_pairs={{0,4},{2,6},{4,0},{6,2},{1,5},{3,7},{5,1},{7,3},{8,12},{10,14},{12... | collective-permute-start | bytes 835592 | tf_op jit(solution)/shard_map/ppermute | solution.py:228
  47.0 9.3 %collective-permute-start.11 = (bf16[136,1024]{1,0:T(8,128)(2,1)S(1)}, bf16[136,1024]{1,0:T(8,128)(2,1)S(1)}, u32[]{:S(2)}, u32[]{:S(2)}) collective-permute-start(bf16[136,1024]{1,0:T(8,128)(2,1)S(1)} %slice.8), channel_id=1, source_target_pairs={{0,2},{2,0},{4,6},{6,4},{1,3},{3,1},{5,7},{7,5},{8,10},{10,8},{12,... | collective-permute-start | bytes 835592 | tf_op jit(solution)/shard_map/ppermute | solution.py:228
  48.0 9.5 %collective-permute-start.10 = (bf16[128,1024]{1,0:T(8,128)(2,1)S(1)}, bf16[128,1024]{1,0:T(8,128)(2,1)S(1)}, u32[]{:S(2)}, u32[]{:S(2)}) collective-permute-start(bf16[128,1024]{1,0:T(8,128)(2,1)S(1)} %get-tuple-element.47), channel_id=1, source_target_pairs={{0,6},{2,4},{4,2},{6,0},{1,7},{3,5},{5,3},{7,1},{8,14},{10,12},{12... | collective-permute-start | bytes 786440 | tf_op jit(solution)/shard_map/ppermute | solution.py:228
  56.3 4.2 %collective-permute-start.16 = (bf16[256,1024]{1,0:T(8,128)(2,1)S(1)}, bf16[256,1024]{1,0:T(8,128)(2,1)S(1)}, u32[]{:S(2)}, u32[]{:S(2)}) collective-permute-start(bf16[256,1024]{1,0:T(8,128)(2,1)S(1)} %get-tuple-element.56), channel_id=1, source_target_pairs={{0,1},{1,0},{2,3},{3,2},{4,5},{5,4},{6,7},{7,6},{8,9},{9,8},{10,11... | collective-permute-start | bytes 1572872 | tf_op jit(solution)/shard_map/ppermute | solution.py:228
  56.4 4.2 %collective-permute-start.17 = (bf16[256,1024]{1,0:T(8,128)(2,1)S(1)}, bf16[256,1024]{1,0:T(8,128)(2,1)S(1)}, u32[]{:S(2)}, u32[]{:S(2)}) collective-permute-start(bf16[256,1024]{1,0:T(8,128)(2,1)S(1)} %get-tuple-element.57), channel_id=1, source_target_pairs={{0,1},{1,0},{2,3},{3,2},{4,5},{5,4},{6,7},{7,6},{8,9},{9,8},{10,11... | collective-permute-start | bytes 1572872 | tf_op jit(solution)/shard_map/ppermute | solution.py:228
  57.0 3.7 %collective-permute-start.14 = (bf16[136,1024]{1,0:T(8,128)(2,1)S(1)}, bf16[136,1024]{1,0:T(8,128)(2,1)S(1)}, u32[]{:S(2)}, u32[]{:S(2)}) collective-permute-start(bf16[136,1024]{1,0:T(8,128)(2,1)S(1)} %collective-permute-done.13.refs_2_), channel_id=1, source_target_pairs={{0,1},{1,0},{2,3},{3,2},{4,5},{5,4},{6,7},{7,6},{8,9},{9,8},{10,11... | collective-permute-start | bytes 835592 | tf_op jit(solution)/shard_map/ppermute | solution.py:228
  57.1 3.6 %collective-permute-start.12 = (bf16[136,1024]{1,0:T(8,128)(2,1)S(1)}, bf16[136,1024]{1,0:T(8,128)(2,1)S(1)}, u32[]{:S(2)}, u32[]{:S(2)}) collective-permute-start(bf16[136,1024]{1,0:T(8,128)(2,1)S(1)} %collective-permute-done.11.refs_0_), channel_id=1, source_target_pairs={{0,1},{1,0},{2,3},{3,2},{4,5},{5,4},{6,7},{7,6},{8,9},{9,8},{10,11... | collective-permute-start | bytes 835592 | tf_op jit(solution)/shard_map/ppermute | solution.py:228
